TPU v7x, 32 devices: a whole 2x2x4 slice. The times are simulated.
32 devices in a mesh: space: 8 (over z, y), snap: 4 (over x, core).
Axes of the slice: x: 2, y: 2, z: 4, core: 2. Of those that a mesh axis runs over, the one named last changes fastest.
Arguments:
- primal: bfloat16 [2048, 98304], P('snap', 'space'), may hold values from -6 to 6
- adjoint_pencils: bfloat16 [1024, 98304], P('snap', 'space'), may hold values from -0.02734375 to 0.02734375
- weights: float32 [98304], P('space'), may hold values from 0.2 to 2
- pencil_map: int32 [768], replicated, may hold values from 0 to 767, as said below
Outputs:
- hankel: float32 [1024, 2048], P('space', 'snap')
Inputs may be any that keep to these rules, and one draw needn't show every extreme that they name: `pencil_map`: each number appears once; each aligned block of 96 entries holds exactly 12 entries from every aligned range of 96 values.
All inputs are finite; a program needn't handle non-finite values.
Results may differ from a plain program's by a relative error of at most 0.0029.
Values may be sent and summed in bfloat16 or wider, within the bound.
No kernel may reach another device: no remote copies, remote signals or barrier semaphores. Data moves between devices by JAX's collectives and lax.ppermute only.
A program may use at most 128 MiB of HBM per device.

v0:
```python
import jax
import jax.numpy as jnp
from jax import lax
from jax.sharding import PartitionSpec as P

PEN_LEN = 128


def on_device(primal, adjoint_pencils, weights, pencil_map):
    rows_here = adjoint_pencils.shape[0]
    points = adjoint_pencils.shape[1]
    pen_dev = points // PEN_LEN
    tiles = lax.axis_size("space")
    share = pen_dev // tiles
    place = lax.axis_index("space")
    weighted = (primal.astype(jnp.float32) * weights[None, :]).astype(jnp.bfloat16)
    all_slots = pencil_map.reshape(tiles, pen_dev)
    targets = all_slots // pen_dev
    orders = jnp.argsort(targets, axis=1, stable=True)
    own_order = lax.dynamic_index_in_dim(orders, place, 0, keepdims=False)
    chosen = lax.dynamic_slice_in_dim(orders, place * share, share, 1)
    arrived = (jnp.take_along_axis(all_slots, chosen, axis=1) - place * pen_dev).reshape(pen_dev)
    blocks = adjoint_pencils.reshape(rows_here, pen_dev, PEN_LEN)
    outgoing = jnp.take(blocks, own_order, axis=1).reshape(rows_here, tiles, share, PEN_LEN)
    incoming = lax.all_to_all(outgoing, "space", split_axis=1, concat_axis=1, tiled=True)
    inverse = jnp.argsort(arrived)
    moving = jnp.take(incoming.reshape(rows_here, pen_dev, PEN_LEN), inverse, axis=1).reshape(
        rows_here, points
    )
    product = lax.dot_general(
        lax.all_gather(moving, "snap", axis=0, tiled=True),
        weighted,
        (((1,), (1,)), ((), ())),
        preferred_element_type=jnp.float32,
    )
    return lax.psum_scatter(product, "space", scatter_dimension=0, tiled=True)


def solution(mesh):
    placed = (P("snap", "space"), P("snap", "space"), P("space"), P())
    return jax.shard_map(
        on_device, mesh=mesh, in_specs=placed, out_specs=P("space", "snap"), check_vma=False
    )
```

profile of v0, /device:TPU:0, one launch (start us, length us, event | category | flops | bytes accessed | tf_op | source)
XLA Modules:
  0.0 464.5 jit_solution(1827210065150487711)
XLA Ops:
  6.5 0.8 reshape.38
  7.3 0.1 copy.16
  7.4 1.5 sort.34
  8.9 0.2 dynamic-slice_reduce_fusion
  9.1 8.6 %copy.18 = bf16[256,12288]{0,1:T(8,128)(2,1)} copy(bf16[256,12288]{1,0:T(8,128)(2,1)} %param.7) | data formatting | bytes 12582912 | tf_op args[1]
  17.8 8.7 %copy.19 = bf16[256,96,128]{2,0,1:T(8,128)(2,1)} copy(bf16[256,96,128]{0,2,1:T(8,128)(2,1)} %bitcast.15) | data formatting | bytes 12582912 | tf_op jit(solution)/shard_map/reshape | solution.py:23
  26.4 8.8 %gather_fusion.1 = bf16[96,256,128]{2,1,0:T(8,128)(2,1)} fusion(bf16[256,96,128]{2,0,1:T(8,128)(2,1)} %copy.19, s32[1024]{0:T(1024)S(1)} %pad_clamp_fusion.1), kind=kCustom, calls=%fused_computation.clone | custom fusion | bytes 12583296 | tf_op jit(solution)/shard_map/jit(_take)/gather | solution.py:24
  35.2 6.1 %broadcast_select_fusion = bf16[96,256,128]{2,1,0:T(8,128)(2,1)} fusion(bf16[96,256,128]{2,1,0:T(8,128)(2,1)} %gather_fusion.1, pred[96]{0:T(512)(128)(4,1)S(1)} %compare_and_fusion.1), kind=kLoop, calls=%fused_computation.7 | loop fusion | flops 3145728 | bytes 12583008 | tf_op jit(solution)/shard_map/jit(_take)/select_n | solution.py:24
  41.3 7.3 %all-to-all-start = ((bf16[256,8,12,128]{3,0,2,1:T(8,128)(2,1)}), bf16[256,8,12,128]{3,0,2,1:T(8,128)(2,1)}, u32[]{:S(2)}, u32[]{:S(2)}) async-start(bf16[256,8,12,128]{3,0,2,1:T(8,128)(2,1)} %bitcast.13), calls=%async_computation | async-start | bytes 12582912 | tf_op jit(solution)/shard_map/all_to_all | solution.py:25
  48.6 0.0 all-gather.2.cloned.1.call-start
  48.6 0.1 copy.17
  48.7 0.1 bitcast_or_fusion
  48.8 0.1 reshape.59
  48.8 1.0 gather_fusion
  49.8 0.1 reshape.62
  49.9 0.1 select_subtract_fusion
  50.0 0.1 sub.19
  50.1 2.5 sort.35
  52.7 134.1 %all-to-all-done = bf16[256,8,12,128]{3,0,2,1:T(8,128)(2,1)} async-done(((bf16[256,8,12,128]{3,0,2,1:T(8,128)(2,1)}), bf16[256,8,12,128]{3,0,2,1:T(8,128)(2,1)}, u32[]{:S(2)}, u32[]{:S(2)}) %all-to-all-start) | async-done | bytes 6291488 | tf_op jit(solution)/shard_map/all_to_all | solution.py:25
  186.8 8.8 %gather_fusion.2 = bf16[96,256,128]{2,1,0:T(8,128)(2,1)} fusion(bf16[256,96,128]{2,0,1:T(8,128)(2,1)} %bitcast.4, s32[1024]{0:T(1024)S(1)} %pad_clamp_fusion), kind=kCustom, calls=%fused_computation.1.clone | custom fusion | bytes 12583296 | tf_op jit(solution)/shard_map/jit(_take)/gather | solution.py:27
  195.6 6.1 %select_bitcast_fusion = bf16[256,96,128]{2,0,1:T(8,128)(2,1)} fusion(bf16[96,256,128]{2,1,0:T(8,128)(2,1)} %gather_fusion.2, pred[96]{0:T(512)(128)(4,1)S(1)} %compare_and_fusion), kind=kLoop, calls=%fused_computation.6 | loop fusion | flops 3145728 | bytes 12583008 | tf_op jit(solution)/shard_map/jit(_take)/select_n | solution.py:27
  201.7 8.6 %copy.20 = bf16[256,96,128]{0,2,1:T(8,128)(2,1)} copy(bf16[256,96,128]{2,0,1:T(8,128)(2,1)} %select_bitcast_fusion) | data formatting | bytes 12582912 | tf_op jit(solution)/shard_map/jit(_take)/select_n | solution.py:27
  210.2 0.0 copy-start
  210.2 0.0 all-gather.2.cloned.1.call-update
  210.3 0.2 reduce-scatter.2.cloned.1.call-start
  210.5 157.1 %all-gather.2.cloned.1.call-done = bf16[1024,12288]{0,1:T(8,128)(2,1)} async-done(((bf16[256,12288]{0,1:T(8,128)(2,1)}), bf16[1024,12288]{0,1:T(8,128)(2,1)}) %all-gather.2.cloned.1.call-update) | async-done | bytes 25165840 | tf_op jit(solution)/shard_map/all_gather | solution.py:31
  367.6 0.0 copy-done
  367.6 21.2 %fusion = f32[1024,512]{1,0:T(8,128)} fusion(bf16[1024,12288]{0,1:T(8,128)(2,1)} %all-gather.2.cloned.1.call-done, bf16[512,12288]{1,0:T(8,128)(2,1)} %param.6, f32[12288]{0:T(1024)S(1)} %copy-done), kind=kOutput, calls=%fused_computation.4 | convolution fusion | flops 12903776256 | bytes 39895040 | tf_op jit(solution)/shard_map/dot_general | solution.py:30
  388.9 0.0 reduce-scatter.2.cloned.1.call-update
  388.9 68.7 %reduce-scatter.2.cloned.1.call-done = f32[128,512]{1,0:T(8,128)} async-done(((f32[1024,512]{1,0:T(8,128)}), f32[128,512]{1,0:T(8,128)}) %reduce-scatter.2.cloned.1.call-update) | async-done | bytes 262160 | tf_op jit(solution)/shard_map/reduce_scatter | solution.py:36
  (9 shorter events, 0.1 us)
Async XLA Ops:
  41.3 145.5 %all-to-all-start = ((bf16[256,8,12,128]{3,0,2,1:T(8,128)(2,1)}), bf16[256,8,12,128]{3,0,2,1:T(8,128)(2,1)}, u32[]{:S(2)}, u32[]{:S(2)}) async-start(bf16[256,8,12,128]{3,0,2,1:T(8,128)(2,1)} %bitcast.13), calls=%async_computation | async-start | bytes 12582912 | tf_op jit(solution)/shard_map/all_to_all | solution.py:25
  48.6 319.1 %all-gather.2.cloned.1.call-start = ((), (), s32[]{:S(2)}) async-start(), calls=%async_computation.2 | async-start | bytes 31457280 | tf_op jit(solution)/shard_map/all_gather | solution.py:31
  210.2 157.4 %copy-start = (f32[12288]{0:T(1024)S(1)}, f32[12288]{0:T(1024)}, u32[]{:S(2)}) copy-start(f32[12288]{0:T(1024)} %param.8) | copy-start | bytes 147460
  210.3 247.4 %reduce-scatter.2.cloned.1.call-start = ((), (), s32[]{:S(2)}) async-start(), calls=%async_computation.3 | async-start | bytes 2359296 | tf_op jit(solution)/shard_map/reduce_scatter | solution.py:36
Sparse Core Ops, SparseCore 0:
  210.4 157.2 all-gather.1
  389.0 68.5 reduce-scatter.1
where the time goes:
time: 465 us; the launch traced here: 464 us
  waiting for transfers between devices  360 us (77%)
  local copies, waits for them, and re-layouts  45.8 us (10%)
  matrix products  21.2 us (5%)
  other arithmetic  16.4 us (4%)
  between operations  13.5 us (3%)
  starting transfers between devices  7.54 us (2%)
    all_gather x1, waiting for transfers between devices, on_device(): lax.all_gather(moving, 'snap', axis=0, tiled=True)  157 us
    all_to_all x1, waiting for transfers between devices, on_device(): lax.all_to_all(outgoing, 'space', split_axis=1, concat_axis=1, tiled=True)  134 us
    reduce_scatter x1, waiting for transfers between devices, on_device(): return lax.psum_scatter(product, 'space', scatter_dimension=0, tiled=True)  68.7 us
    dot_general x1, matrix products, on_device(): lax.dot_general(lax.all_gather(moving, 'snap', axis=0, tiled=True), weigh...  21.2 us
  transfers between devices with their start and end apart: 3, of which 3 were waited for; matrix products, arithmetic and copies ran while one was open for 1% of the time, Pallas kernels for 0%

commit v1 on v0

v1 whole, which is shorter than its diff:
```python
import jax
import jax.numpy as jnp
from jax import lax
from jax.experimental import pallas as pl
from jax.experimental.pallas import tpu as pltpu
from jax.sharding import PartitionSpec as P

PEN_LEN = 128
ROWS = 16
COST_SCALE = 1


def xor_send(x, axis, k):
    n = lax.axis_size(axis)
    return lax.ppermute(x, axis, [(i, i ^ k) for i in range(n)])


def params(mebibytes=16):
    return pltpu.CompilerParams(vmem_limit_bytes=mebibytes * 1024 * 1024)


def cost(flops, nbytes):
    return pl.CostEstimate(flops=flops // COST_SCALE, bytes_accessed=nbytes // COST_SCALE, transcendentals=0)


def pack(adjoint, pencil_map, where, first, count, ks, tiles):
    halves, _, points = adjoint.shape
    pen_dev = points // PEN_LEN
    share = pen_dev // tiles

    def body(map_ref, where_ref, in_ref, *refs):
        outs, (table, seen) = refs[: len(ks)], refs[len(ks) :]
        place = where_ref[0]
        for k in range(tiles):
            seen[k] = 0

        def enter(q, carry):
            k = lax.div(map_ref[place * pen_dev + q], pen_dev) ^ place
            t = seen[k]
            seen[k] = t + 1
            table[k * share + t] = q
            return carry

        lax.fori_loop(0, pen_dev, enter, 0)
        for o, k in enumerate(ks):
            for t in range(share):
                start = pl.multiple_of(table[k * share + t] * PEN_LEN, PEN_LEN)
                for h in range(halves):
                    outs[o][h * count : (h + 1) * count, t * PEN_LEN : (t + 1) * PEN_LEN] = in_ref[
                        h, first : first + count, pl.ds(start, PEN_LEN)
                    ]

    smem, vmem = pl.BlockSpec(memory_space=pltpu.SMEM), pl.BlockSpec(memory_space=pltpu.VMEM)
    return pl.pallas_call(
        body,
        in_specs=[smem, smem, vmem],
        out_specs=[vmem] * len(ks),
        out_shape=[jax.ShapeDtypeStruct((halves * count, share * PEN_LEN), jnp.bfloat16)] * len(ks),
        scratch_shapes=[pltpu.SMEM((pen_dev,), jnp.int32), pltpu.SMEM((tiles,), jnp.int32)],
        compiler_params=params(),
        cost_estimate=cost(0, 4 * halves * count * points),
    )(pencil_map, where, adjoint)


def slots_of(pencil_map, place, tiles):
    pen_dev = pencil_map.shape[0] // tiles
    share = pen_dev // tiles
    local = pencil_map.reshape(tiles, pen_dev) - place * pen_dev
    here = (local >= 0) & (local < pen_dev)
    q = jnp.arange(pen_dev)
    rank = jnp.sum(here[:, None, :] & (q[None, None, :] < q[None, :, None]), axis=2)
    match = here[:, None, :] & (rank[:, None, :] == jnp.arange(share)[None, :, None])
    table = jnp.sum(jnp.where(match, local[:, None, :], 0), axis=2)
    order = jnp.arange(tiles) ^ place
    picked = jnp.sum(jnp.where(order[:, None, None] == jnp.arange(tiles)[None, :, None], table[None], 0), axis=1)
    return picked.reshape(pen_dev).astype(jnp.int32)


def weigh(primal, weights, table, first, count, tiles):
    rows, points = primal.shape
    share = points // PEN_LEN // tiles
    step = 64 if rows % 64 == 0 else rows

    def body(table_ref, in_ref, w_ref, out):
        for k in range(count):
            for t in range(share):
                start = pl.multiple_of(table_ref[(first + k) * share + t] * PEN_LEN, PEN_LEN)
                scale = w_ref[:, pl.ds(start, PEN_LEN)]
                for i in range(0, rows, step):
                    tile = in_ref[i : i + step, pl.ds(start, PEN_LEN)].astype(jnp.float32) * scale
                    out[k, i : i + step, t * PEN_LEN : (t + 1) * PEN_LEN] = tile.astype(jnp.bfloat16)

    vmem = pl.BlockSpec(memory_space=pltpu.VMEM)
    return pl.pallas_call(
        body,
        in_specs=[pl.BlockSpec(memory_space=pltpu.SMEM), vmem, vmem],
        out_specs=vmem,
        out_shape=jax.ShapeDtypeStruct((count, rows, share * PEN_LEN), jnp.bfloat16),
        compiler_params=params(),
        cost_estimate=cost(rows * points // 2, 3 * rows * points),
    )(table, primal, weights.reshape(1, points))


def merge(parts):
    n = len(parts)
    rows, depth = parts[0].shape
    step = rows // 2 if rows % (2 * ROWS) == 0 else rows

    def body(*refs):
        for i in range(n):
            refs[n][i] = refs[i][...]

    return pl.pallas_call(
        body,
        grid=(rows // step,),
        in_specs=[pl.BlockSpec((step, depth), lambda i: (i, 0))] * n,
        out_specs=pl.BlockSpec((n, step, depth), lambda i: (0, i, 0)),
        out_shape=jax.ShapeDtypeStruct((n, rows, depth), parts[0].dtype),
        compiler_params=params(),
        cost_estimate=cost(0, 4 * n * rows * depth),
    )(*parts)


def multiply(groups, own, other, where, before, each, halves, members):
    held = members // 2
    last = before is not None
    depth = groups[0][0][0].shape[-1]
    columns = own.shape[1]
    counts = [g[0][0].shape[0] if g[0][0].ndim == 3 else 1 for g in groups]
    flat = [a for g in groups for a in g[0]]
    rows = halves * each

    def body(where_ref, *refs):
        ins, w_refs = refs[: len(flat)], refs[len(flat) : len(flat) + 2]
        rest = refs[len(flat) + 2 :]
        total = rest[-1] if last else rest[0]
        if last:
            for n in range(held):
                for h in range(halves):
                    at = n * rows + h * each
                    from_row = h * before[0].shape[1] // halves + before[1]
                    total[at : at + each, :] = rest[0][n, from_row : from_row + each, :]
        k = 0
        for g, count in enumerate(counts):
            stride, first = groups[g][1:]
            for i in range(count):
                taken = []
                for ref in ins[g * held : (g + 1) * held]:
                    for h in range(halves):
                        span = slice(h * stride + first, h * stride + first + each)
                        taken.append(ref[i, span, :] if len(ref.shape) == 3 else ref[span, :])
                stacked = jnp.concatenate(taken, axis=0)
                for side in range(2):
                    product = lax.dot_general(
                        stacked, w_refs[side][k], (((1,), (1,)), ((), ())), preferred_element_type=jnp.float32
                    )
                    span = slice(side * columns, (side + 1) * columns)
                    if last:
                        total[:, span] += product
                    else:
                        for n in range(held):
                            value = product[n * rows : (n + 1) * rows]
                            total[n, :, span] = value if k == 0 else total[n, :, span] + value
                k += 1
        if last:
            for n in range(held):
                for h in range(halves):
                    e = ((where_ref[1] ^ (2 * n)) * halves + h) ^ where_ref[0]
                    to = lax.div(e, 2 * halves) * halves + lax.rem(e, halves)
                    at = (n * halves + h) * each
                    for side in range(2):
                        rest[1 + side][to] = total[at : at + each, side * columns : (side + 1) * columns]

    vmem = pl.BlockSpec(memory_space=pltpu.VMEM)
    full = jax.ShapeDtypeStruct((held, rows, 2 * columns), jnp.float32)
    split = [jax.ShapeDtypeStruct((held * halves, each, columns), jnp.float32)] * 2
    return pl.pallas_call(
        body,
        in_specs=[pl.BlockSpec(memory_space=pltpu.SMEM)] + [vmem] * (len(flat) + 2 + last),
        out_specs=[vmem, vmem] if last else vmem,
        out_shape=split if last else full,
        scratch_shapes=[pltpu.VMEM((held * rows, 2 * columns), jnp.float32)] if last else [],
        compiler_params=params(),
        cost_estimate=cost(
            4 * held * rows * columns * depth * sum(counts), 2 * sum(counts) * depth * (held * rows + 2 * columns)
        ),
    )(where, *flat, own, other, *((before[0],) if last else ()))


def after(x, *done):
    return lax.optimization_barrier((x,) + done)[0] if done else x


def on_device(primal, adjoint_pencils, weights, pencil_map):
    rows_here, points = adjoint_pencils.shape
    tiles = lax.axis_size("space")
    members = lax.axis_size("snap")
    place, lane = lax.axis_index("space"), lax.axis_index("snap")
    where = jnp.stack([place, lane]).astype(jnp.int32)
    rows_out = rows_here * members // tiles
    halves = rows_here // rows_out
    adjoint = adjoint_pencils.reshape(halves, rows_out, points)
    half = tiles // 2
    middle = half + half // 2
    units = rows_out // ROWS
    rows_a = units // 2 * ROWS
    rows_b = max(1, 3 * units // 8) * ROWS
    rows_c = rows_out - rows_a - rows_b
    table = slots_of(pencil_map, place, tiles)

    def pack_rows(source, first, count, ks):
        return dict(zip(ks, pack(source, pencil_map, where, first, count, ks, tiles)))

    def over_space(packed, ks, *done):
        return [xor_send(after(packed[k], *done), "space", k) for k in ks]

    def join(found):
        return found[0] if len(found) == 1 else merge(found)

    def across(block, *done):
        found, bit = [block], members // 2
        order = [0]
        while bit > 1:
            found = found + [xor_send(after(b, *done), "snap", bit) for b in found]
            order = order + [n ^ bit for n in order]
            bit //= 2
        return [found[order.index(n)] for n in sorted(order)]

    def spread(mine, got):
        same = (((lane * halves) ^ place) & halves) == 0
        shape = (-1, halves) + mine.shape[1:]
        mine, got = mine.reshape(shape), got.reshape(shape)
        both = jnp.stack([jnp.where(same, mine, got), jnp.where(same, got, mine)], axis=1)
        return both.reshape((-1,) + mine.shape[2:])

    def add_up(pair, *done):
        x = spread(pair[0], xor_send(after(pair[1], *done), "snap", 1))
        bit = 1
        steps = []
        while bit < tiles:
            x = x[0::2] + xor_send(x[1::2], "space", bit)
            steps.append(x)
            bit *= 2
        return steps

    near_a, near_b = list(range(2, 2 + (half - 2) // 2)), list(range(2 + (half - 2) // 2, half))
    low, high = list(range(half, middle)), list(range(middle, tiles))

    start_low, rest_low = low[: len(low) // 2], low[len(low) // 2 :]
    packed_a = pack_rows(adjoint, 0, rows_a, low)
    packed_n = pack_rows(after(adjoint, packed_a[low[0]]), 0, rows_out, list(range(half)))
    low_a = over_space(packed_a, start_low)
    near_1 = over_space(packed_n, [1])[0]
    got_na = over_space(packed_n, near_a)
    cross_0 = across(packed_n[0])
    own_near = weigh(after(primal, packed_n[0]), weights, table, 0, half, tiles)
    own_far = weigh(after(primal, own_near), weights, table, half, half, tiles)

    done = (*low_a, near_1, *got_na, cross_0[-1], own_far)
    low_a = low_a + over_space(packed_a, rest_low, *done)
    got_nb = over_space(packed_n, near_b, *done)
    cross_1 = across(near_1, *done)
    other_near = xor_send(after(own_near, *done), "snap", 1)
    other_far = xor_send(after(own_far, *done), "snap", 1)
    packed_ah = pack_rows(after(adjoint, own_far), 0, rows_a, high)
    packed_bc = pack_rows(after(adjoint, packed_ah[high[0]]), rows_a, rows_b + rows_c, low)
    packed_b = pack_rows(after(adjoint, packed_bc[low[0]]), rows_a, rows_b, high)
    packed_c = pack_rows(after(adjoint, packed_b[high[0]]), rows_a + rows_b, rows_c, high)

    done = (*low_a, *got_nb, cross_1[-1], other_near, other_far, packed_c[high[0]])
    high_a = over_space(packed_ah, high, *done)
    cross_low_a = across(join(low_a), *done)
    cross_na = across(join(got_na), *done)

    done = (*high_a, cross_low_a[-1], cross_na[-1])
    low_bc = over_space(packed_bc, low, *done)
    cross_nb = across(join(got_nb), *done)
    cross_high_a = across(join(high_a), *done)

    done = (*low_bc, cross_nb[-1], cross_high_a[-1])
    high_b = over_space(packed_b, high, *done)
    cross_low_bc = across(join(low_bc), *done)
    groups = [(g, rows_out, 0) for g in (cross_0, cross_1, cross_na, cross_nb)]
    product = multiply(groups, own_near, after(other_near, *done), where, None, rows_out, halves, members)
    groups = [(cross_low_a, rows_a, 0), (cross_high_a, rows_a, 0)]
    pair_a = multiply(groups, own_far, other_far, where, (product, 0), rows_a, halves, members)

    done = (*high_b, cross_low_bc[-1], pair_a[0])
    high_c = over_space(packed_c, high, *done)
    cross_high_b = across(join(high_b), *done)
    sums_a = add_up(pair_a, *done)

    done = (*high_c, cross_high_b[-1], sums_a[0])
    cross_high_c = across(join(high_c), *done)
    groups = [(cross_low_bc, rows_b + rows_c, 0), (cross_high_b, rows_b, 0)]
    pair_b = multiply(groups, own_far, other_far, where, (product, rows_a), rows_b, halves, members)
    sums_b = add_up(pair_b)
    groups = [(cross_low_bc, rows_b + rows_c, rows_b), (cross_high_c, rows_c, 0)]
    pair_c = multiply(groups, own_far, other_far, where, (product, rows_a + rows_b), rows_c, halves, members)
    sums_c = add_up(pair_c)
    return jnp.concatenate([sums_a[-1][0], sums_b[-1][0], sums_c[-1][0]], axis=0)


def solution(mesh):
    placed = (P("snap", "space"), P("snap", "space"), P("space"), P())
    return jax.shard_map(
        on_device, mesh=mesh, in_specs=placed, out_specs=P("space", "snap"), check_vma=False
    )
```

time: 465 us -> 244 us (0.52)
  waiting for transfers between devices: 360 us -> 128 us
  Pallas kernels: 0 us -> 45.8 us
  starting transfers between devices: 7.54 us -> 51 us
  local copies, waits for them, and re-layouts: 45.8 us -> 15.2 us
  matrix products: 21.2 us -> 0 us
  between operations: 13.5 us -> 0.58 us
  other arithmetic: 16.4 us -> 3.67 us
    all_gather x1 -> x0, waiting for transfers between devices: 157 us -> none  [on_device(): lax.all_gather(moving, 'snap', axis=0, tiled=True)]
    all_to_all x1 -> x0, waiting for transfers between devices: 134 us -> none  [on_device(): lax.all_to_all(outgoing, 'space', split_axis=1, concat_axis=1, tiled=True)]
    ppermute x0 -> x36, waiting for transfers between devices: none -> 128 us  [xor_send(): return lax.ppermute(x, axis, [(i, i ^ k) for i in range(n)])]
    reduce_scatter x1 -> x0, waiting for transfers between devices: 68.7 us -> none  [on_device(): return lax.psum_scatter(product, 'space', scatter_dimension=0, tiled=True)]
    ppermute x0 -> x36, starting transfers between devices: none -> 51 us  [xor_send(): return lax.ppermute(x, axis, [(i, i ^ k) for i in range(n)])]
    pallas_call x0 -> x17, Pallas kernels: none -> 45.8 us  [the longest x4 22.3 us: multiply(): pl.pallas_call(body, in_specs=[pl.BlockSpec(memory_space=pltpu.SMEM)] + [...]
    dot_general x1 -> x0, matrix products: 21.2 us -> none  [on_device(): lax.dot_general(lax.all_gather(moving, 'snap', axis=0, tiled=True), weigh...]
    gather x5 -> x0, local copies, waits for them, and re-layouts: 18.7 us -> none  [the longest x1 8.8 us: on_device(): jnp.take(incoming.reshape(rows_here, pen_dev, PEN_LEN), inverse, axis=1)]
  transfers between devices with their start and end apart: 3 -> 36, of which waited for: 3 -> 21; matrix products, arithmetic and copies ran while one was open for 1% -> 1% of each run, Pallas kernels for 0% -> 17%
where the time goes in v1:
time: 244 us
  waiting for transfers between devices  128 us (52%)
  starting transfers between devices  51 us (21%)
  Pallas kernels  45.8 us (19%)
  local copies, waits for them, and re-layouts  15.2 us (6%)
  other arithmetic  3.67 us (2%)
    ppermute x36, waiting for transfers between devices, xor_send(): return lax.ppermute(x, axis, [(i, i ^ k) for i in range(n)])  128 us
    ppermute x36, starting transfers between devices, xor_send(): return lax.ppermute(x, axis, [(i, i ^ k) for i in range(n)])  51 us
    pallas_call x4, Pallas kernels, multiply(): pl.pallas_call(body, in_specs=[pl.BlockSpec(memory_space=pltpu.SMEM)] + [...  22.3 us
    pallas_call x6, Pallas kernels, pack(): pl.pallas_call(body, in_specs=[smem, smem, vmem], out_specs=[vmem] * len(...  18 us
    unnamed x54, local copies, waits for them, and re-layouts  14.7 us
  transfers between devices with their start and end apart: 36, of which 21 were waited for; matrix products, arithmetic and copies ran while one was open for 1% of the time, Pallas kernels for 17%

profile of v1, /device:TPU:0, one launch (start us, length us, event | category | flops | bytes accessed | tf_op | source)
XLA Modules:
  0.0 243.9 jit_solution(5287510831760345336)
XLA Ops:
  0.1 2.8 %copy-done = bf16[256,12288]{1,0:T(8,128)(2,1)S(1)} copy-done((bf16[256,12288]{1,0:T(8,128)(2,1)S(1)}, bf16[256,12288]{1,0:T(8,128)(2,1)}, u32[]{:S(2)}) %copy-start) | copy-done | bytes 6291480
  3.6 3.4 %shard_map.46 = (bf16[128,1536]{1,0:T(8,128)(2,1)}, bf16[128,1536]{1,0:T(8,128)(2,1)S(1)}) custom-call(s32[768]{0:T(1024)S(1)} %copy-done.10, s32[2]{0:T(128)S(1)} %pad_add_fusion.where_ref, bf16[2,128,12288]{2,1,0:T(8,128)(2,1)S(1)} %bitcast.19), custom_call_target="tpu_custom_call" | custom-call | bytes 6291456 | tf_op jit(solution)/shard_map/pallas_call | solution.py:54
  6.9 4.0 %collective-permute-start = (bf16[128,1536]{1,0:T(8,128)(2,1)}, bf16[128,1536]{1,0:T(8,128)(2,1)S(1)}, u32[]{:S(2)}, u32[]{:S(2)}) collective-permute-start(bf16[128,1536]{1,0:T(8,128)(2,1)} %get-tuple-element.54), channel_id=1, source_target_pairs={{0,16},{4,20},{8,24},{12,28},{16,0},{20,4},{24,8},{28,12},{1,17},{... | collective-permute-start | bytes 1179656 | tf_op jit(solution)/shard_map/ppermute | solution.py:15
  11.0 4.4 %shard_map.47 = (bf16[256,1536]{1,0:T(8,128)(2,1)S(1)}, bf16[256,1536]{1,0:T(8,128)(2,1)}, bf16[256,1536]{1,0:T(8,128)(2,1)}, bf16[256,1536]{1,0:T(8,128)(2,1)S(1)}) custom-call(s32[768]{0:T(1024)S(1)} %copy-done.11, s32[2]{0:T(128)S(1)} %pad_add_fusion.where_ref, bf16[2,128,12288]{2,1,0:T(8,128)(2,1)S(1)} %bitcast.20), custom_call_target="tpu_custom_call" | custom-call | bytes 12582912 | tf_op jit(solution)/shard_map/pallas_call | solution.py:54
  21.8 4.6 %copy-done.6 = bf16[512,12288]{1,0:T(8,128)(2,1)S(1)} copy-done((bf16[512,12288]{1,0:T(8,128)(2,1)S(1)}, bf16[512,12288]{1,0:T(8,128)(2,1)}, u32[]{:S(2)}) %copy-start.6) | copy-done | bytes 12582936
  31.0 4.5 %collective-permute-done.1.refs_2_ = bf16[256,1536]{1,0:T(8,128)(2,1)S(1)} collective-permute-done((bf16[256,1536]{1,0:T(8,128)(2,1)}, bf16[256,1536]{1,0:T(8,128)(2,1)S(1)}, u32[]{:S(2)}, u32[]{:S(2)}) %collective-permute-start.1) | collective-permute-done | bytes 786464 | tf_op jit(solution)/shard_map/ppermute | solution.py:15
  35.5 8.5 %collective-permute-done.2.refs_4_ = bf16[256,1536]{1,0:T(8,128)(2,1)S(1)} collective-permute-done((bf16[256,1536]{1,0:T(8,128)(2,1)}, bf16[256,1536]{1,0:T(8,128)(2,1)S(1)}, u32[]{:S(2)}, u32[]{:S(2)}) %collective-permute-start.2) | collective-permute-done | bytes 786464 | tf_op jit(solution)/shard_map/ppermute | solution.py:15
  46.1 3.8 %collective-permute-start.4 = (bf16[128,1536]{1,0:T(8,128)(2,1)S(1)}, bf16[128,1536]{1,0:T(8,128)(2,1)S(1)}, u32[]{:S(2)}, u32[]{:S(2)}) collective-permute-start(bf16[128,1536]{1,0:T(8,128)(2,1)S(1)} %get-tuple-element.62), channel_id=1, source_target_pairs={{0,20},{4,16},{8,28},{12,24},{16,4},{20,0},{24,12},{28,8},{1,21},{... | collective-permute-start | bytes 1179656 | tf_op jit(solution)/shard_map/ppermute | solution.py:15
  60.2 10.0 %collective-permute-done.4.refs_1_ = bf16[128,1536]{1,0:T(8,128)(2,1)S(1)} collective-permute-done((bf16[128,1536]{1,0:T(8,128)(2,1)S(1)}, bf16[128,1536]{1,0:T(8,128)(2,1)S(1)}, u32[]{:S(2)}, u32[]{:S(2)}) %collective-permute-start.4) | collective-permute-done | bytes 393248 | tf_op jit(solution)/shard_map/ppermute | solution.py:15
  70.4 3.0 %collective-permute-done.5.refs_6_ = bf16[256,1536]{1,0:T(8,128)(2,1)S(1)} collective-permute-done((bf16[256,1536]{1,0:T(8,128)(2,1)S(1)}, bf16[256,1536]{1,0:T(8,128)(2,1)S(1)}, u32[]{:S(2)}, u32[]{:S(2)}) %collective-permute-start.5) | collective-permute-done | bytes 786464 | tf_op jit(solution)/shard_map/ppermute | solution.py:15
  79.3 10.1 %collective-permute-done.10.refs_0_ = bf16[128,1536]{1,0:T(8,128)(2,1)S(1)} collective-permute-done((bf16[128,1536]{1,0:T(8,128)(2,1)S(1)}, bf16[128,1536]{1,0:T(8,128)(2,1)S(1)}, u32[]{:S(2)}, u32[]{:S(2)}) %collective-permute-start.10) | collective-permute-done | bytes 393248 | tf_op jit(solution)/shard_map/ppermute | solution.py:15
  89.4 6.1 %collective-permute-done.11.refs_1_ = bf16[128,1536]{1,0:T(8,128)(2,1)S(1)} collective-permute-done((bf16[128,1536]{1,0:T(8,128)(2,1)S(1)}, bf16[128,1536]{1,0:T(8,128)(2,1)S(1)}, u32[]{:S(2)}, u32[]{:S(2)}) %collective-permute-start.11) | collective-permute-done | bytes 393248 | tf_op jit(solution)/shard_map/ppermute | solution.py:15
  95.6 13.3 %collective-permute-done.12.refs_5_ = bf16[256,1536]{1,0:T(8,128)(2,1)S(1)} collective-permute-done((bf16[256,1536]{1,0:T(8,128)(2,1)S(1)}, bf16[256,1536]{1,0:T(8,128)(2,1)S(1)}, u32[]{:S(2)}, u32[]{:S(2)}) %collective-permute-start.12) | collective-permute-done | bytes 786464 | tf_op jit(solution)/shard_map/ppermute | solution.py:15
  111.0 3.4 %collective-permute-start.15 = (bf16[128,1536]{1,0:T(8,128)(2,1)S(1)}, bf16[128,1536]{1,0:T(8,128)(2,1)S(1)}, u32[]{:S(2)}, u32[]{:S(2)}) collective-permute-start(bf16[128,1536]{1,0:T(8,128)(2,1)S(1)} %get-tuple-element.83), channel_id=1, source_target_pairs={{0,16},{4,20},{8,24},{12,28},{16,0},{20,4},{24,8},{28,12},{1,17},{... | collective-permute-start | bytes 1179656 | tf_op jit(solution)/shard_map/ppermute | solution.py:15
  114.4 26.9 %collective-permute-done.15.refs_0_ = bf16[128,1536]{1,0:T(8,128)(2,1)S(1)} collective-permute-done((bf16[128,1536]{1,0:T(8,128)(2,1)S(1)}, bf16[128,1536]{1,0:T(8,128)(2,1)S(1)}, u32[]{:S(2)}, u32[]{:S(2)}) %collective-permute-start.15) | collective-permute-done | bytes 393248 | tf_op jit(solution)/shard_map/ppermute | solution.py:15
  141.2 5.5 %collective-permute-done.16.refs_1_ = bf16[128,1536]{1,0:T(8,128)(2,1)S(1)} collective-permute-done((bf16[128,1536]{1,0:T(8,128)(2,1)S(1)}, bf16[128,1536]{1,0:T(8,128)(2,1)S(1)}, u32[]{:S(2)}, u32[]{:S(2)}) %collective-permute-start.16) | collective-permute-done | bytes 393248 | tf_op jit(solution)/shard_map/ppermute | solution.py:15
  147.1 2.8 %collective-permute-start.17 = (bf16[96,1536]{1,0:T(8,128)(2,1)S(1)}, bf16[96,1536]{1,0:T(8,128)(2,1)S(1)}, u32[]{:S(2)}, u32[]{:S(2)}) collective-permute-start(bf16[96,1536]{1,0:T(8,128)(2,1)S(1)} %get-tuple-element.89), channel_id=1, source_target_pairs={{0,24},{4,28},{8,16},{12,20},{16,8},{20,12},{24,0},{28,4},{1,25},{... | collective-permute-start | bytes 884744 | tf_op jit(solution)/shard_map/ppermute | solution.py:15
  154.6 7.8 %shard_map.56.refs_6_ = f32[2,256,1024]{2,1,0:T(8,128)S(1)} custom-call(s32[2]{0:T(128)S(1)} %pad_add_fusion.where_ref, bf16[256,1536]{1,0:T(8,128)(2,1)S(1)} %copy-done.14, bf16[256,1536]{1,0:T(8,128)(2,1)} %collective-permute-done.3.refs_1_, bf16[256,1536]{1,0:T(8,128)(2,1)S(1)} %copy-done.16, bf16[256,1536]{1,0:T(8,128)(2,1)S(1)} %collective-permute-done.6.refs_3_, ...), custom_call_target="tpu_custom_call" | custom-call | flops 6442450944 | bytes 18874368 | tf_op jit(solution)/shard_map/pallas_call | solution.py:177
  162.4 4.8 %shard_map.57 = (f32[4,64,512]{2,1,0:T(8,128)S(1)}, f32[4,64,512]{2,1,0:T(8,128)}) custom-call(s32[2]{0:T(128)S(1)} %pad_add_fusion.where_ref, bf16[2,128,1536]{2,1,0:T(8,128)(2,1)S(1)} %shard_map.50.refs_0_, bf16[2,128,1536]{2,1,0:T(8,128)(2,1)S(1)} %collective-permute-done.9.refs_1_, bf16[2,128,1536]{2,1,0:T(8,128)(2,1)S(1)} %shard_map.55.refs_2_, ...), custom_call_target="tpu_custom_call" | custom-call | flops 3221225472 | bytes 15728640 | tf_op jit(solution)/shard_map/pallas_call | solution.py:177
  176.1 11.3 %collective-permute-done.24.refs_3_ = bf16[2,96,1536]{2,1,0:T(8,128)(2,1)} collective-permute-done((bf16[2,96,1536]{2,1,0:T(8,128)(2,1)S(1)}, bf16[2,96,1536]{2,1,0:T(8,128)(2,1)}, u32[]{:S(2)}, u32[]{:S(2)}) %collective-permute-start.24) | collective-permute-done | bytes 589856 | tf_op jit(solution)/shard_map/ppermute | solution.py:15
  187.4 2.8 %copy-done.4 = bf16[4,512,1536]{2,1,0:T(8,128)(2,1)S(1)} copy-done((bf16[4,512,1536]{2,1,0:T(8,128)(2,1)S(1)}, bf16[4,512,1536]{2,1,0:T(8,128)(2,1)}, u32[]{:S(2)}) %copy-start.4) | copy-done | bytes 6291480
  190.2 5.3 %shard_map.60 = (f32[4,48,512]{2,1,0:T(8,128)S(1)}, f32[4,48,512]{2,1,0:T(8,128)S(1)}) custom-call(s32[2]{0:T(128)S(1)} %pad_add_fusion.where_ref, bf16[2,128,1536]{2,1,0:T(8,128)(2,1)S(1)} %shard_map.58.refs_0_, bf16[2,128,1536]{2,1,0:T(8,128)(2,1)S(1)} %copy-done.8, bf16[2,96,1536]{2,1,0:T(8,128)(2,1)S(1)} %shard_map.59.refs_2_, ...), custom_call_target="tpu_custom_call" | custom-call | flops 2415919104 | bytes 14942208 | tf_op jit(solution)/shard_map/pallas_call | solution.py:177
  195.6 3.5 %collective-permute-start.29 = (bf16[32,1536]{1,0:T(8,128)(2,1)S(1)}, bf16[32,1536]{1,0:T(8,128)(2,1)S(1)}, u32[]{:S(2)}, u32[]{:S(2)}) collective-permute-start(bf16[32,1536]{1,0:T(8,128)(2,1)S(1)} %copy-done.24), channel_id=1, source_target_pairs={{0,24},{4,28},{8,16},{12,20},{16,8},{20,12},{24,0},{28,4},{1,25},{... | collective-permute-start | bytes 294920 | tf_op jit(solution)/shard_map/ppermute | solution.py:15
  199.4 3.7 %collective-permute-done.29.refs_0_ = bf16[32,1536]{1,0:T(8,128)(2,1)S(1)} collective-permute-done((bf16[32,1536]{1,0:T(8,128)(2,1)S(1)}, bf16[32,1536]{1,0:T(8,128)(2,1)S(1)}, u32[]{:S(2)}, u32[]{:S(2)}) %collective-permute-start.29) | collective-permute-done | bytes 98336 | tf_op jit(solution)/shard_map/ppermute | solution.py:15
  203.1 3.6 %collective-permute-done.30.refs_1_ = bf16[32,1536]{1,0:T(8,128)(2,1)S(1)} collective-permute-done((bf16[32,1536]{1,0:T(8,128)(2,1)S(1)}, bf16[32,1536]{1,0:T(8,128)(2,1)S(1)}, u32[]{:S(2)}, u32[]{:S(2)}) %collective-permute-start.30) | collective-permute-done | bytes 98336 | tf_op jit(solution)/shard_map/ppermute | solution.py:15
  207.2 3.9 %collective-permute-start.22 = (f32[2,64,512]{2,1,0:T(8,128)S(1)}, f32[2,64,512]{2,1,0:T(8,128)S(1)}, u32[]{:S(2)}, u32[]{:S(2)}) collective-permute-start(f32[2,64,512]{2,1,0:T(8,128)S(1)} %slice.63), channel_id=1, source_target_pairs={{0,8},{4,12},{8,0},{12,4},{16,24},{20,28},{24,16},{28,20},{1,9},{5... | collective-permute-start | bytes 786440 | tf_op jit(solution)/shard_map/ppermute | solution.py:15
  213.1 4.2 %collective-permute-done.31.refs_3_ = bf16[2,32,1536]{2,1,0:T(8,128)(2,1)S(1)} collective-permute-done((bf16[2,32,1536]{2,1,0:T(8,128)(2,1)S(1)}, bf16[2,32,1536]{2,1,0:T(8,128)(2,1)S(1)}, u32[]{:S(2)}, u32[]{:S(2)}) %collective-permute-start.31) | collective-permute-done | bytes 196640 | tf_op jit(solution)/shard_map/ppermute | solution.py:15
  217.3 4.4 %shard_map.62 = (f32[4,16,512]{2,1,0:T(8,128)S(1)}, f32[4,16,512]{2,1,0:T(8,128)S(1)}) custom-call(s32[2]{0:T(128)S(1)} %pad_add_fusion.where_ref, bf16[2,128,1536]{2,1,0:T(8,128)(2,1)S(1)} %shard_map.58.refs_0_, bf16[2,128,1536]{2,1,0:T(8,128)(2,1)S(1)} %copy-done.8, bf16[2,32,1536]{2,1,0:T(8,128)(2,1)S(1)} %shard_map.61.refs_2_, ...), custom_call_target="tpu_custom_call" | custom-call | flops 805306368 | bytes 13369344 | tf_op jit(solution)/shard_map/pallas_call | solution.py:177
  225.9 2.9 %collective-permute-done.33 = f32[4,16,512]{2,1,0:T(8,128)S(1)} collective-permute-done((f32[4,16,512]{2,1,0:T(8,128)S(1)}, f32[4,16,512]{2,1,0:T(8,128)S(1)}, u32[]{:S(2)}, u32[]{:S(2)}) %collective-permute-start.33) | collective-permute-done | bytes 131104 | tf_op jit(solution)/shard_map/ppermute | solution.py:15
  231.5 3.7 %collective-permute-done.34 = f32[2,16,512]{2,1,0:T(8,128)S(1)} collective-permute-done((f32[2,16,512]{2,1,0:T(8,128)S(1)}, f32[2,16,512]{2,1,0:T(8,128)S(1)}, u32[]{:S(2)}, u32[]{:S(2)}) %collective-permute-start.34) | collective-permute-done | bytes 65568 | tf_op jit(solution)/shard_map/ppermute | solution.py:15
  235.6 2.7 %collective-permute-start.28 = (f32[1,48,512]{2,1,0:T(8,128)S(1)}, f32[1,48,512]{2,1,0:T(8,128)S(1)}, u32[]{:S(2)}, u32[]{:S(2)}) collective-permute-start(f32[1,48,512]{2,1,0:T(8,128)S(1)} %slice.81), channel_id=1, source_target_pairs={{0,16},{4,20},{8,24},{12,28},{16,0},{20,4},{24,8},{28,12},{1,17},{... | collective-permute-start | bytes 294920 | tf_op jit(solution)/shard_map/ppermute | solution.py:15
  238.3 2.8 %collective-permute-done.35 = f32[1,16,512]{2,1,0:T(8,128)S(1)} collective-permute-done((f32[1,16,512]{2,1,0:T(8,128)S(1)}, f32[1,16,512]{2,1,0:T(8,128)S(1)}, u32[]{:S(2)}, u32[]{:S(2)}) %collective-permute-start.35) | collective-permute-done | bytes 32800 | tf_op jit(solution)/shard_map/ppermute | solution.py:15
  (152 shorter events, 58.8 us)
Async XLA Ops:
  6.9 24.0 %collective-permute-start = (bf16[128,1536]{1,0:T(8,128)(2,1)}, bf16[128,1536]{1,0:T(8,128)(2,1)S(1)}, u32[]{:S(2)}, u32[]{:S(2)}) collective-permute-start(bf16[128,1536]{1,0:T(8,128)(2,1)} %get-tuple-element.54), channel_id=1, source_target_pairs={{0,16},{4,20},{8,24},{12,28},{16,0},{20,4},{24,8},{28,12},{1,17},{... | collective-permute-start | bytes 1179656 | tf_op jit(solution)/shard_map/ppermute | solution.py:15
  16.3 19.2 %collective-permute-start.1 = (bf16[256,1536]{1,0:T(8,128)(2,1)}, bf16[256,1536]{1,0:T(8,128)(2,1)S(1)}, u32[]{:S(2)}, u32[]{:S(2)}) collective-permute-start(bf16[256,1536]{1,0:T(8,128)(2,1)} %get-tuple-element.57), channel_id=1, source_target_pairs={{0,4},{4,0},{8,12},{12,8},{16,20},{20,16},{24,28},{28,24},{1,5},{5... | collective-permute-start | bytes 2359304 | tf_op jit(solution)/shard_map/ppermute | solution.py:15
  17.8 26.2 %collective-permute-start.2 = (bf16[256,1536]{1,0:T(8,128)(2,1)}, bf16[256,1536]{1,0:T(8,128)(2,1)S(1)}, u32[]{:S(2)}, u32[]{:S(2)}) collective-permute-start(bf16[256,1536]{1,0:T(8,128)(2,1)} %get-tuple-element.58), channel_id=1, source_target_pairs={{0,8},{4,12},{8,0},{12,4},{16,24},{20,28},{24,16},{28,20},{1,9},{5... | collective-permute-start | bytes 2359304 | tf_op jit(solution)/shard_map/ppermute | solution.py:15
  19.4 24.6 %collective-permute-start.3 = (bf16[256,1536]{1,0:T(8,128)(2,1)S(1)}, bf16[256,1536]{1,0:T(8,128)(2,1)}, u32[]{:S(2)}, u32[]{:S(2)}) collective-permute-start(bf16[256,1536]{1,0:T(8,128)(2,1)S(1)} %get-tuple-element.59.refs_0_), channel_id=1, source_target_pairs={{0,2},{1,3},{2,0},{3,1},{4,6},{5,7},{6,4},{7,5},{8,10},{9,11},{10,... | collective-permute-start | bytes 2359304 | tf_op jit(solution)/shard_map/ppermute | solution.py:15
  44.0 29.4 %collective-permute-start.7 = (bf16[4,512,1536]{2,1,0:T(8,128)(2,1)S(1)}, bf16[4,512,1536]{2,1,0:T(8,128)(2,1)S(1)}, u32[]{:S(2)}, u32[]{:S(2)}) collective-permute-start(bf16[4,512,1536]{2,1,0:T(8,128)(2,1)S(1)} %shard_map.48.refs_8_), channel_id=1, source_target_pairs={{0,1},{1,0},{2,3},{3,2},{4,5},{5,4},{6,7},{7,6},{8,9},{9,8},{10,11... | collective-permute-start | bytes 18874376 | tf_op jit(solution)/shard_map/ppermute | solution.py:15
  44.0 29.4 %collective-permute-start.8 = (bf16[4,512,1536]{2,1,0:T(8,128)(2,1)S(1)}, bf16[4,512,1536]{2,1,0:T(8,128)(2,1)S(1)}, u32[]{:S(2)}, u32[]{:S(2)}) collective-permute-start(bf16[4,512,1536]{2,1,0:T(8,128)(2,1)S(1)} %shard_map.49.refs_4_), channel_id=1, source_target_pairs={{0,1},{1,0},{2,3},{3,2},{4,5},{5,4},{6,7},{7,6},{8,9},{9,8},{10,11... | collective-permute-start | bytes 18874376 | tf_op jit(solution)/shard_map/ppermute | solution.py:15
  44.5 28.8 %collective-permute-start.5 = (bf16[256,1536]{1,0:T(8,128)(2,1)S(1)}, bf16[256,1536]{1,0:T(8,128)(2,1)S(1)}, u32[]{:S(2)}, u32[]{:S(2)}) collective-permute-start(bf16[256,1536]{1,0:T(8,128)(2,1)S(1)} %copy-done.20), channel_id=1, source_target_pairs={{0,12},{4,8},{8,4},{12,0},{16,28},{20,24},{24,20},{28,16},{1,13},{... | collective-permute-start | bytes 2359304 | tf_op jit(solution)/shard_map/ppermute | solution.py:15
  44.5 28.8 %collective-permute-start.6 = (bf16[256,1536]{1,0:T(8,128)(2,1)S(1)}, bf16[256,1536]{1,0:T(8,128)(2,1)S(1)}, u32[]{:S(2)}, u32[]{:S(2)}) collective-permute-start(bf16[256,1536]{1,0:T(8,128)(2,1)S(1)} %collective-permute-done.1.refs_2_), channel_id=1, source_target_pairs={{0,2},{1,3},{2,0},{3,1},{4,6},{5,7},{6,4},{7,5},{8,10},{9,11},{10,... | collective-permute-start | bytes 2359304 | tf_op jit(solution)/shard_map/ppermute | solution.py:15
  46.1 24.2 %collective-permute-start.4 = (bf16[128,1536]{1,0:T(8,128)(2,1)S(1)}, bf16[128,1536]{1,0:T(8,128)(2,1)S(1)}, u32[]{:S(2)}, u32[]{:S(2)}) collective-permute-start(bf16[128,1536]{1,0:T(8,128)(2,1)S(1)} %get-tuple-element.62), channel_id=1, source_target_pairs={{0,20},{4,16},{8,28},{12,24},{16,4},{20,0},{24,12},{28,8},{1,21},{... | collective-permute-start | bytes 1179656 | tf_op jit(solution)/shard_map/ppermute | solution.py:15
  73.4 22.3 %collective-permute-start.9 = (bf16[2,128,1536]{2,1,0:T(8,128)(2,1)S(1)}, bf16[2,128,1536]{2,1,0:T(8,128)(2,1)S(1)}, u32[]{:S(2)}, u32[]{:S(2)}) collective-permute-start(bf16[2,128,1536]{2,1,0:T(8,128)(2,1)S(1)} %shard_map.50.refs_0_), channel_id=1, source_target_pairs={{0,2},{1,3},{2,0},{3,1},{4,6},{5,7},{6,4},{7,5},{8,10},{9,11},{10,... | collective-permute-start | bytes 2359304 | tf_op jit(solution)/shard_map/ppermute | solution.py:15
  75.0 34.0 %collective-permute-start.12 = (bf16[256,1536]{1,0:T(8,128)(2,1)S(1)}, bf16[256,1536]{1,0:T(8,128)(2,1)S(1)}, u32[]{:S(2)}, u32[]{:S(2)}) collective-permute-start(bf16[256,1536]{1,0:T(8,128)(2,1)S(1)} %collective-permute-done.2.refs_4_), channel_id=1, source_target_pairs={{0,2},{1,3},{2,0},{3,1},{4,6},{5,7},{6,4},{7,5},{8,10},{9,11},{10,... | collective-permute-start | bytes 2359304 | tf_op jit(solution)/shard_map/ppermute | solution.py:15
  75.5 13.9 %collective-permute-start.10 = (bf16[128,1536]{1,0:T(8,128)(2,1)S(1)}, bf16[128,1536]{1,0:T(8,128)(2,1)S(1)}, u32[]{:S(2)}, u32[]{:S(2)}) collective-permute-start(bf16[128,1536]{1,0:T(8,128)(2,1)S(1)} %get-tuple-element.77), channel_id=1, source_target_pairs={{0,24},{4,28},{8,16},{12,20},{16,8},{20,12},{24,0},{28,4},{1,25},{... | collective-permute-start | bytes 1179656 | tf_op jit(solution)/shard_map/ppermute | solution.py:15
  77.9 17.6 %collective-permute-start.11 = (bf16[128,1536]{1,0:T(8,128)(2,1)S(1)}, bf16[128,1536]{1,0:T(8,128)(2,1)S(1)}, u32[]{:S(2)}, u32[]{:S(2)}) collective-permute-start(bf16[128,1536]{1,0:T(8,128)(2,1)S(1)} %get-tuple-element.79), channel_id=1, source_target_pairs={{0,28},{4,24},{8,20},{12,16},{16,12},{20,8},{24,4},{28,0},{1,29},{... | collective-permute-start | bytes 1179656 | tf_op jit(solution)/shard_map/ppermute | solution.py:15
  109.0 38.1 %collective-permute-start.13 = (bf16[2,128,1536]{2,1,0:T(8,128)(2,1)S(1)}, bf16[2,128,1536]{2,1,0:T(8,128)(2,1)S(1)}, u32[]{:S(2)}, u32[]{:S(2)}) collective-permute-start(bf16[2,128,1536]{2,1,0:T(8,128)(2,1)S(1)} %shard_map.55.refs_2_), channel_id=1, source_target_pairs={{0,2},{1,3},{2,0},{3,1},{4,6},{5,7},{6,4},{7,5},{8,10},{9,11},{10,... | collective-permute-start | bytes 2359304 | tf_op jit(solution)/shard_map/ppermute | solution.py:15
  110.5 36.5 %collective-permute-start.14 = (bf16[256,1536]{1,0:T(8,128)(2,1)S(1)}, bf16[256,1536]{1,0:T(8,128)(2,1)S(1)}, u32[]{:S(2)}, u32[]{:S(2)}) collective-permute-start(bf16[256,1536]{1,0:T(8,128)(2,1)S(1)} %collective-permute-done.5.refs_6_), channel_id=1, source_target_pairs={{0,2},{1,3},{2,0},{3,1},{4,6},{5,7},{6,4},{7,5},{8,10},{9,11},{10,... | collective-permute-start | bytes 2359304 | tf_op jit(solution)/shard_map/ppermute | solution.py:15
  111.0 30.2 %collective-permute-start.15 = (bf16[128,1536]{1,0:T(8,128)(2,1)S(1)}, bf16[128,1536]{1,0:T(8,128)(2,1)S(1)}, u32[]{:S(2)}, u32[]{:S(2)}) collective-permute-start(bf16[128,1536]{1,0:T(8,128)(2,1)S(1)} %get-tuple-element.83), channel_id=1, source_target_pairs={{0,16},{4,20},{8,24},{12,28},{16,0},{20,4},{24,8},{28,12},{1,17},{... | collective-permute-start | bytes 1179656 | tf_op jit(solution)/shard_map/ppermute | solution.py:15
  114.4 32.4 %collective-permute-start.16 = (bf16[128,1536]{1,0:T(8,128)(2,1)S(1)}, bf16[128,1536]{1,0:T(8,128)(2,1)S(1)}, u32[]{:S(2)}, u32[]{:S(2)}) collective-permute-start(bf16[128,1536]{1,0:T(8,128)(2,1)S(1)} %get-tuple-element.85), channel_id=1, source_target_pairs={{0,20},{4,16},{8,28},{12,24},{16,4},{20,0},{24,12},{28,8},{1,21},{... | collective-permute-start | bytes 1179656 | tf_op jit(solution)/shard_map/ppermute | solution.py:15
  147.1 21.0 %collective-permute-start.17 = (bf16[96,1536]{1,0:T(8,128)(2,1)S(1)}, bf16[96,1536]{1,0:T(8,128)(2,1)S(1)}, u32[]{:S(2)}, u32[]{:S(2)}) collective-permute-start(bf16[96,1536]{1,0:T(8,128)(2,1)S(1)} %get-tuple-element.89), channel_id=1, source_target_pairs={{0,24},{4,28},{8,16},{12,20},{16,8},{20,12},{24,0},{28,4},{1,25},{... | collective-permute-start | bytes 884744 | tf_op jit(solution)/shard_map/ppermute | solution.py:15
  149.8 18.2 %collective-permute-start.18 = (bf16[96,1536]{1,0:T(8,128)(2,1)S(1)}, bf16[96,1536]{1,0:T(8,128)(2,1)S(1)}, u32[]{:S(2)}, u32[]{:S(2)}) collective-permute-start(bf16[96,1536]{1,0:T(8,128)(2,1)S(1)} %get-tuple-element.91), channel_id=1, source_target_pairs={{0,28},{4,24},{8,20},{12,16},{16,12},{20,8},{24,4},{28,0},{1,29},{... | collective-permute-start | bytes 884744 | tf_op jit(solution)/shard_map/ppermute | solution.py:15
  151.8 18.6 %collective-permute-start.19 = (bf16[2,128,1536]{2,1,0:T(8,128)(2,1)S(1)}, bf16[2,128,1536]{2,1,0:T(8,128)(2,1)S(1)}, u32[]{:S(2)}, u32[]{:S(2)}) collective-permute-start(bf16[2,128,1536]{2,1,0:T(8,128)(2,1)S(1)} %shard_map.58.refs_0_), channel_id=1, source_target_pairs={{0,2},{1,3},{2,0},{3,1},{4,6},{5,7},{6,4},{7,5},{8,10},{9,11},{10,... | collective-permute-start | bytes 2359304 | tf_op jit(solution)/shard_map/ppermute | solution.py:15
  171.5 15.9 %collective-permute-start.24 = (bf16[2,96,1536]{2,1,0:T(8,128)(2,1)S(1)}, bf16[2,96,1536]{2,1,0:T(8,128)(2,1)}, u32[]{:S(2)}, u32[]{:S(2)}) collective-permute-start(bf16[2,96,1536]{2,1,0:T(8,128)(2,1)S(1)} %shard_map.59.refs_2_), channel_id=1, source_target_pairs={{0,2},{1,3},{2,0},{3,1},{4,6},{5,7},{6,4},{7,5},{8,10},{9,11},{10,... | collective-permute-start | bytes 1769480 | tf_op jit(solution)/shard_map/ppermute | solution.py:15
  175.5 31.6 %collective-permute-start.21 = (f32[4,64,512]{2,1,0:T(8,128)S(1)}, f32[4,64,512]{2,1,0:T(8,128)S(1)}, u32[]{:S(2)}, u32[]{:S(2)}) collective-permute-start(f32[4,64,512]{2,1,0:T(8,128)S(1)} %slice.61), channel_id=1, source_target_pairs={{0,4},{4,0},{8,12},{12,8},{16,20},{20,16},{24,28},{28,24},{1,5},{5... | collective-permute-start | bytes 1572872 | tf_op jit(solution)/shard_map/ppermute | solution.py:15
  195.5 17.1 %collective-permute-start.25 = (f32[4,48,512]{2,1,0:T(8,128)S(1)}, f32[4,48,512]{2,1,0:T(8,128)S(1)}, u32[]{:S(2)}, u32[]{:S(2)}) collective-permute-start(f32[4,48,512]{2,1,0:T(8,128)S(1)} %get-tuple-element.96), channel_id=1, source_target_pairs={{0,1},{1,0},{2,3},{3,2},{4,5},{5,4},{6,7},{7,6},{8,9},{9,8},{10,11... | collective-permute-start | bytes 1179656 | tf_op jit(solution)/shard_map/ppermute | solution.py:15
  195.6 7.6 %collective-permute-start.29 = (bf16[32,1536]{1,0:T(8,128)(2,1)S(1)}, bf16[32,1536]{1,0:T(8,128)(2,1)S(1)}, u32[]{:S(2)}, u32[]{:S(2)}) collective-permute-start(bf16[32,1536]{1,0:T(8,128)(2,1)S(1)} %copy-done.24), channel_id=1, source_target_pairs={{0,24},{4,28},{8,16},{12,20},{16,8},{20,12},{24,0},{28,4},{1,25},{... | collective-permute-start | bytes 294920 | tf_op jit(solution)/shard_map/ppermute | solution.py:15
  199.1 7.7 %collective-permute-start.30 = (bf16[32,1536]{1,0:T(8,128)(2,1)S(1)}, bf16[32,1536]{1,0:T(8,128)(2,1)S(1)}, u32[]{:S(2)}, u32[]{:S(2)}) collective-permute-start(bf16[32,1536]{1,0:T(8,128)(2,1)S(1)} %copy-done.22), channel_id=1, source_target_pairs={{0,28},{4,24},{8,20},{12,16},{16,12},{20,8},{24,4},{28,0},{1,29},{... | collective-permute-start | bytes 294920 | tf_op jit(solution)/shard_map/ppermute | solution.py:15
  207.2 14.6 %collective-permute-start.22 = (f32[2,64,512]{2,1,0:T(8,128)S(1)}, f32[2,64,512]{2,1,0:T(8,128)S(1)}, u32[]{:S(2)}, u32[]{:S(2)}) collective-permute-start(f32[2,64,512]{2,1,0:T(8,128)S(1)} %slice.63), channel_id=1, source_target_pairs={{0,8},{4,12},{8,0},{12,4},{16,24},{20,28},{24,16},{28,20},{1,9},{5... | collective-permute-start | bytes 786440 | tf_op jit(solution)/shard_map/ppermute | solution.py:15
  211.1 6.2 %collective-permute-start.31 = (bf16[2,32,1536]{2,1,0:T(8,128)(2,1)S(1)}, bf16[2,32,1536]{2,1,0:T(8,128)(2,1)S(1)}, u32[]{:S(2)}, u32[]{:S(2)}) collective-permute-start(bf16[2,32,1536]{2,1,0:T(8,128)(2,1)S(1)} %shard_map.61.refs_2_), channel_id=1, source_target_pairs={{0,2},{1,3},{2,0},{3,1},{4,6},{5,7},{6,4},{7,5},{8,10},{9,11},{10,... | collective-permute-start | bytes 589832 | tf_op jit(solution)/shard_map/ppermute | solution.py:15
  212.9 11.2 %collective-permute-start.26 = (f32[4,48,512]{2,1,0:T(8,128)S(1)}, f32[4,48,512]{2,1,0:T(8,128)S(1)}, u32[]{:S(2)}, u32[]{:S(2)}) collective-permute-start(f32[4,48,512]{2,1,0:T(8,128)S(1)} %slice.67), channel_id=1, source_target_pairs={{0,4},{4,0},{8,12},{12,8},{16,20},{20,16},{24,28},{28,24},{1,5},{5... | collective-permute-start | bytes 1179656 | tf_op jit(solution)/shard_map/ppermute | solution.py:15
  221.9 9.6 %collective-permute-start.23 = (f32[1,64,512]{2,1,0:T(8,128)S(1)}, f32[1,64,512]{2,1,0:T(8,128)S(1)}, u32[]{:S(2)}, u32[]{:S(2)}) collective-permute-start(f32[1,64,512]{2,1,0:T(8,128)S(1)} %slice.79), channel_id=1, source_target_pairs={{0,16},{4,20},{8,24},{12,28},{16,0},{20,4},{24,8},{28,12},{1,17},{... | collective-permute-start | bytes 393224 | tf_op jit(solution)/shard_map/ppermute | solution.py:15
  224.2 11.3 %collective-permute-start.27 = (f32[2,48,512]{2,1,0:T(8,128)S(1)}, f32[2,48,512]{2,1,0:T(8,128)S(1)}, u32[]{:S(2)}, u32[]{:S(2)}) collective-permute-start(f32[2,48,512]{2,1,0:T(8,128)S(1)} %slice.69), channel_id=1, source_target_pairs={{0,8},{4,12},{8,0},{12,4},{16,24},{20,28},{24,16},{28,20},{1,9},{5... | collective-permute-start | bytes 589832 | tf_op jit(solution)/shard_map/ppermute | solution.py:15
  228.9 6.2 %collective-permute-start.34 = (f32[2,16,512]{2,1,0:T(8,128)S(1)}, f32[2,16,512]{2,1,0:T(8,128)S(1)}, u32[]{:S(2)}, u32[]{:S(2)}) collective-permute-start(f32[2,16,512]{2,1,0:T(8,128)S(1)} %slice.75), channel_id=1, source_target_pairs={{0,8},{4,12},{8,0},{12,4},{16,24},{20,28},{24,16},{28,20},{1,9},{5... | collective-permute-start | bytes 196616 | tf_op jit(solution)/shard_map/ppermute | solution.py:15
  235.6 7.6 %collective-permute-start.28 = (f32[1,48,512]{2,1,0:T(8,128)S(1)}, f32[1,48,512]{2,1,0:T(8,128)S(1)}, u32[]{:S(2)}, u32[]{:S(2)}) collective-permute-start(f32[1,48,512]{2,1,0:T(8,128)S(1)} %slice.81), channel_id=1, source_target_pairs={{0,16},{4,20},{8,24},{12,28},{16,0},{20,4},{24,8},{28,12},{1,17},{... | collective-permute-start | bytes 294920 | tf_op jit(solution)/shard_map/ppermute | solution.py:15
  (31 other events, 893.6 us)

commit v2 on v1

v2 whole, which is shorter than its diff:
```python
import jax
import jax.numpy as jnp
from jax import lax
from jax.experimental import pallas as pl
from jax.experimental.pallas import tpu as pltpu
from jax.sharding import PartitionSpec as P

PEN_LEN = 128
ROWS = 16
COST_SCALE = 1
LIMIT = 50


def xor_send(x, axis, k):
    n = lax.axis_size(axis)
    return lax.ppermute(x, axis, [(i, i ^ k) for i in range(n)])


def params(mebibytes=8):
    return pltpu.CompilerParams(vmem_limit_bytes=mebibytes * 1024 * 1024)


def cost(flops, nbytes):
    return pl.CostEstimate(flops=flops // COST_SCALE, bytes_accessed=nbytes // COST_SCALE, transcendentals=0)


def pack(adjoint, table, where, first, count, ks, tiles):
    halves, _, points = adjoint.shape
    pen_dev = points // PEN_LEN
    share = pen_dev // tiles
    build = table.shape[0] != pen_dev
    magic = (1 << 20) // pen_dev + 1
    exact = all(x * magic >> 20 == x // pen_dev for x in range(tiles * pen_dev))

    def body(table_ref, where_ref, in_ref, *refs):
        outs = refs[: len(ks)]
        if build:
            made, seen = refs[len(ks) :]
            place = where_ref[0]
            for k in range(tiles):
                seen[k] = 0

            def enter(q, carry):
                slot = table_ref[place * pen_dev + q]
                k = (slot * magic >> 20 if exact else lax.div(slot, pen_dev)) ^ place
                t = seen[k]
                seen[k] = t + 1
                made[k * share + t] = q
                return carry

            lax.fori_loop(0, pen_dev, enter, 0, unroll=8)
        else:
            made = table_ref
        for o, k in enumerate(ks):
            for t in range(share):
                start = pl.multiple_of(made[k * share + t] * PEN_LEN, PEN_LEN)
                for h in range(halves):
                    outs[o][h * count : (h + 1) * count, t * PEN_LEN : (t + 1) * PEN_LEN] = in_ref[
                        h, first : first + count, pl.ds(start, PEN_LEN)
                    ]

    smem, vmem = pl.BlockSpec(memory_space=pltpu.SMEM), pl.BlockSpec(memory_space=pltpu.VMEM)
    return pl.pallas_call(
        body,
        in_specs=[smem, smem, vmem],
        out_specs=[vmem] * len(ks) + [smem] * build,
        out_shape=[jax.ShapeDtypeStruct((halves * count, share * PEN_LEN), jnp.bfloat16)] * len(ks)
        + [jax.ShapeDtypeStruct((pen_dev,), jnp.int32)] * build,
        scratch_shapes=[pltpu.SMEM((tiles,), jnp.int32)] * build,
        compiler_params=params(),
        cost_estimate=cost(0, 4 * halves * count * points),
    )(table, where, adjoint)


def slots_of(pencil_map, place, tiles):
    pen_dev = pencil_map.shape[0] // tiles
    share = pen_dev // tiles
    local = pencil_map.reshape(tiles, pen_dev) - place * pen_dev
    here = (local >= 0) & (local < pen_dev)
    q = jnp.arange(pen_dev)
    rank = jnp.sum(here[:, None, :] & (q[None, None, :] < q[None, :, None]), axis=2)
    match = here[:, None, :] & (rank[:, None, :] == jnp.arange(share)[None, :, None])
    table = jnp.sum(jnp.where(match, local[:, None, :], 0), axis=2)
    order = jnp.arange(tiles) ^ place
    picked = jnp.sum(jnp.where(order[:, None, None] == jnp.arange(tiles)[None, :, None], table[None], 0), axis=1)
    return picked.reshape(pen_dev).astype(jnp.int32)


def weigh(primal, weights, table, first, count, tiles):
    rows, points = primal.shape
    share = points // PEN_LEN // tiles
    step = 64 if rows % 64 == 0 else rows

    def body(table_ref, in_ref, w_ref, out):
        for k in range(count):
            for t in range(share):
                start = pl.multiple_of(table_ref[(first + k) * share + t] * PEN_LEN, PEN_LEN)
                scale = w_ref[:, pl.ds(start, PEN_LEN)]
                for i in range(0, rows, step):
                    tile = in_ref[i : i + step, pl.ds(start, PEN_LEN)].astype(jnp.float32) * scale
                    out[k, i : i + step, t * PEN_LEN : (t + 1) * PEN_LEN] = tile.astype(jnp.bfloat16)

    vmem = pl.BlockSpec(memory_space=pltpu.VMEM)
    return pl.pallas_call(
        body,
        in_specs=[pl.BlockSpec(memory_space=pltpu.SMEM), vmem, vmem],
        out_specs=vmem,
        out_shape=jax.ShapeDtypeStruct((count, rows, share * PEN_LEN), jnp.bfloat16),
        compiler_params=params(),
        cost_estimate=cost(rows * points // 2, 3 * rows * points),
    )(table, primal, weights.reshape(1, points))


def merge(parts):
    n = len(parts)
    rows, depth = parts[0].shape
    step = rows // 2 if rows % (2 * ROWS) == 0 else rows

    def body(*refs):
        for i in range(n):
            refs[n][i] = refs[i][...]

    return pl.pallas_call(
        body,
        grid=(rows // step,),
        in_specs=[pl.BlockSpec((step, depth), lambda i: (i, 0))] * n,
        out_specs=pl.BlockSpec((n, step, depth), lambda i: (0, i, 0)),
        out_shape=jax.ShapeDtypeStruct((n, rows, depth), parts[0].dtype),
        compiler_params=params(),
        cost_estimate=cost(0, 4 * n * rows * depth),
    )(*parts)


def whole_rows(stride, first, each):
    return lambda i, h: [(i, h * stride + first, each)]


def multiply(groups, own, other, at_k, where, before, each, halves, members, spread=True):
    held = members // 2
    last = before is not None and spread
    depth = groups[0][0][0].shape[-1]
    columns = own.shape[1]
    flat = [a for g in groups for a in g[0]]
    total_count = sum(g[1] for g in groups)
    rows = halves * each

    def body(where_ref, *refs):
        ins, w_refs = refs[: len(flat)], refs[len(flat) : len(flat) + 2]
        rest, (held_w, sems) = refs[len(flat) + 2 : -2], refs[-2:]
        total = rest[-1]
        copies = [
            [
                pltpu.make_async_copy(w_refs[side].at[at_k + k], held_w.at[k, side], sems.at[k, side])
                for side in range(2)
            ]
            for k in range(total_count)
        ]
        for pair in copies:
            for copy in pair:
                copy.start()
        starts = [h * before[0].shape[1] // halves + before[1] for h in range(halves)] if before is not None else []
        if last:
            for n in range(held):
                for h, start in enumerate(starts):
                    at = n * rows + h * each
                    total[at : at + each, :] = rest[0][n, start : start + each, :]
        k = 0
        for g, (_, count, pieces) in enumerate(groups):
            for i in range(count):
                taken = []
                for ref in ins[g * held : (g + 1) * held]:
                    for h in range(halves):
                        for slot, start, length in pieces(i, h):
                            span = slice(start, start + length)
                            taken.append(ref[slot, span, :] if len(ref.shape) == 3 else ref[span, :])
                stacked = jnp.concatenate(taken, axis=0)
                for side in range(2):
                    copies[k][side].wait()
                    product = lax.dot_general(
                        stacked, held_w[k, side], (((1,), (1,)), ((), ())), preferred_element_type=jnp.float32
                    )
                    span = slice(side * columns, (side + 1) * columns)
                    if last:
                        total[:, span] += product
                    else:
                        for n in range(held):
                            value = product[n * rows : (n + 1) * rows]
                            if k:
                                value = value + total[n, :, span]
                            elif before is not None:
                                value = value + jnp.concatenate([rest[0][n, at : at + each, span] for at in starts], axis=0)
                            total[n, :, span] = value
                k += 1
        if last:
            for n in range(held):
                for h in range(halves):
                    e = ((where_ref[1] ^ (2 * n)) * halves + h) ^ where_ref[0]
                    to, low = lax.div(e, 2 * halves), lax.rem(e, halves)
                    at = (n * halves + h) * each
                    for which in range(halves):

                        @pl.when(low == which)
                        def _(to=to, at=at, which=which):
                            for side in range(2):
                                rest[1 + side * halves + which][to] = total[
                                    at : at + each, side * columns : (side + 1) * columns
                                ]

    vmem, anywhere = pl.BlockSpec(memory_space=pltpu.VMEM), pl.BlockSpec(memory_space=pl.ANY)
    full = jax.ShapeDtypeStruct((held, rows, 2 * columns), jnp.float32)
    split = [jax.ShapeDtypeStruct((held, each, columns), jnp.float32)] * (2 * halves)
    return pl.pallas_call(
        body,
        in_specs=[pl.BlockSpec(memory_space=pltpu.SMEM)]
        + [vmem] * len(flat)
        + [anywhere] * 2
        + [vmem] * (before is not None),
        out_specs=[vmem] * (2 * halves) if last else vmem,
        out_shape=split if last else full,
        scratch_shapes=([pltpu.VMEM((held * rows, 2 * columns), jnp.float32)] if last else [])
        + [pltpu.VMEM((total_count, 2, columns, depth), jnp.bfloat16), pltpu.SemaphoreType.DMA((total_count, 2))],
        compiler_params=params(LIMIT),
        cost_estimate=cost(
            4 * held * rows * columns * depth * total_count, 2 * total_count * depth * (held * rows + 2 * columns)
        ),
    )(where, *flat, own, other, *((before[0],) if before is not None else ()))


def after(x, *done):
    return lax.optimization_barrier((x,) + done)[0] if done else x


def on_device(primal, adjoint_pencils, weights, pencil_map):
    rows_here, points = adjoint_pencils.shape
    tiles = lax.axis_size("space")
    members = lax.axis_size("snap")
    place, lane = lax.axis_index("space"), lax.axis_index("snap")
    where = jnp.stack([place, lane]).astype(jnp.int32)
    rows_out = rows_here * members // tiles
    halves = rows_here // rows_out
    adjoint = adjoint_pencils.reshape(halves, rows_out, points)
    half = tiles // 2
    middle = half + half // 2
    units = rows_out // ROWS
    rows_a = units // 2 * ROWS
    rows_b = max(1, 3 * units // 8) * ROWS
    rows_c = rows_out - rows_a - rows_b
    table = slots_of(pencil_map, place, tiles)

    tables = [pencil_map]

    def pack_rows(source, first, count, ks):
        packed = pack(source, tables[-1], where, first, count, ks, tiles)
        tables.extend(packed[len(ks) :])
        return dict(zip(ks, packed))

    def over_space(packed, ks, *done):
        return [xor_send(after(packed[k], *done), "space", k) for k in ks]

    def join(found):
        return found[0] if len(found) == 1 else merge(found)

    def across(block, *done):
        found, bit = [block], members // 2
        order = [0]
        while bit > 1:
            found = found + [xor_send(after(b, *done), "snap", bit) for b in found]
            order = order + [n ^ bit for n in order]
            bit //= 2
        return [found[order.index(n)] for n in sorted(order)]

    def swap_send(x, bit):
        pairs = [(i, i ^ (bit * members + 1)) for i in range(tiles * members)]
        return lax.ppermute(x, ("space", "snap"), pairs)

    same = (((lane * halves) ^ place) & halves) == 0

    class Sum:
        def __init__(self, parts, *done):
            self.mine, self.give = parts[:halves], parts[halves:]
            self.got = [
                (xor_send(after(self.mine[low], *done), "space", low), swap_send(after(self.give[low], *done), low))
                for low in range(1, halves)
            ]

        def swap(self, *done):
            self.swapped = xor_send(after(self.give[0], *done), "snap", 1)
            return self

        def finish(self, *done):
            own = sum([g[0] for g in self.got], self.mine[0])
            rest = sum([g[1] for g in self.got], self.swapped)
            zero, one = jnp.where(same, own, rest), jnp.where(same, rest, own)
            total = zero[0]
            self.last = []
            for hi in range(members // 2):
                for core, part in enumerate((zero, one)):
                    if hi or core:
                        self.last.append(xor_send(after(part[hi], *done), "space", halves * (core + 2 * hi)))
            return sum(self.last, total)

    near_a, near_b = list(range(2, 2 + (half - 2) // 2)), list(range(2 + (half - 2) // 2, half))
    low, high = list(range(half, middle)), list(range(middle, tiles))

    rows_bc = rows_b + rows_c
    start_low, rest_low = low[: len(low) // 2], low[len(low) // 2 :]
    early = 2 + len(near_a)

    packed_a = pack_rows(adjoint, 0, rows_a, start_low)
    packed_n = pack_rows(after(adjoint, packed_a[low[0]]), 0, rows_out, [0, 1])
    packed_na = pack_rows(after(adjoint, packed_n[0]), 0, rows_a, near_a)
    low_a = over_space(packed_a, start_low)
    near_1 = over_space(packed_n, [1])[0]
    got_na = over_space(packed_na, near_a)
    cross_0 = across(packed_n[0])
    own_1 = weigh(after(primal, packed_na[near_a[0]]), weights, table, 0, early, tiles)
    own_2 = weigh(after(primal, own_1), weights, table, early, tiles - early, tiles)
    packed_ar = pack_rows(after(adjoint, own_2), 0, rows_a, rest_low)
    packed_nr = pack_rows(after(adjoint, packed_ar[rest_low[0]]), rows_a, rows_bc, near_a)

    done = (*low_a, near_1, *got_na, cross_0[-1], packed_nr[near_a[0]])
    low_a = low_a + over_space(packed_ar, rest_low, *done)
    got_na = got_na + over_space(packed_nr, near_a, *done)
    cross_1 = across(near_1, *done)
    other_1 = xor_send(after(own_1, *done), "snap", 1)
    other_2 = xor_send(after(own_2, *done), "snap", 1)
    packed_nb = pack_rows(after(adjoint, *done), 0, rows_a, near_b)
    packed_ah = pack_rows(after(adjoint, packed_nb[near_b[0]]), 0, rows_a, high)
    packed_bc = pack_rows(after(adjoint, packed_ah[high[0]]), rows_a, rows_bc, low + near_b)
    packed_b = pack_rows(after(adjoint, packed_bc[low[0]]), rows_a, rows_b, high)
    packed_c = pack_rows(after(adjoint, packed_b[high[0]]), rows_a + rows_b, rows_c, high)

    done = (*low_a, *got_na, cross_1[-1], other_1, other_2, packed_c[high[0]])
    high_a = over_space(packed_ah, high, *done)
    got_nb = over_space(packed_nb, near_b, *done)
    cross_low_a = across(join(low_a), *done)
    cross_na = across(join(got_na), *done)

    done = (*high_a, *got_nb, cross_low_a[-1], cross_na[-1])
    low_bc = over_space(packed_bc, low, *done)
    got_nb_bc = over_space(packed_bc, near_b, *done)
    cross_nb = across(join(got_nb), *done)
    cross_high_a = across(join(high_a), *done)

    def two_runs(i, h):
        return [(i, h * rows_a, rows_a), (len(near_a) + i, h * rows_bc, rows_bc)]

    plain = whole_rows(rows_out, 0, rows_out)
    groups = [(cross_0, 1, plain), (cross_1, 1, plain), (cross_na, len(near_a), two_runs)]
    product = multiply(groups, own_1, after(other_1, *done), 0, where, None, rows_out, halves, members)

    done = (*low_bc, *got_nb_bc, cross_nb[-1], cross_high_a[-1], product)
    high_b = over_space(packed_b, high, *done)
    cross_low_bc = across(join(low_bc), *done)
    cross_nb_bc = across(join(got_nb_bc), *done)
    rows = whole_rows(rows_a, 0, rows_a)
    groups = [(cross_nb, len(near_b), rows), (cross_low_a, len(low), rows), (cross_high_a, len(high), rows)]
    pair_a = multiply(groups, own_2, other_2, 0, where, (product, 0), rows_a, halves, members)

    done = (*high_b, cross_low_bc[-1], cross_nb_bc[-1], pair_a[0])
    high_c = over_space(packed_c, high, *done)
    cross_high_b = across(join(high_b), *done)
    sum_a = Sum(pair_a, *done)
    rows = whole_rows(rows_bc, 0, rows_bc)
    groups = [(cross_nb_bc, len(near_b), rows), (cross_low_bc, len(low), rows)]
    first_high = len(near_b) + len(low)
    product_bc = multiply(
        groups, own_2, after(other_2, *done), 0, where, (product, rows_a), rows_bc, halves, members, False
    )

    done = (*high_c, cross_high_b[-1], *[g for pair in sum_a.got for g in pair], product_bc)
    cross_high_c = across(join(high_c), *done)
    total_a = sum_a.swap(*done).finish()
    groups = [(cross_high_b, len(high), whole_rows(rows_b, 0, rows_b))]
    pair_b = multiply(groups, own_2, after(other_2, *done), first_high, where, (product_bc, 0), rows_b, halves, members)
    sum_b = Sum(pair_b, sum_a.swapped).swap()
    groups = [(cross_high_c, len(high), whole_rows(rows_c, 0, rows_c))]
    pair_c = multiply(
        groups, own_2, after(other_2, *sum_a.last), first_high, where, (product_bc, rows_b), rows_c, halves, members
    )
    sum_c = Sum(pair_c).swap()
    return jnp.concatenate([total_a, sum_b.finish(), sum_c.finish()], axis=0)


def solution(mesh):
    placed = (P("snap", "space"), P("snap", "space"), P("space"), P())
    return jax.shard_map(
        on_device, mesh=mesh, in_specs=placed, out_specs=P("space", "snap"), check_vma=False
    )
```

time: 244 us -> 219 us (0.90)
  waiting for transfers between devices: 128 us -> 92.8 us
  starting transfers between devices: 51 us -> 61.5 us
  Pallas kernels: 45.8 us -> 50.3 us
  local copies, waits for them, and re-layouts: 15.2 us -> 10.8 us
    ppermute x36 -> x42, waiting for transfers between devices: 128 us -> 91.5 us  [xor_send(): return lax.ppermute(x, axis, [(i, i ^ k) for i in range(n)])]
    pallas_call x4 -> x5, Pallas kernels: 22.3 us -> 34.6 us  [multiply(): pl.pallas_call(body, in_specs=[pl.BlockSpec(memory_space=pltpu.SMEM)] + [...]
    ppermute x36 -> x42, starting transfers between devices: 51 us -> 59.4 us  [xor_send(): return lax.ppermute(x, axis, [(i, i ^ k) for i in range(n)])]
    pallas_call x6 -> x10, Pallas kernels: 18 us -> 10.4 us  [pack(): pl.pallas_call(body, in_specs=[smem, smem, vmem], out_specs=[vmem] * len(...]
    unnamed x54 -> x50, local copies, waits for them, and re-layouts: 14.7 us -> 10.5 us
  transfers between devices with their start and end apart: 36 -> 45, of which waited for: 21 -> 21; matrix products, arithmetic and copies ran while one was open for 1% -> 1% of each run, Pallas kernels for 17% -> 22%
where the time goes in v2:
time: 219 us
  waiting for transfers between devices  92.8 us (42%)
  starting transfers between devices  61.5 us (28%)
  Pallas kernels  50.3 us (23%)
  local copies, waits for them, and re-layouts  10.8 us (5%)
  other arithmetic  2.69 us (1%)
    ppermute x42, waiting for transfers between devices, xor_send(): return lax.ppermute(x, axis, [(i, i ^ k) for i in range(n)])  91.5 us
    ppermute x42, starting transfers between devices, xor_send(): return lax.ppermute(x, axis, [(i, i ^ k) for i in range(n)])  59.4 us
    pallas_call x5, Pallas kernels, multiply(): pl.pallas_call(body, in_specs=[pl.BlockSpec(memory_space=pltpu.SMEM)] + [...  34.6 us
    unnamed x50, local copies, waits for them, and re-layouts  10.5 us
    pallas_call x10, Pallas kernels, pack(): pl.pallas_call(body, in_specs=[smem, smem, vmem], out_specs=[vmem] * len(...  10.4 us
    pallas_call x2, Pallas kernels, weigh(): pl.pallas_call(body, in_specs=[pl.BlockSpec(memory_space=pltpu.SMEM), vme...  4.5 us
  transfers between devices with their start and end apart: 45, of which 21 were waited for; matrix products, arithmetic and copies ran while one was open for 1% of the time, Pallas kernels for 22%

profile of v2, /device:TPU:0, one launch (start us, length us, event | category | flops | bytes accessed | tf_op | source)
XLA Modules:
  0.0 218.7 jit_solution(2501069630409765672)
XLA Ops:
  0.1 2.8 %copy-done = bf16[256,12288]{1,0:T(8,128)(2,1)S(1)} copy-done((bf16[256,12288]{1,0:T(8,128)(2,1)S(1)}, bf16[256,12288]{1,0:T(8,128)(2,1)}, u32[]{:S(2)}) %copy-start) | copy-done | bytes 6291480
  5.3 4.1 %collective-permute-start = (bf16[128,1536]{1,0:T(8,128)(2,1)S(1)}, bf16[128,1536]{1,0:T(8,128)(2,1)S(1)}, u32[]{:S(2)}, u32[]{:S(2)}) collective-permute-start(bf16[128,1536]{1,0:T(8,128)(2,1)S(1)} %get-tuple-element.74), channel_id=1, source_target_pairs={{0,16},{4,20},{8,24},{12,28},{16,0},{20,4},{24,8},{28,12},{1,17},{... | collective-permute-start | bytes 1179656 | tf_op jit(solution)/shard_map/ppermute | solution.py:16
  9.4 2.2 %shard_map.47 = (bf16[256,1536]{1,0:T(8,128)(2,1)}, bf16[256,1536]{1,0:T(8,128)(2,1)}) custom-call(s32[96]{0:T(128)S(1)} %get-tuple-element.73.table_ref, s32[2]{0:T(128)S(1)} %pad_add_fusion.where_ref, bf16[2,128,12288]{2,1,0:T(8,128)(2,1)S(1)} %bitcast.47), custom_call_target="tpu_custom_call" | custom-call | bytes 12582912 | tf_op jit(solution)/shard_map/pallas_call | solution.py:63
  17.9 4.6 %copy-done.3 = bf16[512,12288]{1,0:T(8,128)(2,1)S(1)} copy-done((bf16[512,12288]{1,0:T(8,128)(2,1)S(1)}, bf16[512,12288]{1,0:T(8,128)(2,1)}, u32[]{:S(2)}) %copy-start.3) | copy-done | bytes 12582936
  24.3 2.7 %shard_map.50.refs_6_.refs_4_.refs_2_ = bf16[5,512,1536]{2,1,0:T(8,128)(2,1)S(1)} custom-call(s32[96]{0:T(128)S(1)} %reshape.70.table_ref, bf16[512,12288]{1,0:T(8,128)(2,1)S(1)} %copy-done.3, f32[1,12288]{1,0:T(1,128)S(1)} %bitcast.59), custom_call_target="tpu_custom_call" | custom-call | flops 3145728 | bytes 18874368 | tf_op jit(solution)/shard_map/pallas_call | solution.py:104
  28.8 2.6 %collective-permute-done.2.refs_0_ = bf16[128,1536]{1,0:T(8,128)(2,1)S(1)} collective-permute-done((bf16[128,1536]{1,0:T(8,128)(2,1)S(1)}, bf16[128,1536]{1,0:T(8,128)(2,1)S(1)}, u32[]{:S(2)}, u32[]{:S(2)}) %collective-permute-start.2) | collective-permute-done | bytes 393248 | tf_op jit(solution)/shard_map/ppermute | solution.py:16
  31.4 2.8 %collective-permute-done.1.refs_2_ = bf16[256,1536]{1,0:T(8,128)(2,1)} collective-permute-done((bf16[256,1536]{1,0:T(8,128)(2,1)}, bf16[256,1536]{1,0:T(8,128)(2,1)}, u32[]{:S(2)}, u32[]{:S(2)}) %collective-permute-start.1) | collective-permute-done | bytes 786464 | tf_op jit(solution)/shard_map/ppermute | solution.py:16
  35.7 2.2 collective-permute-start.4
  43.1 10.0 %collective-permute-done.5.refs_1_ = bf16[128,1536]{1,0:T(8,128)(2,1)S(1)} collective-permute-done((bf16[128,1536]{1,0:T(8,128)(2,1)S(1)}, bf16[128,1536]{1,0:T(8,128)(2,1)S(1)}, u32[]{:S(2)}, u32[]{:S(2)}) %collective-permute-start.5) | collective-permute-done | bytes 393248 | tf_op jit(solution)/shard_map/ppermute | solution.py:16
  53.3 3.2 %collective-permute-done.4.refs_1_ = bf16[128,1536]{1,0:T(8,128)(2,1)S(1)} collective-permute-done((bf16[128,1536]{1,0:T(8,128)(2,1)S(1)}, bf16[128,1536]{1,0:T(8,128)(2,1)S(1)}, u32[]{:S(2)}, u32[]{:S(2)}) %collective-permute-start.4) | collective-permute-done | bytes 393248 | tf_op jit(solution)/shard_map/ppermute | solution.py:16
  58.8 3.2 %collective-permute-start.11 = (bf16[128,1536]{1,0:T(8,128)(2,1)S(1)}, bf16[128,1536]{1,0:T(8,128)(2,1)S(1)}, u32[]{:S(2)}, u32[]{:S(2)}) collective-permute-start(bf16[128,1536]{1,0:T(8,128)(2,1)S(1)} %get-tuple-element.100), channel_id=1, source_target_pairs={{0,28},{4,24},{8,20},{12,16},{16,12},{20,8},{24,4},{28,0},{1,29},{... | collective-permute-start | bytes 1179656 | tf_op jit(solution)/shard_map/ppermute | solution.py:16
  63.5 10.1 %collective-permute-done.11.refs_1_ = bf16[128,1536]{1,0:T(8,128)(2,1)S(1)} collective-permute-done((bf16[128,1536]{1,0:T(8,128)(2,1)S(1)}, bf16[128,1536]{1,0:T(8,128)(2,1)S(1)}, u32[]{:S(2)}, u32[]{:S(2)}) %collective-permute-start.11) | collective-permute-done | bytes 393248 | tf_op jit(solution)/shard_map/ppermute | solution.py:16
  73.7 8.0 %collective-permute-done.10.refs_0_ = bf16[128,1536]{1,0:T(8,128)(2,1)S(1)} collective-permute-done((bf16[128,1536]{1,0:T(8,128)(2,1)S(1)}, bf16[128,1536]{1,0:T(8,128)(2,1)S(1)}, u32[]{:S(2)}, u32[]{:S(2)}) %collective-permute-start.10) | collective-permute-done | bytes 393248 | tf_op jit(solution)/shard_map/ppermute | solution.py:16
  81.8 6.4 %collective-permute-done.9.refs_0_ = bf16[128,1536]{1,0:T(8,128)(2,1)S(1)} collective-permute-done((bf16[128,1536]{1,0:T(8,128)(2,1)S(1)}, bf16[128,1536]{1,0:T(8,128)(2,1)S(1)}, u32[]{:S(2)}, u32[]{:S(2)}) %collective-permute-start.9) | collective-permute-done | bytes 393248 | tf_op jit(solution)/shard_map/ppermute | solution.py:16
  88.2 2.8 %collective-permute-done.12.refs_3_ = bf16[2,128,1536]{2,1,0:T(8,128)(2,1)S(1)} collective-permute-done((bf16[2,128,1536]{2,1,0:T(8,128)(2,1)S(1)}, bf16[2,128,1536]{2,1,0:T(8,128)(2,1)S(1)}, u32[]{:S(2)}, u32[]{:S(2)}) %collective-permute-start.12) | collective-permute-done | bytes 786464 | tf_op jit(solution)/shard_map/ppermute | solution.py:16
  93.0 6.1 %collective-permute-start.18 = (bf16[128,1536]{1,0:T(8,128)(2,1)S(1)}, bf16[128,1536]{1,0:T(8,128)(2,1)S(1)}, u32[]{:S(2)}, u32[]{:S(2)}) collective-permute-start(bf16[128,1536]{1,0:T(8,128)(2,1)S(1)} %get-tuple-element.112), channel_id=1, source_target_pairs={{0,12},{4,8},{8,4},{12,0},{16,28},{20,24},{24,20},{28,16},{1,13},{... | collective-permute-start | bytes 1179656 | tf_op jit(solution)/shard_map/ppermute | solution.py:16
  101.3 10.5 %shard_map.61.refs_8_.refs_6_ = f32[2,256,1024]{2,1,0:T(8,128)} custom-call(s32[2]{0:T(128)S(1)} %pad_add_fusion.where_ref, bf16[256,1536]{1,0:T(8,128)(2,1)} %get-tuple-element.77.refs_0_, bf16[256,1536]{1,0:T(8,128)(2,1)} %collective-permute-done.3.refs_1_, bf16[256,1536]{1,0:T(8,128)(2,1)} %collective-permute-done.1.refs_2_, ...), custom_call_target="tpu_custom_call" | custom-call | flops 4831838208 | bytes 14155776 | tf_op jit(solution)/shard_map/pallas_call | solution.py:212
  111.8 16.7 %collective-permute-done.17.refs_1_ = bf16[128,1536]{1,0:T(8,128)(2,1)S(1)} collective-permute-done((bf16[128,1536]{1,0:T(8,128)(2,1)}, bf16[128,1536]{1,0:T(8,128)(2,1)S(1)}, u32[]{:S(2)}, u32[]{:S(2)}) %collective-permute-start.17) | collective-permute-done | bytes 393248 | tf_op jit(solution)/shard_map/ppermute | solution.py:16
  128.5 4.2 %collective-permute-done.16.refs_0_ = bf16[128,1536]{1,0:T(8,128)(2,1)S(1)} collective-permute-done((bf16[128,1536]{1,0:T(8,128)(2,1)}, bf16[128,1536]{1,0:T(8,128)(2,1)S(1)}, u32[]{:S(2)}, u32[]{:S(2)}) %collective-permute-start.16) | collective-permute-done | bytes 393248 | tf_op jit(solution)/shard_map/ppermute | solution.py:16
  135.1 5.8 %collective-permute-start.20 = (bf16[96,1536]{1,0:T(8,128)(2,1)S(1)}, bf16[96,1536]{1,0:T(8,128)(2,1)S(1)}, u32[]{:S(2)}, u32[]{:S(2)}) collective-permute-start(bf16[96,1536]{1,0:T(8,128)(2,1)S(1)} %copy-done.14), channel_id=1, source_target_pairs={{0,28},{4,24},{8,20},{12,16},{16,12},{20,8},{24,4},{28,0},{1,29},{... | collective-permute-start | bytes 884744 | tf_op jit(solution)/shard_map/ppermute | solution.py:16
  141.9 9.0 %shard_map.62 = (f32[2,64,512]{2,1,0:T(8,128)S(1)}, f32[2,64,512]{2,1,0:T(8,128)S(1)}, f32[2,64,512]{2,1,0:T(8,128)S(1)}, f32[2,64,512]{2,1,0:T(8,128)S(1)}) custom-call(s32[2]{0:T(128)S(1)} %pad_add_fusion.where_ref, bf16[128,1536]{1,0:T(8,128)(2,1)S(1)} %collective-permute-done.9.refs_0_, bf16[128,1536]{1,0:T(8,128)(2,1)S(1)} %collective-permute-done.14.refs_1_, ...), custom_call_target="tpu_custom_call" | custom-call | flops 4026531840 | bytes 19660800 | tf_op jit(solution)/shard_map/pallas_call | solution.py:212
  150.9 2.6 %collective-permute-done.19.refs_0_ = bf16[96,1536]{1,0:T(8,128)(2,1)S(1)} collective-permute-done((bf16[96,1536]{1,0:T(8,128)(2,1)S(1)}, bf16[96,1536]{1,0:T(8,128)(2,1)S(1)}, u32[]{:S(2)}, u32[]{:S(2)}) %collective-permute-start.19) | collective-permute-done | bytes 294944 | tf_op jit(solution)/shard_map/ppermute | solution.py:16
  153.6 5.6 %collective-permute-done.22.refs_1_ = bf16[128,1536]{1,0:T(8,128)(2,1)S(1)} collective-permute-done((bf16[128,1536]{1,0:T(8,128)(2,1)S(1)}, bf16[128,1536]{1,0:T(8,128)(2,1)S(1)}, u32[]{:S(2)}, u32[]{:S(2)}) %collective-permute-start.22) | collective-permute-done | bytes 393248 | tf_op jit(solution)/shard_map/ppermute | solution.py:16
  162.2 2.8 %collective-permute-start.23 = (f32[2,64,512]{2,1,0:T(8,128)S(1)}, f32[2,64,512]{2,1,0:T(8,128)S(1)}, u32[]{:S(2)}, u32[]{:S(2)}) collective-permute-start(f32[2,64,512]{2,1,0:T(8,128)S(1)} %get-tuple-element.118), channel_id=1, source_target_pairs={{0,4},{4,0},{8,12},{12,8},{16,20},{20,16},{24,28},{28,24},{1,5},{5... | collective-permute-start | bytes 786440 | tf_op jit(solution)/shard_map/ppermute | solution.py:16
  165.7 2.7 %collective-permute-start.24 = (bf16[32,1536]{1,0:T(8,128)(2,1)S(1)}, bf16[32,1536]{1,0:T(8,128)(2,1)S(1)}, u32[]{:S(2)}, u32[]{:S(2)}) collective-permute-start(bf16[32,1536]{1,0:T(8,128)(2,1)S(1)} %copy-done.16), channel_id=1, source_target_pairs={{0,24},{4,28},{8,16},{12,20},{16,8},{20,12},{24,0},{28,4},{1,25},{... | collective-permute-start | bytes 294920 | tf_op jit(solution)/shard_map/ppermute | solution.py:16
  168.3 6.4 %shard_map.65.refs_4_ = f32[2,128,1024]{2,1,0:T(8,128)S(1)} custom-call(s32[2]{0:T(128)S(1)} %pad_add_fusion.where_ref, bf16[128,1536]{1,0:T(8,128)(2,1)S(1)} %collective-permute-done.18.refs_0_, bf16[128,1536]{1,0:T(8,128)(2,1)S(1)} %collective-permute-done.22.refs_1_, bf16[2,128,1536]{2,1,0:T(8,128)(2,1)S(1)} %shard_map.63.refs_2_, ...), custom_call_target="tpu_custom_call" | custom-call | flops 2415919104 | bytes 11796480 | tf_op jit(solution)/shard_map/pallas_call | solution.py:212
  174.8 2.5 %collective-permute-done.23 = f32[2,64,512]{2,1,0:T(8,128)S(1)} collective-permute-done((f32[2,64,512]{2,1,0:T(8,128)S(1)}, f32[2,64,512]{2,1,0:T(8,128)S(1)}, u32[]{:S(2)}, u32[]{:S(2)}) %collective-permute-start.23) | collective-permute-done | bytes 262176 | tf_op jit(solution)/shard_map/ppermute | solution.py:16
  180.0 2.3 %collective-permute-start.29 = (f32[64,512]{1,0:T(8,128)S(1)}, f32[64,512]{1,0:T(8,128)S(1)}, u32[]{:S(2)}, u32[]{:S(2)}) collective-permute-start(f32[64,512]{1,0:T(8,128)S(1)} %get-tuple-element.148), channel_id=1, source_target_pairs={{0,8},{4,12},{8,0},{12,4},{16,24},{20,28},{24,16},{28,20},{1,9},{5... | collective-permute-start | bytes 393224 | tf_op jit(solution)/shard_map/ppermute | solution.py:16
  184.1 4.5 %shard_map.66 = (f32[2,48,512]{2,1,0:T(8,128)S(1)}, f32[2,48,512]{2,1,0:T(8,128)S(1)}, f32[2,48,512]{2,1,0:T(8,128)S(1)}, f32[2,48,512]{2,1,0:T(8,128)S(1)}) custom-call(s32[2]{0:T(128)S(1)} %pad_add_fusion.where_ref, bf16[2,96,1536]{2,1,0:T(8,128)(2,1)S(1)} %shard_map.64.refs_0_, bf16[2,96,1536]{2,1,0:T(8,128)(2,1)S(1)} %collective-permute-done.26.refs_1_, ...), custom_call_target="tpu_custom_call" | custom-call | flops 1207959552 | bytes 7471104 | tf_op jit(solution)/shard_map/pallas_call | solution.py:212
  191.1 4.9 %collective-permute-done.30 = f32[64,512]{1,0:T(8,128)S(1)} collective-permute-done((f32[64,512]{1,0:T(8,128)S(1)}, f32[64,512]{1,0:T(8,128)S(1)}, u32[]{:S(2)}, u32[]{:S(2)}) %collective-permute-start.30) | collective-permute-done | bytes 131104 | tf_op jit(solution)/shard_map/ppermute | solution.py:16
  196.0 4.2 %shard_map.68 = (f32[2,16,512]{2,1,0:T(8,128)S(1)}, f32[2,16,512]{2,1,0:T(8,128)S(1)}, f32[2,16,512]{2,1,0:T(8,128)S(1)}, f32[2,16,512]{2,1,0:T(8,128)S(1)}) custom-call(s32[2]{0:T(128)S(1)} %pad_add_fusion.where_ref, bf16[2,32,1536]{2,1,0:T(8,128)(2,1)S(1)} %shard_map.67.refs_0_, bf16[2,32,1536]{2,1,0:T(8,128)(2,1)S(1)} %collective-permute-done.38.refs_1_, ...), custom_call_target="tpu_custom_call" | custom-call | flops 402653184 | bytes 6684672 | tf_op jit(solution)/shard_map/pallas_call | solution.py:212
  213.7 4.2 %collective-permute-done.36 = f32[48,512]{1,0:T(8,128)S(1)} collective-permute-done((f32[48,512]{1,0:T(8,128)S(1)}, f32[48,512]{1,0:T(8,128)S(1)}, u32[]{:S(2)}, u32[]{:S(2)}) %collective-permute-start.36) | collective-permute-done | bytes 98336 | tf_op jit(solution)/shard_map/ppermute | solution.py:16
  (157 shorter events, 55.6 us)
Async XLA Ops:
  5.3 26.1 %collective-permute-start = (bf16[128,1536]{1,0:T(8,128)(2,1)S(1)}, bf16[128,1536]{1,0:T(8,128)(2,1)S(1)}, u32[]{:S(2)}, u32[]{:S(2)}) collective-permute-start(bf16[128,1536]{1,0:T(8,128)(2,1)S(1)} %get-tuple-element.74), channel_id=1, source_target_pairs={{0,16},{4,20},{8,24},{12,28},{16,0},{20,4},{24,8},{28,12},{1,17},{... | collective-permute-start | bytes 1179656 | tf_op jit(solution)/shard_map/ppermute | solution.py:16
  11.6 19.8 %collective-permute-start.3 = (bf16[256,1536]{1,0:T(8,128)(2,1)}, bf16[256,1536]{1,0:T(8,128)(2,1)}, u32[]{:S(2)}, u32[]{:S(2)}) collective-permute-start(bf16[256,1536]{1,0:T(8,128)(2,1)} %get-tuple-element.77.refs_0_), channel_id=1, source_target_pairs={{0,2},{1,3},{2,0},{3,1},{4,6},{5,7},{6,4},{7,5},{8,10},{9,11},{10,... | collective-permute-start | bytes 2359304 | tf_op jit(solution)/shard_map/ppermute | solution.py:16
  13.8 17.6 %collective-permute-start.2 = (bf16[128,1536]{1,0:T(8,128)(2,1)S(1)}, bf16[128,1536]{1,0:T(8,128)(2,1)S(1)}, u32[]{:S(2)}, u32[]{:S(2)}) collective-permute-start(bf16[128,1536]{1,0:T(8,128)(2,1)S(1)} %shard_map.48), channel_id=1, source_target_pairs={{0,8},{4,12},{8,0},{12,4},{16,24},{20,28},{24,16},{28,20},{1,9},{5... | collective-permute-start | bytes 1179656 | tf_op jit(solution)/shard_map/ppermute | solution.py:16
  15.4 18.8 %collective-permute-start.1 = (bf16[256,1536]{1,0:T(8,128)(2,1)}, bf16[256,1536]{1,0:T(8,128)(2,1)}, u32[]{:S(2)}, u32[]{:S(2)}) collective-permute-start(bf16[256,1536]{1,0:T(8,128)(2,1)} %get-tuple-element.76), channel_id=1, source_target_pairs={{0,4},{4,0},{8,12},{12,8},{16,20},{20,16},{24,28},{28,24},{1,5},{5... | collective-permute-start | bytes 2359304 | tf_op jit(solution)/shard_map/ppermute | solution.py:16
  34.2 22.5 %collective-permute-start.8 = (bf16[5,512,1536]{2,1,0:T(8,128)(2,1)S(1)}, bf16[5,512,1536]{2,1,0:T(8,128)(2,1)S(1)}, u32[]{:S(2)}, u32[]{:S(2)}) collective-permute-start(bf16[5,512,1536]{2,1,0:T(8,128)(2,1)S(1)} %shard_map.50.refs_6_.refs_4_.refs_2_), channel_id=1, source_target_pairs={{0,1},{1,0},{2,3},{3,2},{4,5},{5,4},{6,7},{7,6},{8,9},{9,8},{10,11... | collective-permute-start | bytes 23592968 | tf_op jit(solution)/shard_map/ppermute | solution.py:16
  34.2 22.5 %collective-permute-start.7 = (bf16[3,512,1536]{2,1,0:T(8,128)(2,1)S(1)}, bf16[3,512,1536]{2,1,0:T(8,128)(2,1)S(1)}, u32[]{:S(2)}, u32[]{:S(2)}) collective-permute-start(bf16[3,512,1536]{2,1,0:T(8,128)(2,1)S(1)} %shard_map.49.refs_6_), channel_id=1, source_target_pairs={{0,1},{1,0},{2,3},{3,2},{4,5},{5,4},{6,7},{7,6},{8,9},{9,8},{10,11... | collective-permute-start | bytes 14155784 | tf_op jit(solution)/shard_map/ppermute | solution.py:16
  34.7 21.9 %collective-permute-start.6 = (bf16[256,1536]{1,0:T(8,128)(2,1)}, bf16[256,1536]{1,0:T(8,128)(2,1)S(1)}, u32[]{:S(2)}, u32[]{:S(2)}) collective-permute-start(bf16[256,1536]{1,0:T(8,128)(2,1)} %collective-permute-done.1.refs_2_), channel_id=1, source_target_pairs={{0,2},{1,3},{2,0},{3,1},{4,6},{5,7},{6,4},{7,5},{8,10},{9,11},{10,... | collective-permute-start | bytes 2359304 | tf_op jit(solution)/shard_map/ppermute | solution.py:16
  35.2 17.9 %collective-permute-start.5 = (bf16[128,1536]{1,0:T(8,128)(2,1)S(1)}, bf16[128,1536]{1,0:T(8,128)(2,1)S(1)}, u32[]{:S(2)}, u32[]{:S(2)}) collective-permute-start(bf16[128,1536]{1,0:T(8,128)(2,1)S(1)} %shard_map.52), channel_id=1, source_target_pairs={{0,8},{4,12},{8,0},{12,4},{16,24},{20,28},{24,16},{28,20},{1,9},{5... | collective-permute-start | bytes 1179656 | tf_op jit(solution)/shard_map/ppermute | solution.py:16
  35.7 20.8 %collective-permute-start.4 = (bf16[128,1536]{1,0:T(8,128)(2,1)S(1)}, bf16[128,1536]{1,0:T(8,128)(2,1)S(1)}, u32[]{:S(2)}, u32[]{:S(2)}) collective-permute-start(bf16[128,1536]{1,0:T(8,128)(2,1)S(1)} %shard_map.51), channel_id=1, source_target_pairs={{0,20},{4,16},{8,28},{12,24},{16,4},{20,0},{24,12},{28,8},{1,21},{... | collective-permute-start | bytes 1179656 | tf_op jit(solution)/shard_map/ppermute | solution.py:16
  56.7 31.5 %collective-permute-start.13 = (bf16[2,128,1536]{2,1,0:T(8,128)(2,1)S(1)}, bf16[2,128,1536]{2,1,0:T(8,128)(2,1)S(1)}, u32[]{:S(2)}, u32[]{:S(2)}) collective-permute-start(bf16[2,128,1536]{2,1,0:T(8,128)(2,1)S(1)} %shard_map.59.refs_4_), channel_id=1, source_target_pairs={{0,2},{1,3},{2,0},{3,1},{4,6},{5,7},{6,4},{7,5},{8,10},{9,11},{10,... | collective-permute-start | bytes 2359304 | tf_op jit(solution)/shard_map/ppermute | solution.py:16
  58.2 32.8 %collective-permute-start.12 = (bf16[2,128,1536]{2,1,0:T(8,128)(2,1)S(1)}, bf16[2,128,1536]{2,1,0:T(8,128)(2,1)S(1)}, u32[]{:S(2)}, u32[]{:S(2)}) collective-permute-start(bf16[2,128,1536]{2,1,0:T(8,128)(2,1)S(1)} %shard_map.58.refs_2_), channel_id=1, source_target_pairs={{0,2},{1,3},{2,0},{3,1},{4,6},{5,7},{6,4},{7,5},{8,10},{9,11},{10,... | collective-permute-start | bytes 2359304 | tf_op jit(solution)/shard_map/ppermute | solution.py:16
  58.8 14.9 %collective-permute-start.11 = (bf16[128,1536]{1,0:T(8,128)(2,1)S(1)}, bf16[128,1536]{1,0:T(8,128)(2,1)S(1)}, u32[]{:S(2)}, u32[]{:S(2)}) collective-permute-start(bf16[128,1536]{1,0:T(8,128)(2,1)S(1)} %get-tuple-element.100), channel_id=1, source_target_pairs={{0,28},{4,24},{8,20},{12,16},{16,12},{20,8},{24,4},{28,0},{1,29},{... | collective-permute-start | bytes 1179656 | tf_op jit(solution)/shard_map/ppermute | solution.py:16
  62.0 19.7 %collective-permute-start.10 = (bf16[128,1536]{1,0:T(8,128)(2,1)S(1)}, bf16[128,1536]{1,0:T(8,128)(2,1)S(1)}, u32[]{:S(2)}, u32[]{:S(2)}) collective-permute-start(bf16[128,1536]{1,0:T(8,128)(2,1)S(1)} %get-tuple-element.98), channel_id=1, source_target_pairs={{0,24},{4,28},{8,16},{12,20},{16,8},{20,12},{24,0},{28,4},{1,25},{... | collective-permute-start | bytes 1179656 | tf_op jit(solution)/shard_map/ppermute | solution.py:16
  63.5 24.7 %collective-permute-start.9 = (bf16[128,1536]{1,0:T(8,128)(2,1)S(1)}, bf16[128,1536]{1,0:T(8,128)(2,1)S(1)}, u32[]{:S(2)}, u32[]{:S(2)}) collective-permute-start(bf16[128,1536]{1,0:T(8,128)(2,1)S(1)} %shard_map.53), channel_id=1, source_target_pairs={{0,12},{4,8},{8,4},{12,0},{16,28},{20,24},{24,20},{28,16},{1,13},{... | collective-permute-start | bytes 1179656 | tf_op jit(solution)/shard_map/ppermute | solution.py:16
  91.0 42.0 %collective-permute-start.15 = (bf16[2,128,1536]{2,1,0:T(8,128)(2,1)S(1)}, bf16[2,128,1536]{2,1,0:T(8,128)(2,1)S(1)}, u32[]{:S(2)}, u32[]{:S(2)}) collective-permute-start(bf16[2,128,1536]{2,1,0:T(8,128)(2,1)S(1)} %shard_map.60.refs_4_), channel_id=1, source_target_pairs={{0,2},{1,3},{2,0},{3,1},{4,6},{5,7},{6,4},{7,5},{8,10},{9,11},{10,... | collective-permute-start | bytes 2359304 | tf_op jit(solution)/shard_map/ppermute | solution.py:16
  91.0 42.0 %collective-permute-start.14 = (bf16[128,1536]{1,0:T(8,128)(2,1)S(1)}, bf16[128,1536]{1,0:T(8,128)(2,1)S(1)}, u32[]{:S(2)}, u32[]{:S(2)}) collective-permute-start(bf16[128,1536]{1,0:T(8,128)(2,1)S(1)} %collective-permute-done.9.refs_0_), channel_id=1, source_target_pairs={{0,2},{1,3},{2,0},{3,1},{4,6},{5,7},{6,4},{7,5},{8,10},{9,11},{10,... | collective-permute-start | bytes 1179656 | tf_op jit(solution)/shard_map/ppermute | solution.py:16
  93.0 40.0 %collective-permute-start.18 = (bf16[128,1536]{1,0:T(8,128)(2,1)S(1)}, bf16[128,1536]{1,0:T(8,128)(2,1)S(1)}, u32[]{:S(2)}, u32[]{:S(2)}) collective-permute-start(bf16[128,1536]{1,0:T(8,128)(2,1)S(1)} %get-tuple-element.112), channel_id=1, source_target_pairs={{0,12},{4,8},{8,4},{12,0},{16,28},{20,24},{24,20},{28,16},{1,13},{... | collective-permute-start | bytes 1179656 | tf_op jit(solution)/shard_map/ppermute | solution.py:16
  99.2 29.3 %collective-permute-start.17 = (bf16[128,1536]{1,0:T(8,128)(2,1)}, bf16[128,1536]{1,0:T(8,128)(2,1)S(1)}, u32[]{:S(2)}, u32[]{:S(2)}) collective-permute-start(bf16[128,1536]{1,0:T(8,128)(2,1)} %get-tuple-element.110), channel_id=1, source_target_pairs={{0,20},{4,16},{8,28},{12,24},{16,4},{20,0},{24,12},{28,8},{1,21},{... | collective-permute-start | bytes 1179656 | tf_op jit(solution)/shard_map/ppermute | solution.py:16
  99.5 33.2 %collective-permute-start.16 = (bf16[128,1536]{1,0:T(8,128)(2,1)}, bf16[128,1536]{1,0:T(8,128)(2,1)S(1)}, u32[]{:S(2)}, u32[]{:S(2)}) collective-permute-start(bf16[128,1536]{1,0:T(8,128)(2,1)} %get-tuple-element.108), channel_id=1, source_target_pairs={{0,16},{4,20},{8,24},{12,28},{16,0},{20,4},{24,8},{28,12},{1,17},{... | collective-permute-start | bytes 1179656 | tf_op jit(solution)/shard_map/ppermute | solution.py:16
  133.0 26.2 %collective-permute-start.21 = (bf16[2,128,1536]{2,1,0:T(8,128)(2,1)S(1)}, bf16[2,128,1536]{2,1,0:T(8,128)(2,1)S(1)}, u32[]{:S(2)}, u32[]{:S(2)}) collective-permute-start(bf16[2,128,1536]{2,1,0:T(8,128)(2,1)S(1)} %shard_map.63.refs_2_), channel_id=1, source_target_pairs={{0,2},{1,3},{2,0},{3,1},{4,6},{5,7},{6,4},{7,5},{8,10},{9,11},{10,... | collective-permute-start | bytes 2359304 | tf_op jit(solution)/shard_map/ppermute | solution.py:16
  134.8 24.5 %collective-permute-start.22 = (bf16[128,1536]{1,0:T(8,128)(2,1)S(1)}, bf16[128,1536]{1,0:T(8,128)(2,1)S(1)}, u32[]{:S(2)}, u32[]{:S(2)}) collective-permute-start(bf16[128,1536]{1,0:T(8,128)(2,1)S(1)} %collective-permute-done.18.refs_0_), channel_id=1, source_target_pairs={{0,2},{1,3},{2,0},{3,1},{4,6},{5,7},{6,4},{7,5},{8,10},{9,11},{10,... | collective-permute-start | bytes 1179656 | tf_op jit(solution)/shard_map/ppermute | solution.py:16
  135.1 15.8 %collective-permute-start.20 = (bf16[96,1536]{1,0:T(8,128)(2,1)S(1)}, bf16[96,1536]{1,0:T(8,128)(2,1)S(1)}, u32[]{:S(2)}, u32[]{:S(2)}) collective-permute-start(bf16[96,1536]{1,0:T(8,128)(2,1)S(1)} %copy-done.14), channel_id=1, source_target_pairs={{0,28},{4,24},{8,20},{12,16},{16,12},{20,8},{24,4},{28,0},{1,29},{... | collective-permute-start | bytes 884744 | tf_op jit(solution)/shard_map/ppermute | solution.py:16
  140.9 12.6 %collective-permute-start.19 = (bf16[96,1536]{1,0:T(8,128)(2,1)S(1)}, bf16[96,1536]{1,0:T(8,128)(2,1)S(1)}, u32[]{:S(2)}, u32[]{:S(2)}) collective-permute-start(bf16[96,1536]{1,0:T(8,128)(2,1)S(1)} %copy-done.12), channel_id=1, source_target_pairs={{0,24},{4,28},{8,16},{12,20},{16,8},{20,12},{24,0},{28,4},{1,25},{... | collective-permute-start | bytes 884744 | tf_op jit(solution)/shard_map/ppermute | solution.py:16
  159.2 18.0 %collective-permute-start.26 = (bf16[2,96,1536]{2,1,0:T(8,128)(2,1)S(1)}, bf16[2,96,1536]{2,1,0:T(8,128)(2,1)S(1)}, u32[]{:S(2)}, u32[]{:S(2)}) collective-permute-start(bf16[2,96,1536]{2,1,0:T(8,128)(2,1)S(1)} %shard_map.64.refs_0_), channel_id=1, source_target_pairs={{0,2},{1,3},{2,0},{3,1},{4,6},{5,7},{6,4},{7,5},{8,10},{9,11},{10,... | collective-permute-start | bytes 1769480 | tf_op jit(solution)/shard_map/ppermute | solution.py:16
  160.9 13.9 %collective-permute-start.27 = (f32[2,64,512]{2,1,0:T(8,128)S(1)}, f32[2,64,512]{2,1,0:T(8,128)S(1)}, u32[]{:S(2)}, u32[]{:S(2)}) collective-permute-start(f32[2,64,512]{2,1,0:T(8,128)S(1)} %get-tuple-element.125), channel_id=1, source_target_pairs={{0,5},{1,4},{2,7},{3,6},{4,1},{5,0},{6,3},{7,2},{8,13},{9,12},{10,... | collective-permute-start | bytes 786440 | tf_op jit(solution)/shard_map/ppermute | solution.py:274
  162.2 15.0 %collective-permute-start.23 = (f32[2,64,512]{2,1,0:T(8,128)S(1)}, f32[2,64,512]{2,1,0:T(8,128)S(1)}, u32[]{:S(2)}, u32[]{:S(2)}) collective-permute-start(f32[2,64,512]{2,1,0:T(8,128)S(1)} %get-tuple-element.118), channel_id=1, source_target_pairs={{0,4},{4,0},{8,12},{12,8},{16,20},{20,16},{24,28},{28,24},{1,5},{5... | collective-permute-start | bytes 786440 | tf_op jit(solution)/shard_map/ppermute | solution.py:16
  177.3 18.7 %collective-permute-start.38 = (bf16[2,32,1536]{2,1,0:T(8,128)(2,1)S(1)}, bf16[2,32,1536]{2,1,0:T(8,128)(2,1)S(1)}, u32[]{:S(2)}, u32[]{:S(2)}) collective-permute-start(bf16[2,32,1536]{2,1,0:T(8,128)(2,1)S(1)} %shard_map.67.refs_0_), channel_id=1, source_target_pairs={{0,2},{1,3},{2,0},{3,1},{4,6},{5,7},{6,4},{7,5},{8,10},{9,11},{10,... | collective-permute-start | bytes 589832 | tf_op jit(solution)/shard_map/ppermute | solution.py:16
  184.1 12.0 %collective-permute-start.30 = (f32[64,512]{1,0:T(8,128)S(1)}, f32[64,512]{1,0:T(8,128)S(1)}, u32[]{:S(2)}, u32[]{:S(2)}) collective-permute-start(f32[64,512]{1,0:T(8,128)S(1)} %slice_bitcast_fusion.1), channel_id=1, source_target_pairs={{0,16},{4,20},{8,24},{12,28},{16,0},{20,4},{24,8},{28,12},{1,17},{... | collective-permute-start | bytes 393224 | tf_op jit(solution)/shard_map/ppermute | solution.py:16
  188.7 13.4 %collective-permute-start.33 = (f32[2,48,512]{2,1,0:T(8,128)S(1)}, f32[2,48,512]{2,1,0:T(8,128)S(1)}, u32[]{:S(2)}, u32[]{:S(2)}) collective-permute-start(f32[2,48,512]{2,1,0:T(8,128)S(1)} %get-tuple-element.132), channel_id=1, source_target_pairs={{0,1},{1,0},{2,3},{3,2},{4,5},{5,4},{6,7},{7,6},{8,9},{9,8},{10,11... | collective-permute-start | bytes 589832 | tf_op jit(solution)/shard_map/ppermute | solution.py:16
  188.8 13.8 %collective-permute-start.32 = (f32[2,48,512]{2,1,0:T(8,128)S(1)}, f32[2,48,512]{2,1,0:T(8,128)S(1)}, u32[]{:S(2)}, u32[]{:S(2)}) collective-permute-start(f32[2,48,512]{2,1,0:T(8,128)S(1)} %get-tuple-element.131), channel_id=1, source_target_pairs={{0,4},{4,0},{8,12},{12,8},{16,20},{20,16},{24,28},{28,24},{1,5},{5... | collective-permute-start | bytes 589832 | tf_op jit(solution)/shard_map/ppermute | solution.py:16
  190.7 11.8 %collective-permute-start.34 = (f32[2,48,512]{2,1,0:T(8,128)S(1)}, f32[2,48,512]{2,1,0:T(8,128)S(1)}, u32[]{:S(2)}, u32[]{:S(2)}) collective-permute-start(f32[2,48,512]{2,1,0:T(8,128)S(1)} %get-tuple-element.134), channel_id=1, source_target_pairs={{0,5},{1,4},{2,7},{3,6},{4,1},{5,0},{6,3},{7,2},{8,13},{9,12},{10,... | collective-permute-start | bytes 589832 | tf_op jit(solution)/shard_map/ppermute | solution.py:274
  202.6 11.1 %collective-permute-start.35 = (f32[48,512]{1,0:T(8,128)S(1)}, f32[48,512]{1,0:T(8,128)S(1)}, u32[]{:S(2)}, u32[]{:S(2)}) collective-permute-start(f32[48,512]{1,0:T(8,128)S(1)} %get-tuple-element.149), channel_id=1, source_target_pairs={{0,8},{4,12},{8,0},{12,4},{16,24},{20,28},{24,16},{28,20},{1,9},{5... | collective-permute-start | bytes 294920 | tf_op jit(solution)/shard_map/ppermute | solution.py:16
  (38 other events, 566.5 us)

commit v3 on v2

--- a/solution.py
+++ b/solution.py
@@ -24,7 +24,7 @@
     return pl.CostEstimate(flops=flops // COST_SCALE, bytes_accessed=nbytes // COST_SCALE, transcendentals=0)
 
 
-def pack(adjoint, table, where, first, count, ks, tiles):
+def pack(adjoint, table, where, jobs, tiles):
     halves, _, points = adjoint.shape
     pen_dev = points // PEN_LEN
     share = pen_dev // tiles
@@ -33,9 +33,9 @@
     exact = all(x * magic >> 20 == x // pen_dev for x in range(tiles * pen_dev))
 
     def body(table_ref, where_ref, in_ref, *refs):
-        outs = refs[: len(ks)]
+        outs = refs[: len(jobs)]
         if build:
-            made, seen = refs[len(ks) :]
+            made, seen = refs[len(jobs) :]
             place = where_ref[0]
             for k in range(tiles):
                 seen[k] = 0
@@ -51,7 +51,7 @@
             lax.fori_loop(0, pen_dev, enter, 0, unroll=8)
         else:
             made = table_ref
-        for o, k in enumerate(ks):
+        for o, (k, first, count) in enumerate(jobs):
             for t in range(share):
                 start = pl.multiple_of(made[k * share + t] * PEN_LEN, PEN_LEN)
                 for h in range(halves):
@@ -63,12 +63,12 @@
     return pl.pallas_call(
         body,
         in_specs=[smem, smem, vmem],
-        out_specs=[vmem] * len(ks) + [smem] * build,
-        out_shape=[jax.ShapeDtypeStruct((halves * count, share * PEN_LEN), jnp.bfloat16)] * len(ks)
+        out_specs=[vmem] * len(jobs) + [smem] * build,
+        out_shape=[jax.ShapeDtypeStruct((halves * count, share * PEN_LEN), jnp.bfloat16) for _, _, count in jobs]
         + [jax.ShapeDtypeStruct((pen_dev,), jnp.int32)] * build,
         scratch_shapes=[pltpu.SMEM((tiles,), jnp.int32)] * build,
         compiler_params=params(),
-        cost_estimate=cost(0, 4 * halves * count * points),
+        cost_estimate=cost(0, 4 * halves * sum(count for _, _, count in jobs) * share * PEN_LEN),
     )(table, where, adjoint)
 
 
@@ -249,10 +249,12 @@
 
     tables = [pencil_map]
 
-    def pack_rows(source, first, count, ks):
-        packed = pack(source, tables[-1], where, first, count, ks, tiles)
-        tables.extend(packed[len(ks) :])
-        return dict(zip(ks, packed))
+    def pack_rows(source, *runs):
+        jobs = [(k, first, count) for first, count, ks in runs for k in ks]
+        packed = pack(source, tables[-1], where, jobs, tiles)
+        tables.extend(packed[len(jobs) :])
+        out = [dict(zip(ks, packed[sum(len(r[2]) for r in runs[:i]) :])) for i, (_, _, ks) in enumerate(runs)]
+        return out[0] if len(out) == 1 else out
 
     def over_space(packed, ks, *done):
         return [xor_send(after(packed[k], *done), "space", k) for k in ks]
@@ -306,17 +308,17 @@
     start_low, rest_low = low[: len(low) // 2], low[len(low) // 2 :]
     early = 2 + len(near_a)
 
-    packed_a = pack_rows(adjoint, 0, rows_a, start_low)
-    packed_n = pack_rows(after(adjoint, packed_a[low[0]]), 0, rows_out, [0, 1])
-    packed_na = pack_rows(after(adjoint, packed_n[0]), 0, rows_a, near_a)
+    packed_n, packed_a, packed_na = pack_rows(
+        adjoint, (0, rows_out, [0, 1]), (0, rows_a, start_low), (0, rows_a, near_a)
+    )
     low_a = over_space(packed_a, start_low)
     near_1 = over_space(packed_n, [1])[0]
     got_na = over_space(packed_na, near_a)
     cross_0 = across(packed_n[0])
     own_1 = weigh(after(primal, packed_na[near_a[0]]), weights, table, 0, early, tiles)
     own_2 = weigh(after(primal, own_1), weights, table, early, tiles - early, tiles)
-    packed_ar = pack_rows(after(adjoint, own_2), 0, rows_a, rest_low)
-    packed_nr = pack_rows(after(adjoint, packed_ar[rest_low[0]]), rows_a, rows_bc, near_a)
+    packed_ar = pack_rows(after(adjoint, own_2), (0, rows_a, rest_low))
+    packed_nr = pack_rows(after(adjoint, packed_ar[rest_low[0]]), (rows_a, rows_bc, near_a))
 
     done = (*low_a, near_1, *got_na, cross_0[-1], packed_nr[near_a[0]])
     low_a = low_a + over_space(packed_ar, rest_low, *done)
@@ -324,11 +326,11 @@
     cross_1 = across(near_1, *done)
     other_1 = xor_send(after(own_1, *done), "snap", 1)
     other_2 = xor_send(after(own_2, *done), "snap", 1)
-    packed_nb = pack_rows(after(adjoint, *done), 0, rows_a, near_b)
-    packed_ah = pack_rows(after(adjoint, packed_nb[near_b[0]]), 0, rows_a, high)
-    packed_bc = pack_rows(after(adjoint, packed_ah[high[0]]), rows_a, rows_bc, low + near_b)
-    packed_b = pack_rows(after(adjoint, packed_bc[low[0]]), rows_a, rows_b, high)
-    packed_c = pack_rows(after(adjoint, packed_b[high[0]]), rows_a + rows_b, rows_c, high)
+    packed_nb = pack_rows(after(adjoint, *done), (0, rows_a, near_b))
+    packed_ah = pack_rows(after(adjoint, packed_nb[near_b[0]]), (0, rows_a, high))
+    packed_bc = pack_rows(after(adjoint, packed_ah[high[0]]), (rows_a, rows_bc, low + near_b))
+    packed_b = pack_rows(after(adjoint, packed_bc[low[0]]), (rows_a, rows_b, high))
+    packed_c = pack_rows(after(adjoint, packed_b[high[0]]), (rows_a + rows_b, rows_c, high))
 
     done = (*low_a, *got_na, cross_1[-1], other_1, other_2, packed_c[high[0]])
     high_a = over_space(packed_ah, high, *done)
@@ -349,7 +351,7 @@
     groups = [(cross_0, 1, plain), (cross_1, 1, plain), (cross_na, len(near_a), two_runs)]
     product = multiply(groups, own_1, after(other_1, *done), 0, where, None, rows_out, halves, members)
 
-    done = (*low_bc, *got_nb_bc, cross_nb[-1], cross_high_a[-1], product)
+    done = (*got_nb_bc, *low_bc, cross_nb[-1], cross_high_a[-1], product)
     high_b = over_space(packed_b, high, *done)
     cross_low_bc = across(join(low_bc), *done)
     cross_nb_bc = across(join(got_nb_bc), *done)
@@ -376,7 +378,7 @@
     sum_b = Sum(pair_b, sum_a.swapped).swap()
     groups = [(cross_high_c, len(high), whole_rows(rows_c, 0, rows_c))]
     pair_c = multiply(
-        groups, own_2, after(other_2, *sum_a.last), first_high, where, (product_bc, rows_b), rows_c, halves, members
+        groups, own_2, after(other_2, *sum_a.last[::2]), first_high, where, (product_bc, rows_b), rows_c, halves, members
     )
     sum_c = Sum(pair_c).swap()
     return jnp.concatenate([total_a, sum_b.finish(), sum_c.finish()], axis=0)

time: 219 us -> 214 us (0.977)
  starting transfers between devices: 61.5 us -> 57.5 us
  waiting for transfers between devices: 92.8 us -> 95.6 us
  Pallas kernels: 50.3 us -> 48.1 us
    ppermute x42, starting transfers between devices: 59.4 us -> 55.2 us  [xor_send(): return lax.ppermute(x, axis, [(i, i ^ k) for i in range(n)])]
    pallas_call x10 -> x8, Pallas kernels: 10.4 us -> 8.45 us  [pack(): pl.pallas_call(body, in_specs=[smem, smem, vmem], out_specs=[vmem] * len(...]
    unnamed x50 -> x44, local copies, waits for them, and re-layouts: 10.5 us -> 9.44 us
  transfers between devices with their start and end apart: 45 -> 45, of which waited for: 21 -> 21; matrix products, arithmetic and copies ran while one was open for 1% -> 1% of each run, Pallas kernels for 22% -> 21%
where the time goes in v3:
time: 214 us
  waiting for transfers between devices  95.6 us (45%)
  starting transfers between devices  57.5 us (27%)
  Pallas kernels  48.1 us (22%)
  local copies, waits for them, and re-layouts  9.74 us (5%)
  other arithmetic  2.69 us (1%)
    ppermute x42, waiting for transfers between devices, xor_send(): return lax.ppermute(x, axis, [(i, i ^ k) for i in range(n)])  93.6 us
    ppermute x42, starting transfers between devices, xor_send(): return lax.ppermute(x, axis, [(i, i ^ k) for i in range(n)])  55.2 us
    pallas_call x5, Pallas kernels, multiply(): pl.pallas_call(body, in_specs=[pl.BlockSpec(memory_space=pltpu.SMEM)] + [...  34.3 us
    unnamed x44, local copies, waits for them, and re-layouts  9.44 us
    pallas_call x8, Pallas kernels, pack(): pl.pallas_call(body, in_specs=[smem, smem, vmem], out_specs=[vmem] * len(...  8.45 us
    pallas_call x2, Pallas kernels, weigh(): pl.pallas_call(body, in_specs=[pl.BlockSpec(memory_space=pltpu.SMEM), vme...  4.48 us
  transfers between devices with their start and end apart: 45, of which 21 were waited for; matrix products, arithmetic and copies ran while one was open for 1% of the time, Pallas kernels for 21%

profile of v3, /device:TPU:0, one launch (start us, length us, event | category | flops | bytes accessed | tf_op | source)
XLA Modules:
  0.0 214.1 jit_solution(12532744857319271356)
XLA Ops:
  0.1 2.8 %copy-done = bf16[256,12288]{1,0:T(8,128)(2,1)S(1)} copy-done((bf16[256,12288]{1,0:T(8,128)(2,1)S(1)}, bf16[256,12288]{1,0:T(8,128)(2,1)}, u32[]{:S(2)}) %copy-start) | copy-done | bytes 6291480
  3.6 2.8 %shard_map.46 = (bf16[256,1536]{1,0:T(8,128)(2,1)S(1)}, bf16[256,1536]{1,0:T(8,128)(2,1)}, bf16[128,1536]{1,0:T(8,128)(2,1)S(1)}, bf16[128,1536]{1,0:T(8,128)(2,1)}, s32[96]{0:T(128)S(1)}) custom-call(s32[768]{0:T(1024)S(1)} %copy-done.6, s32[2]{0:T(128)S(1)} %pad_add_fusion.where_ref, bf16[2,128,12288]{2,1,0:T(8,128)(2,1)S(1)} %bitcast.46), custom_call_target="tpu_custom_call" | custom-call | bytes 4718592 | tf_op jit(solution)/shard_map/pallas_call | solution.py:63
  6.4 3.1 %collective-permute-start.2 = (bf16[128,1536]{1,0:T(8,128)(2,1)}, bf16[128,1536]{1,0:T(8,128)(2,1)S(1)}, u32[]{:S(2)}, u32[]{:S(2)}) collective-permute-start(bf16[128,1536]{1,0:T(8,128)(2,1)} %get-tuple-element.75), channel_id=1, source_target_pairs={{0,8},{4,12},{8,0},{12,4},{16,24},{20,28},{24,16},{28,20},{1,9},{5... | collective-permute-start | bytes 1179656 | tf_op jit(solution)/shard_map/ppermute | solution.py:16
  9.5 2.6 %collective-permute-start = (bf16[128,1536]{1,0:T(8,128)(2,1)S(1)}, bf16[128,1536]{1,0:T(8,128)(2,1)S(1)}, u32[]{:S(2)}, u32[]{:S(2)}) collective-permute-start(bf16[128,1536]{1,0:T(8,128)(2,1)S(1)} %get-tuple-element.73), channel_id=1, source_target_pairs={{0,16},{4,20},{8,24},{12,28},{16,0},{20,4},{24,8},{28,12},{1,17},{... | collective-permute-start | bytes 1179656 | tf_op jit(solution)/shard_map/ppermute | solution.py:16
  16.0 4.6 %copy-done.2 = bf16[512,12288]{1,0:T(8,128)(2,1)S(1)} copy-done((bf16[512,12288]{1,0:T(8,128)(2,1)S(1)}, bf16[512,12288]{1,0:T(8,128)(2,1)}, u32[]{:S(2)}) %copy-start.2) | copy-done | bytes 12582936
  22.5 2.7 %shard_map.48.refs_6_.refs_4_.refs_2_ = bf16[5,512,1536]{2,1,0:T(8,128)(2,1)S(1)} custom-call(s32[96]{0:T(128)S(1)} %reshape.70.table_ref, bf16[512,12288]{1,0:T(8,128)(2,1)S(1)} %copy-done.2, f32[1,12288]{1,0:T(1,128)S(1)} %bitcast.57), custom_call_target="tpu_custom_call" | custom-call | flops 3145728 | bytes 18874368 | tf_op jit(solution)/shard_map/pallas_call | solution.py:104
  27.2 3.7 %collective-permute-done.3.refs_1_ = bf16[256,1536]{1,0:T(8,128)(2,1)} collective-permute-done((bf16[256,1536]{1,0:T(8,128)(2,1)S(1)}, bf16[256,1536]{1,0:T(8,128)(2,1)}, u32[]{:S(2)}, u32[]{:S(2)}) %collective-permute-start.3) | collective-permute-done | bytes 786464 | tf_op jit(solution)/shard_map/ppermute | solution.py:16
  40.7 9.7 %collective-permute-done.5.refs_1_ = bf16[128,1536]{1,0:T(8,128)(2,1)S(1)} collective-permute-done((bf16[128,1536]{1,0:T(8,128)(2,1)S(1)}, bf16[128,1536]{1,0:T(8,128)(2,1)S(1)}, u32[]{:S(2)}, u32[]{:S(2)}) %collective-permute-start.5) | collective-permute-done | bytes 393248 | tf_op jit(solution)/shard_map/ppermute | solution.py:16
  50.6 4.1 %collective-permute-done.4.refs_1_ = bf16[128,1536]{1,0:T(8,128)(2,1)S(1)} collective-permute-done((bf16[128,1536]{1,0:T(8,128)(2,1)S(1)}, bf16[128,1536]{1,0:T(8,128)(2,1)S(1)}, u32[]{:S(2)}, u32[]{:S(2)}) %collective-permute-start.4) | collective-permute-done | bytes 393248 | tf_op jit(solution)/shard_map/ppermute | solution.py:16
  56.9 2.3 %collective-permute-start.11 = (bf16[128,1536]{1,0:T(8,128)(2,1)S(1)}, bf16[128,1536]{1,0:T(8,128)(2,1)S(1)}, u32[]{:S(2)}, u32[]{:S(2)}) collective-permute-start(bf16[128,1536]{1,0:T(8,128)(2,1)S(1)} %get-tuple-element.98), channel_id=1, source_target_pairs={{0,28},{4,24},{8,20},{12,16},{16,12},{20,8},{24,4},{28,0},{1,29},{... | collective-permute-start | bytes 1179656 | tf_op jit(solution)/shard_map/ppermute | solution.py:16
  59.2 2.5 %collective-permute-start.10 = (bf16[128,1536]{1,0:T(8,128)(2,1)S(1)}, bf16[128,1536]{1,0:T(8,128)(2,1)S(1)}, u32[]{:S(2)}, u32[]{:S(2)}) collective-permute-start(bf16[128,1536]{1,0:T(8,128)(2,1)S(1)} %get-tuple-element.96), channel_id=1, source_target_pairs={{0,24},{4,28},{8,16},{12,20},{16,8},{20,12},{24,0},{28,4},{1,25},{... | collective-permute-start | bytes 1179656 | tf_op jit(solution)/shard_map/ppermute | solution.py:16
  61.7 10.0 %collective-permute-done.11.refs_1_ = bf16[128,1536]{1,0:T(8,128)(2,1)S(1)} collective-permute-done((bf16[128,1536]{1,0:T(8,128)(2,1)S(1)}, bf16[128,1536]{1,0:T(8,128)(2,1)S(1)}, u32[]{:S(2)}, u32[]{:S(2)}) %collective-permute-start.11) | collective-permute-done | bytes 393248 | tf_op jit(solution)/shard_map/ppermute | solution.py:16
  71.7 8.4 %collective-permute-done.10.refs_0_ = bf16[128,1536]{1,0:T(8,128)(2,1)S(1)} collective-permute-done((bf16[128,1536]{1,0:T(8,128)(2,1)S(1)}, bf16[128,1536]{1,0:T(8,128)(2,1)S(1)}, u32[]{:S(2)}, u32[]{:S(2)}) %collective-permute-start.10) | collective-permute-done | bytes 393248 | tf_op jit(solution)/shard_map/ppermute | solution.py:16
  80.3 3.7 %collective-permute-done.9.refs_0_ = bf16[128,1536]{1,0:T(8,128)(2,1)S(1)} collective-permute-done((bf16[128,1536]{1,0:T(8,128)(2,1)S(1)}, bf16[128,1536]{1,0:T(8,128)(2,1)S(1)}, u32[]{:S(2)}, u32[]{:S(2)}) %collective-permute-start.9) | collective-permute-done | bytes 393248 | tf_op jit(solution)/shard_map/ppermute | solution.py:16
  84.0 5.4 %collective-permute-done.12.refs_3_ = bf16[2,128,1536]{2,1,0:T(8,128)(2,1)S(1)} collective-permute-done((bf16[2,128,1536]{2,1,0:T(8,128)(2,1)S(1)}, bf16[2,128,1536]{2,1,0:T(8,128)(2,1)S(1)}, u32[]{:S(2)}, u32[]{:S(2)}) %collective-permute-start.12) | collective-permute-done | bytes 786464 | tf_op jit(solution)/shard_map/ppermute | solution.py:16
  91.5 5.7 %collective-permute-start.18 = (bf16[128,1536]{1,0:T(8,128)(2,1)}, bf16[128,1536]{1,0:T(8,128)(2,1)S(1)}, u32[]{:S(2)}, u32[]{:S(2)}) collective-permute-start(bf16[128,1536]{1,0:T(8,128)(2,1)} %get-tuple-element.110), channel_id=1, source_target_pairs={{0,20},{4,16},{8,28},{12,24},{16,4},{20,0},{24,12},{28,8},{1,21},{... | collective-permute-start | bytes 1179656 | tf_op jit(solution)/shard_map/ppermute | solution.py:16
  98.0 10.2 %shard_map.59.refs_8_.refs_6_ = f32[2,256,1024]{2,1,0:T(8,128)} custom-call(s32[2]{0:T(128)S(1)} %pad_add_fusion.where_ref, bf16[256,1536]{1,0:T(8,128)(2,1)S(1)} %get-tuple-element.76.refs_0_, bf16[256,1536]{1,0:T(8,128)(2,1)} %collective-permute-done.3.refs_1_, bf16[256,1536]{1,0:T(8,128)(2,1)} %collective-permute-done.1.refs_2_, ...), custom_call_target="tpu_custom_call" | custom-call | flops 4831838208 | bytes 14155776 | tf_op jit(solution)/shard_map/pallas_call | solution.py:212
  108.2 14.8 %collective-permute-done.18.refs_1_ = bf16[128,1536]{1,0:T(8,128)(2,1)S(1)} collective-permute-done((bf16[128,1536]{1,0:T(8,128)(2,1)}, bf16[128,1536]{1,0:T(8,128)(2,1)S(1)}, u32[]{:S(2)}, u32[]{:S(2)}) %collective-permute-start.18) | collective-permute-done | bytes 393248 | tf_op jit(solution)/shard_map/ppermute | solution.py:16
  123.0 7.2 %collective-permute-done.17.refs_0_ = bf16[128,1536]{1,0:T(8,128)(2,1)S(1)} collective-permute-done((bf16[128,1536]{1,0:T(8,128)(2,1)S(1)}, bf16[128,1536]{1,0:T(8,128)(2,1)S(1)}, u32[]{:S(2)}, u32[]{:S(2)}) %collective-permute-start.17) | collective-permute-done | bytes 393248 | tf_op jit(solution)/shard_map/ppermute | solution.py:16
  132.6 2.7 %collective-permute-start.20 = (bf16[96,1536]{1,0:T(8,128)(2,1)S(1)}, bf16[96,1536]{1,0:T(8,128)(2,1)S(1)}, u32[]{:S(2)}, u32[]{:S(2)}) collective-permute-start(bf16[96,1536]{1,0:T(8,128)(2,1)S(1)} %copy-done.11), channel_id=1, source_target_pairs={{0,28},{4,24},{8,20},{12,16},{16,12},{20,8},{24,4},{28,0},{1,29},{... | collective-permute-start | bytes 884744 | tf_op jit(solution)/shard_map/ppermute | solution.py:16
  137.2 9.0 %shard_map.60 = (f32[2,64,512]{2,1,0:T(8,128)S(1)}, f32[2,64,512]{2,1,0:T(8,128)S(1)}, f32[2,64,512]{2,1,0:T(8,128)S(1)}, f32[2,64,512]{2,1,0:T(8,128)S(1)}) custom-call(s32[2]{0:T(128)S(1)} %pad_add_fusion.where_ref, bf16[128,1536]{1,0:T(8,128)(2,1)S(1)} %collective-permute-done.9.refs_0_, bf16[128,1536]{1,0:T(8,128)(2,1)S(1)} %collective-permute-done.14.refs_1_, ...), custom_call_target="tpu_custom_call" | custom-call | flops 4026531840 | bytes 19660800 | tf_op jit(solution)/shard_map/pallas_call | solution.py:212
  146.2 3.4 %collective-permute-done.19.refs_0_ = bf16[96,1536]{1,0:T(8,128)(2,1)S(1)} collective-permute-done((bf16[96,1536]{1,0:T(8,128)(2,1)S(1)}, bf16[96,1536]{1,0:T(8,128)(2,1)S(1)}, u32[]{:S(2)}, u32[]{:S(2)}) %collective-permute-start.19) | collective-permute-done | bytes 294944 | tf_op jit(solution)/shard_map/ppermute | solution.py:16
  149.8 7.5 %collective-permute-done.22.refs_1_ = bf16[128,1536]{1,0:T(8,128)(2,1)S(1)} collective-permute-done((bf16[128,1536]{1,0:T(8,128)(2,1)S(1)}, bf16[128,1536]{1,0:T(8,128)(2,1)S(1)}, u32[]{:S(2)}, u32[]{:S(2)}) %collective-permute-start.22) | collective-permute-done | bytes 393248 | tf_op jit(solution)/shard_map/ppermute | solution.py:16
  159.2 2.0 collective-permute-start.23
  161.5 2.9 %collective-permute-start.24 = (bf16[32,1536]{1,0:T(8,128)(2,1)S(1)}, bf16[32,1536]{1,0:T(8,128)(2,1)S(1)}, u32[]{:S(2)}, u32[]{:S(2)}) collective-permute-start(bf16[32,1536]{1,0:T(8,128)(2,1)S(1)} %copy-done.13), channel_id=1, source_target_pairs={{0,24},{4,28},{8,16},{12,20},{16,8},{20,12},{24,0},{28,4},{1,25},{... | collective-permute-start | bytes 294920 | tf_op jit(solution)/shard_map/ppermute | solution.py:16
  164.5 6.4 %shard_map.63.refs_4_ = f32[2,128,1024]{2,1,0:T(8,128)S(1)} custom-call(s32[2]{0:T(128)S(1)} %pad_add_fusion.where_ref, bf16[128,1536]{1,0:T(8,128)(2,1)S(1)} %collective-permute-done.16.refs_0_, bf16[128,1536]{1,0:T(8,128)(2,1)S(1)} %collective-permute-done.22.refs_1_, bf16[2,128,1536]{2,1,0:T(8,128)(2,1)S(1)} %shard_map.61.refs_2_, ...), custom_call_target="tpu_custom_call" | custom-call | flops 2415919104 | bytes 11796480 | tf_op jit(solution)/shard_map/pallas_call | solution.py:212
  170.9 4.4 %collective-permute-done.23 = f32[2,64,512]{2,1,0:T(8,128)S(1)} collective-permute-done((f32[2,64,512]{2,1,0:T(8,128)S(1)}, f32[2,64,512]{2,1,0:T(8,128)S(1)}, u32[]{:S(2)}, u32[]{:S(2)}) %collective-permute-start.23) | collective-permute-done | bytes 262176 | tf_op jit(solution)/shard_map/ppermute | solution.py:16
  178.3 2.0 collective-permute-start.31
  181.7 4.5 %shard_map.64 = (f32[2,48,512]{2,1,0:T(8,128)S(1)}, f32[2,48,512]{2,1,0:T(8,128)S(1)}, f32[2,48,512]{2,1,0:T(8,128)S(1)}, f32[2,48,512]{2,1,0:T(8,128)S(1)}) custom-call(s32[2]{0:T(128)S(1)} %pad_add_fusion.where_ref, bf16[2,96,1536]{2,1,0:T(8,128)(2,1)S(1)} %shard_map.62.refs_0_, bf16[2,96,1536]{2,1,0:T(8,128)(2,1)S(1)} %collective-permute-done.26.refs_1_, ...), custom_call_target="tpu_custom_call" | custom-call | flops 1207959552 | bytes 7471104 | tf_op jit(solution)/shard_map/pallas_call | solution.py:212
  188.2 4.2 %shard_map.66 = (f32[2,16,512]{2,1,0:T(8,128)S(1)}, f32[2,16,512]{2,1,0:T(8,128)S(1)}, f32[2,16,512]{2,1,0:T(8,128)S(1)}, f32[2,16,512]{2,1,0:T(8,128)S(1)}) custom-call(s32[2]{0:T(128)S(1)} %pad_add_fusion.where_ref, bf16[2,32,1536]{2,1,0:T(8,128)(2,1)S(1)} %shard_map.65.refs_0_, bf16[2,32,1536]{2,1,0:T(8,128)(2,1)S(1)} %collective-permute-done.38.refs_1_, ...), custom_call_target="tpu_custom_call" | custom-call | flops 402653184 | bytes 6684672 | tf_op jit(solution)/shard_map/pallas_call | solution.py:212
  195.4 2.0 collective-permute-done.34
  209.5 3.8 %collective-permute-done.36 = f32[48,512]{1,0:T(8,128)S(1)} collective-permute-done((f32[48,512]{1,0:T(8,128)S(1)}, f32[48,512]{1,0:T(8,128)S(1)}, u32[]{:S(2)}, u32[]{:S(2)}) %collective-permute-start.36) | collective-permute-done | bytes 98336 | tf_op jit(solution)/shard_map/ppermute | solution.py:16
  (149 shorter events, 52.5 us)
Async XLA Ops:
  6.4 20.8 %collective-permute-start.2 = (bf16[128,1536]{1,0:T(8,128)(2,1)}, bf16[128,1536]{1,0:T(8,128)(2,1)S(1)}, u32[]{:S(2)}, u32[]{:S(2)}) collective-permute-start(bf16[128,1536]{1,0:T(8,128)(2,1)} %get-tuple-element.75), channel_id=1, source_target_pairs={{0,8},{4,12},{8,0},{12,4},{16,24},{20,28},{24,16},{28,20},{1,9},{5... | collective-permute-start | bytes 1179656 | tf_op jit(solution)/shard_map/ppermute | solution.py:16
  9.5 17.8 %collective-permute-start = (bf16[128,1536]{1,0:T(8,128)(2,1)S(1)}, bf16[128,1536]{1,0:T(8,128)(2,1)S(1)}, u32[]{:S(2)}, u32[]{:S(2)}) collective-permute-start(bf16[128,1536]{1,0:T(8,128)(2,1)S(1)} %get-tuple-element.73), channel_id=1, source_target_pairs={{0,16},{4,20},{8,24},{12,28},{16,0},{20,4},{24,8},{28,12},{1,17},{... | collective-permute-start | bytes 1179656 | tf_op jit(solution)/shard_map/ppermute | solution.py:16
  12.1 18.8 %collective-permute-start.3 = (bf16[256,1536]{1,0:T(8,128)(2,1)S(1)}, bf16[256,1536]{1,0:T(8,128)(2,1)}, u32[]{:S(2)}, u32[]{:S(2)}) collective-permute-start(bf16[256,1536]{1,0:T(8,128)(2,1)S(1)} %get-tuple-element.76.refs_0_), channel_id=1, source_target_pairs={{0,2},{1,3},{2,0},{3,1},{4,6},{5,7},{6,4},{7,5},{8,10},{9,11},{10,... | collective-permute-start | bytes 2359304 | tf_op jit(solution)/shard_map/ppermute | solution.py:16
  13.6 18.8 %collective-permute-start.1 = (bf16[256,1536]{1,0:T(8,128)(2,1)}, bf16[256,1536]{1,0:T(8,128)(2,1)}, u32[]{:S(2)}, u32[]{:S(2)}) collective-permute-start(bf16[256,1536]{1,0:T(8,128)(2,1)} %get-tuple-element.74), channel_id=1, source_target_pairs={{0,4},{4,0},{8,12},{12,8},{16,20},{20,16},{24,28},{28,24},{1,5},{5... | collective-permute-start | bytes 2359304 | tf_op jit(solution)/shard_map/ppermute | solution.py:16
  32.3 22.5 %collective-permute-start.8 = (bf16[5,512,1536]{2,1,0:T(8,128)(2,1)S(1)}, bf16[5,512,1536]{2,1,0:T(8,128)(2,1)S(1)}, u32[]{:S(2)}, u32[]{:S(2)}) collective-permute-start(bf16[5,512,1536]{2,1,0:T(8,128)(2,1)S(1)} %shard_map.48.refs_6_.refs_4_.refs_2_), channel_id=1, source_target_pairs={{0,1},{1,0},{2,3},{3,2},{4,5},{5,4},{6,7},{7,6},{8,9},{9,8},{10,11... | collective-permute-start | bytes 23592968 | tf_op jit(solution)/shard_map/ppermute | solution.py:16
  32.3 22.4 %collective-permute-start.7 = (bf16[3,512,1536]{2,1,0:T(8,128)(2,1)S(1)}, bf16[3,512,1536]{2,1,0:T(8,128)(2,1)S(1)}, u32[]{:S(2)}, u32[]{:S(2)}) collective-permute-start(bf16[3,512,1536]{2,1,0:T(8,128)(2,1)S(1)} %shard_map.47.refs_6_), channel_id=1, source_target_pairs={{0,1},{1,0},{2,3},{3,2},{4,5},{5,4},{6,7},{7,6},{8,9},{9,8},{10,11... | collective-permute-start | bytes 14155784 | tf_op jit(solution)/shard_map/ppermute | solution.py:16
  32.8 21.9 %collective-permute-start.6 = (bf16[256,1536]{1,0:T(8,128)(2,1)}, bf16[256,1536]{1,0:T(8,128)(2,1)S(1)}, u32[]{:S(2)}, u32[]{:S(2)}) collective-permute-start(bf16[256,1536]{1,0:T(8,128)(2,1)} %collective-permute-done.1.refs_2_), channel_id=1, source_target_pairs={{0,2},{1,3},{2,0},{3,1},{4,6},{5,7},{6,4},{7,5},{8,10},{9,11},{10,... | collective-permute-start | bytes 2359304 | tf_op jit(solution)/shard_map/ppermute | solution.py:16
  33.4 17.0 %collective-permute-start.5 = (bf16[128,1536]{1,0:T(8,128)(2,1)S(1)}, bf16[128,1536]{1,0:T(8,128)(2,1)S(1)}, u32[]{:S(2)}, u32[]{:S(2)}) collective-permute-start(bf16[128,1536]{1,0:T(8,128)(2,1)S(1)} %shard_map.50), channel_id=1, source_target_pairs={{0,8},{4,12},{8,0},{12,4},{16,24},{20,28},{24,16},{28,20},{1,9},{5... | collective-permute-start | bytes 1179656 | tf_op jit(solution)/shard_map/ppermute | solution.py:16
  33.8 20.8 %collective-permute-start.4 = (bf16[128,1536]{1,0:T(8,128)(2,1)S(1)}, bf16[128,1536]{1,0:T(8,128)(2,1)S(1)}, u32[]{:S(2)}, u32[]{:S(2)}) collective-permute-start(bf16[128,1536]{1,0:T(8,128)(2,1)S(1)} %shard_map.49), channel_id=1, source_target_pairs={{0,20},{4,16},{8,28},{12,24},{16,4},{20,0},{24,12},{28,8},{1,21},{... | collective-permute-start | bytes 1179656 | tf_op jit(solution)/shard_map/ppermute | solution.py:16
  54.8 29.2 %collective-permute-start.13 = (bf16[2,128,1536]{2,1,0:T(8,128)(2,1)S(1)}, bf16[2,128,1536]{2,1,0:T(8,128)(2,1)S(1)}, u32[]{:S(2)}, u32[]{:S(2)}) collective-permute-start(bf16[2,128,1536]{2,1,0:T(8,128)(2,1)S(1)} %shard_map.57.refs_4_), channel_id=1, source_target_pairs={{0,2},{1,3},{2,0},{3,1},{4,6},{5,7},{6,4},{7,5},{8,10},{9,11},{10,... | collective-permute-start | bytes 2359304 | tf_op jit(solution)/shard_map/ppermute | solution.py:16
  56.4 33.1 %collective-permute-start.12 = (bf16[2,128,1536]{2,1,0:T(8,128)(2,1)S(1)}, bf16[2,128,1536]{2,1,0:T(8,128)(2,1)S(1)}, u32[]{:S(2)}, u32[]{:S(2)}) collective-permute-start(bf16[2,128,1536]{2,1,0:T(8,128)(2,1)S(1)} %shard_map.56.refs_2_), channel_id=1, source_target_pairs={{0,2},{1,3},{2,0},{3,1},{4,6},{5,7},{6,4},{7,5},{8,10},{9,11},{10,... | collective-permute-start | bytes 2359304 | tf_op jit(solution)/shard_map/ppermute | solution.py:16
  56.9 14.8 %collective-permute-start.11 = (bf16[128,1536]{1,0:T(8,128)(2,1)S(1)}, bf16[128,1536]{1,0:T(8,128)(2,1)S(1)}, u32[]{:S(2)}, u32[]{:S(2)}) collective-permute-start(bf16[128,1536]{1,0:T(8,128)(2,1)S(1)} %get-tuple-element.98), channel_id=1, source_target_pairs={{0,28},{4,24},{8,20},{12,16},{16,12},{20,8},{24,4},{28,0},{1,29},{... | collective-permute-start | bytes 1179656 | tf_op jit(solution)/shard_map/ppermute | solution.py:16
  59.2 20.9 %collective-permute-start.10 = (bf16[128,1536]{1,0:T(8,128)(2,1)S(1)}, bf16[128,1536]{1,0:T(8,128)(2,1)S(1)}, u32[]{:S(2)}, u32[]{:S(2)}) collective-permute-start(bf16[128,1536]{1,0:T(8,128)(2,1)S(1)} %get-tuple-element.96), channel_id=1, source_target_pairs={{0,24},{4,28},{8,16},{12,20},{16,8},{20,12},{24,0},{28,4},{1,25},{... | collective-permute-start | bytes 1179656 | tf_op jit(solution)/shard_map/ppermute | solution.py:16
  61.7 22.3 %collective-permute-start.9 = (bf16[128,1536]{1,0:T(8,128)(2,1)S(1)}, bf16[128,1536]{1,0:T(8,128)(2,1)S(1)}, u32[]{:S(2)}, u32[]{:S(2)}) collective-permute-start(bf16[128,1536]{1,0:T(8,128)(2,1)S(1)} %shard_map.51), channel_id=1, source_target_pairs={{0,12},{4,8},{8,4},{12,0},{16,28},{20,24},{24,20},{28,16},{1,13},{... | collective-permute-start | bytes 1179656 | tf_op jit(solution)/shard_map/ppermute | solution.py:16
  89.4 41.1 %collective-permute-start.15 = (bf16[2,128,1536]{2,1,0:T(8,128)(2,1)S(1)}, bf16[2,128,1536]{2,1,0:T(8,128)(2,1)S(1)}, u32[]{:S(2)}, u32[]{:S(2)}) collective-permute-start(bf16[2,128,1536]{2,1,0:T(8,128)(2,1)S(1)} %shard_map.58.refs_4_), channel_id=1, source_target_pairs={{0,2},{1,3},{2,0},{3,1},{4,6},{5,7},{6,4},{7,5},{8,10},{9,11},{10,... | collective-permute-start | bytes 2359304 | tf_op jit(solution)/shard_map/ppermute | solution.py:16
  90.1 40.4 %collective-permute-start.14 = (bf16[128,1536]{1,0:T(8,128)(2,1)S(1)}, bf16[128,1536]{1,0:T(8,128)(2,1)S(1)}, u32[]{:S(2)}, u32[]{:S(2)}) collective-permute-start(bf16[128,1536]{1,0:T(8,128)(2,1)S(1)} %collective-permute-done.9.refs_0_), channel_id=1, source_target_pairs={{0,2},{1,3},{2,0},{3,1},{4,6},{5,7},{6,4},{7,5},{8,10},{9,11},{10,... | collective-permute-start | bytes 1179656 | tf_op jit(solution)/shard_map/ppermute | solution.py:16
  91.5 31.5 %collective-permute-start.18 = (bf16[128,1536]{1,0:T(8,128)(2,1)}, bf16[128,1536]{1,0:T(8,128)(2,1)S(1)}, u32[]{:S(2)}, u32[]{:S(2)}) collective-permute-start(bf16[128,1536]{1,0:T(8,128)(2,1)} %get-tuple-element.110), channel_id=1, source_target_pairs={{0,20},{4,16},{8,28},{12,24},{16,4},{20,0},{24,12},{28,8},{1,21},{... | collective-permute-start | bytes 1179656 | tf_op jit(solution)/shard_map/ppermute | solution.py:16
  97.2 33.0 %collective-permute-start.17 = (bf16[128,1536]{1,0:T(8,128)(2,1)S(1)}, bf16[128,1536]{1,0:T(8,128)(2,1)S(1)}, u32[]{:S(2)}, u32[]{:S(2)}) collective-permute-start(bf16[128,1536]{1,0:T(8,128)(2,1)S(1)} %get-tuple-element.108), channel_id=1, source_target_pairs={{0,16},{4,20},{8,24},{12,28},{16,0},{20,4},{24,8},{28,12},{1,17},{... | collective-permute-start | bytes 1179656 | tf_op jit(solution)/shard_map/ppermute | solution.py:16
  97.2 33.3 %collective-permute-start.16 = (bf16[128,1536]{1,0:T(8,128)(2,1)S(1)}, bf16[128,1536]{1,0:T(8,128)(2,1)S(1)}, u32[]{:S(2)}, u32[]{:S(2)}) collective-permute-start(bf16[128,1536]{1,0:T(8,128)(2,1)S(1)} %get-tuple-element.107), channel_id=1, source_target_pairs={{0,12},{4,8},{8,4},{12,0},{16,28},{20,24},{24,20},{28,16},{1,13},{... | collective-permute-start | bytes 1179656 | tf_op jit(solution)/shard_map/ppermute | solution.py:16
  130.5 26.8 %collective-permute-start.21 = (bf16[2,128,1536]{2,1,0:T(8,128)(2,1)S(1)}, bf16[2,128,1536]{2,1,0:T(8,128)(2,1)S(1)}, u32[]{:S(2)}, u32[]{:S(2)}) collective-permute-start(bf16[2,128,1536]{2,1,0:T(8,128)(2,1)S(1)} %shard_map.61.refs_2_), channel_id=1, source_target_pairs={{0,2},{1,3},{2,0},{3,1},{4,6},{5,7},{6,4},{7,5},{8,10},{9,11},{10,... | collective-permute-start | bytes 2359304 | tf_op jit(solution)/shard_map/ppermute | solution.py:16
  132.3 25.0 %collective-permute-start.22 = (bf16[128,1536]{1,0:T(8,128)(2,1)S(1)}, bf16[128,1536]{1,0:T(8,128)(2,1)S(1)}, u32[]{:S(2)}, u32[]{:S(2)}) collective-permute-start(bf16[128,1536]{1,0:T(8,128)(2,1)S(1)} %collective-permute-done.16.refs_0_), channel_id=1, source_target_pairs={{0,2},{1,3},{2,0},{3,1},{4,6},{5,7},{6,4},{7,5},{8,10},{9,11},{10,... | collective-permute-start | bytes 1179656 | tf_op jit(solution)/shard_map/ppermute | solution.py:16
  132.6 13.6 %collective-permute-start.20 = (bf16[96,1536]{1,0:T(8,128)(2,1)S(1)}, bf16[96,1536]{1,0:T(8,128)(2,1)S(1)}, u32[]{:S(2)}, u32[]{:S(2)}) collective-permute-start(bf16[96,1536]{1,0:T(8,128)(2,1)S(1)} %copy-done.11), channel_id=1, source_target_pairs={{0,28},{4,24},{8,20},{12,16},{16,12},{20,8},{24,4},{28,0},{1,29},{... | collective-permute-start | bytes 884744 | tf_op jit(solution)/shard_map/ppermute | solution.py:16
  135.3 14.3 %collective-permute-start.19 = (bf16[96,1536]{1,0:T(8,128)(2,1)S(1)}, bf16[96,1536]{1,0:T(8,128)(2,1)S(1)}, u32[]{:S(2)}, u32[]{:S(2)}) collective-permute-start(bf16[96,1536]{1,0:T(8,128)(2,1)S(1)} %copy-done.9), channel_id=1, source_target_pairs={{0,24},{4,28},{8,16},{12,20},{16,8},{20,12},{24,0},{28,4},{1,25},{... | collective-permute-start | bytes 884744 | tf_op jit(solution)/shard_map/ppermute | solution.py:16
  157.3 18.0 %collective-permute-start.26 = (bf16[2,96,1536]{2,1,0:T(8,128)(2,1)S(1)}, bf16[2,96,1536]{2,1,0:T(8,128)(2,1)S(1)}, u32[]{:S(2)}, u32[]{:S(2)}) collective-permute-start(bf16[2,96,1536]{2,1,0:T(8,128)(2,1)S(1)} %shard_map.62.refs_0_), channel_id=1, source_target_pairs={{0,2},{1,3},{2,0},{3,1},{4,6},{5,7},{6,4},{7,5},{8,10},{9,11},{10,... | collective-permute-start | bytes 1769480 | tf_op jit(solution)/shard_map/ppermute | solution.py:16
  159.0 11.9 %collective-permute-start.27 = (f32[2,64,512]{2,1,0:T(8,128)S(1)}, f32[2,64,512]{2,1,0:T(8,128)S(1)}, u32[]{:S(2)}, u32[]{:S(2)}) collective-permute-start(f32[2,64,512]{2,1,0:T(8,128)S(1)} %get-tuple-element.123), channel_id=1, source_target_pairs={{0,5},{1,4},{2,7},{3,6},{4,1},{5,0},{6,3},{7,2},{8,13},{9,12},{10,... | collective-permute-start | bytes 786440 | tf_op jit(solution)/shard_map/ppermute | solution.py:276
  159.2 16.1 %collective-permute-start.23 = (f32[2,64,512]{2,1,0:T(8,128)S(1)}, f32[2,64,512]{2,1,0:T(8,128)S(1)}, u32[]{:S(2)}, u32[]{:S(2)}) collective-permute-start(f32[2,64,512]{2,1,0:T(8,128)S(1)} %get-tuple-element.116), channel_id=1, source_target_pairs={{0,4},{4,0},{8,12},{12,8},{16,20},{20,16},{24,28},{28,24},{1,5},{5... | collective-permute-start | bytes 786440 | tf_op jit(solution)/shard_map/ppermute | solution.py:16
  161.2 9.7 %collective-permute-start.25 = (bf16[32,1536]{1,0:T(8,128)(2,1)S(1)}, bf16[32,1536]{1,0:T(8,128)(2,1)S(1)}, u32[]{:S(2)}, u32[]{:S(2)}) collective-permute-start(bf16[32,1536]{1,0:T(8,128)(2,1)S(1)} %copy-done.15), channel_id=1, source_target_pairs={{0,28},{4,24},{8,20},{12,16},{16,12},{20,8},{24,4},{28,0},{1,29},{... | collective-permute-start | bytes 294920 | tf_op jit(solution)/shard_map/ppermute | solution.py:16
  175.4 12.8 %collective-permute-start.38 = (bf16[2,32,1536]{2,1,0:T(8,128)(2,1)S(1)}, bf16[2,32,1536]{2,1,0:T(8,128)(2,1)S(1)}, u32[]{:S(2)}, u32[]{:S(2)}) collective-permute-start(bf16[2,32,1536]{2,1,0:T(8,128)(2,1)S(1)} %shard_map.65.refs_0_), channel_id=1, source_target_pairs={{0,2},{1,3},{2,0},{3,1},{4,6},{5,7},{6,4},{7,5},{8,10},{9,11},{10,... | collective-permute-start | bytes 589832 | tf_op jit(solution)/shard_map/ppermute | solution.py:16
  180.3 13.5 %collective-permute-start.30 = (f32[64,512]{1,0:T(8,128)S(1)}, f32[64,512]{1,0:T(8,128)S(1)}, u32[]{:S(2)}, u32[]{:S(2)}) collective-permute-start(f32[64,512]{1,0:T(8,128)S(1)} %slice_bitcast_fusion.1), channel_id=1, source_target_pairs={{0,16},{4,20},{8,24},{12,28},{16,0},{20,4},{24,8},{28,12},{1,17},{... | collective-permute-start | bytes 393224 | tf_op jit(solution)/shard_map/ppermute | solution.py:16
  187.5 9.9 %collective-permute-start.34 = (f32[2,48,512]{2,1,0:T(8,128)S(1)}, f32[2,48,512]{2,1,0:T(8,128)S(1)}, u32[]{:S(2)}, u32[]{:S(2)}) collective-permute-start(f32[2,48,512]{2,1,0:T(8,128)S(1)} %get-tuple-element.132), channel_id=1, source_target_pairs={{0,5},{1,4},{2,7},{3,6},{4,1},{5,0},{6,3},{7,2},{8,13},{9,12},{10,... | collective-permute-start | bytes 589832 | tf_op jit(solution)/shard_map/ppermute | solution.py:276
  197.5 12.0 %collective-permute-start.35 = (f32[48,512]{1,0:T(8,128)S(1)}, f32[48,512]{1,0:T(8,128)S(1)}, u32[]{:S(2)}, u32[]{:S(2)}) collective-permute-start(f32[48,512]{1,0:T(8,128)S(1)} %get-tuple-element.147), channel_id=1, source_target_pairs={{0,8},{4,12},{8,0},{12,4},{16,24},{20,28},{24,16},{28,20},{1,9},{5... | collective-permute-start | bytes 294920 | tf_op jit(solution)/shard_map/ppermute | solution.py:16
  199.1 10.4 %collective-permute-start.37 = (f32[48,512]{1,0:T(8,128)S(1)}, f32[48,512]{1,0:T(8,128)S(1)}, u32[]{:S(2)}, u32[]{:S(2)}) collective-permute-start(f32[48,512]{1,0:T(8,128)S(1)} %get-tuple-element.148), channel_id=1, source_target_pairs={{0,24},{4,28},{8,16},{12,20},{16,8},{20,12},{24,0},{28,4},{1,25},{... | collective-permute-start | bytes 294920 | tf_op jit(solution)/shard_map/ppermute | solution.py:16
  (35 other events, 474.9 us)

commit v4 on v3

--- a/solution.py
+++ b/solution.py
@@ -16,7 +16,7 @@
     return lax.ppermute(x, axis, [(i, i ^ k) for i in range(n)])
 
 
-def params(mebibytes=8):
+def params(mebibytes=3):
     return pltpu.CompilerParams(vmem_limit_bytes=mebibytes * 1024 * 1024)
 
 
@@ -278,20 +278,24 @@
     same = (((lane * halves) ^ place) & halves) == 0
 
     class Sum:
-        def __init__(self, parts, *done):
+        def __init__(self, parts):
             self.mine, self.give = parts[:halves], parts[halves:]
-            self.got = [
-                (xor_send(after(self.mine[low], *done), "space", low), swap_send(after(self.give[low], *done), low))
-                for low in range(1, halves)
-            ]
+
+        def halve_mine(self, *done):
+            self.got = [xor_send(after(self.mine[low], *done), "space", low) for low in range(1, halves)]
+            return self
+
+        def halve_give(self, *done):
+            self.got_give = [swap_send(after(self.give[low], *done), low) for low in range(1, halves)]
+            return self
 
         def swap(self, *done):
             self.swapped = xor_send(after(self.give[0], *done), "snap", 1)
             return self
 
         def finish(self, *done):
-            own = sum([g[0] for g in self.got], self.mine[0])
-            rest = sum([g[1] for g in self.got], self.swapped)
+            own = sum(self.got, self.mine[0])
+            rest = sum(self.got_give, self.swapped)
             zero, one = jnp.where(same, own, rest), jnp.where(same, rest, own)
             total = zero[0]
             self.last = []
@@ -359,10 +363,12 @@
     groups = [(cross_nb, len(near_b), rows), (cross_low_a, len(low), rows), (cross_high_a, len(high), rows)]
     pair_a = multiply(groups, own_2, other_2, 0, where, (product, 0), rows_a, halves, members)
 
-    done = (*high_b, cross_low_bc[-1], cross_nb_bc[-1], pair_a[0])
+    sum_a = Sum(pair_a).halve_mine()
+
+    done = (*high_b, cross_low_bc[-1], cross_nb_bc[-1], pair_a[0], *sum_a.got)
     high_c = over_space(packed_c, high, *done)
     cross_high_b = across(join(high_b), *done)
-    sum_a = Sum(pair_a, *done)
+    sum_a.halve_give(*done).swap(*done)
     rows = whole_rows(rows_bc, 0, rows_bc)
     groups = [(cross_nb_bc, len(near_b), rows), (cross_low_bc, len(low), rows)]
     first_high = len(near_b) + len(low)
@@ -370,18 +376,19 @@
         groups, own_2, after(other_2, *done), 0, where, (product, rows_a), rows_bc, halves, members, False
     )
 
-    done = (*high_c, cross_high_b[-1], *[g for pair in sum_a.got for g in pair], product_bc)
+    done = (*high_c, cross_high_b[-1], *sum_a.got_give, sum_a.swapped, product_bc)
     cross_high_c = across(join(high_c), *done)
-    total_a = sum_a.swap(*done).finish()
+    total_a = sum_a.finish(*done)
     groups = [(cross_high_b, len(high), whole_rows(rows_b, 0, rows_b))]
     pair_b = multiply(groups, own_2, after(other_2, *done), first_high, where, (product_bc, 0), rows_b, halves, members)
-    sum_b = Sum(pair_b, sum_a.swapped).swap()
+    crossed = cross_high_c[-1]
+    sum_b = Sum(pair_b).halve_mine(cross_high_c[-1]).halve_give(cross_high_c[-1]).swap(cross_high_c[-1])
     groups = [(cross_high_c, len(high), whole_rows(rows_c, 0, rows_c))]
     pair_c = multiply(
-        groups, own_2, after(other_2, *sum_a.last[::2]), first_high, where, (product_bc, rows_b), rows_c, halves, members
+        groups, own_2, after(other_2, *sum_a.last[::2], sum_b.swapped), first_high, where, (product_bc, rows_b), rows_c, halves, members
     )
-    sum_c = Sum(pair_c).swap()
-    return jnp.concatenate([total_a, sum_b.finish(), sum_c.finish()], axis=0)
+    sum_c = Sum(pair_c).halve_mine().halve_give().swap()
+    return jnp.concatenate([total_a, sum_b.finish(pair_c[0]), sum_c.finish()], axis=0)
 
 
 def solution(mesh):

time: 214 us -> 212 us (level)
  waiting for transfers between devices: 95.6 us -> 88.4 us
  local copies, waits for them, and re-layouts: 9.74 us -> 12 us
    ppermute x42, waiting for transfers between devices: 93.6 us -> 88.4 us  [xor_send(): return lax.ppermute(x, axis, [(i, i ^ k) for i in range(n)])]
    unnamed x44 -> x56, local copies, waits for them, and re-layouts: 9.44 us -> 11.7 us
  transfers between devices with their start and end apart: 45 -> 45, of which waited for: 21 -> 19; matrix products, arithmetic and copies ran while one was open for 1% -> 1% of each run, Pallas kernels for 21% -> 22%
where the time goes in v4:
time: 212 us; the launch traced here: 211 us
  waiting for transfers between devices  88.4 us (42%)
  starting transfers between devices  58.2 us (27%)
  Pallas kernels  49.2 us (23%)
  local copies, waits for them, and re-layouts  12 us (6%)
  other arithmetic  2.8 us (1%)
    ppermute x42, waiting for transfers between devices, xor_send(): return lax.ppermute(x, axis, [(i, i ^ k) for i in range(n)])  88.4 us
    ppermute x42, starting transfers between devices, xor_send(): return lax.ppermute(x, axis, [(i, i ^ k) for i in range(n)])  55.1 us
    pallas_call x5, Pallas kernels, multiply(): pl.pallas_call(body, in_specs=[pl.BlockSpec(memory_space=pltpu.SMEM)] + [...  35.2 us
    unnamed x56, local copies, waits for them, and re-layouts  11.7 us
    pallas_call x8, Pallas kernels, pack(): pl.pallas_call(body, in_specs=[smem, smem, vmem], out_specs=[vmem] * len(...  8.67 us
    pallas_call x2, Pallas kernels, weigh(): pl.pallas_call(body, in_specs=[pl.BlockSpec(memory_space=pltpu.SMEM), vme...  4.46 us
  transfers between devices with their start and end apart: 45, of which 19 were waited for; matrix products, arithmetic and copies ran while one was open for 1% of the time, Pallas kernels for 22%

profile of v4, /device:TPU:0, one launch (start us, length us, event | category | flops | bytes accessed | tf_op | source)
XLA Modules:
  0.0 211.2 jit_solution(2355114635130336613)
XLA Ops:
  0.1 2.8 %copy-done = bf16[256,12288]{1,0:T(8,128)(2,1)S(1)} copy-done((bf16[256,12288]{1,0:T(8,128)(2,1)S(1)}, bf16[256,12288]{1,0:T(8,128)(2,1)}, u32[]{:S(2)}) %copy-start) | copy-done | bytes 6291480
  3.6 2.8 %shard_map.46 = (bf16[256,1536]{1,0:T(8,128)(2,1)S(1)}, bf16[256,1536]{1,0:T(8,128)(2,1)}, bf16[128,1536]{1,0:T(8,128)(2,1)S(1)}, bf16[128,1536]{1,0:T(8,128)(2,1)}, s32[96]{0:T(128)S(1)}) custom-call(s32[768]{0:T(1024)S(1)} %copy-done.10, s32[2]{0:T(128)S(1)} %pad_add_fusion.where_ref, bf16[2,128,12288]{2,1,0:T(8,128)(2,1)S(1)} %bitcast.46), custom_call_target="tpu_custom_call" | custom-call | bytes 4718592 | tf_op jit(solution)/shard_map/pallas_call | solution.py:63
  6.3 3.1 %collective-permute-start.2 = (bf16[128,1536]{1,0:T(8,128)(2,1)}, bf16[128,1536]{1,0:T(8,128)(2,1)S(1)}, u32[]{:S(2)}, u32[]{:S(2)}) collective-permute-start(bf16[128,1536]{1,0:T(8,128)(2,1)} %get-tuple-element.81), channel_id=1, source_target_pairs={{0,8},{4,12},{8,0},{12,4},{16,24},{20,28},{24,16},{28,20},{1,9},{5... | collective-permute-start | bytes 1179656 | tf_op jit(solution)/shard_map/ppermute | solution.py:16
  9.4 2.6 %collective-permute-start = (bf16[128,1536]{1,0:T(8,128)(2,1)S(1)}, bf16[128,1536]{1,0:T(8,128)(2,1)S(1)}, u32[]{:S(2)}, u32[]{:S(2)}) collective-permute-start(bf16[128,1536]{1,0:T(8,128)(2,1)S(1)} %get-tuple-element.79), channel_id=1, source_target_pairs={{0,16},{4,20},{8,24},{12,28},{16,0},{20,4},{24,8},{28,12},{1,17},{... | collective-permute-start | bytes 1179656 | tf_op jit(solution)/shard_map/ppermute | solution.py:16
  16.0 4.6 %copy-done.2 = bf16[512,12288]{1,0:T(8,128)(2,1)S(1)} copy-done((bf16[512,12288]{1,0:T(8,128)(2,1)S(1)}, bf16[512,12288]{1,0:T(8,128)(2,1)}, u32[]{:S(2)}) %copy-start.2) | copy-done | bytes 12582936
  22.4 2.7 %shard_map.48.refs_6_.refs_4_.refs_2_ = bf16[5,512,1536]{2,1,0:T(8,128)(2,1)S(1)} custom-call(s32[96]{0:T(128)S(1)} %reshape.70.table_ref, bf16[512,12288]{1,0:T(8,128)(2,1)S(1)} %copy-done.2, f32[1,12288]{1,0:T(1,128)S(1)} %bitcast.57), custom_call_target="tpu_custom_call" | custom-call | flops 3145728 | bytes 18874368 | tf_op jit(solution)/shard_map/pallas_call | solution.py:104
  27.2 3.7 %collective-permute-done.3.refs_1_ = bf16[256,1536]{1,0:T(8,128)(2,1)} collective-permute-done((bf16[256,1536]{1,0:T(8,128)(2,1)S(1)}, bf16[256,1536]{1,0:T(8,128)(2,1)}, u32[]{:S(2)}, u32[]{:S(2)}) %collective-permute-start.3) | collective-permute-done | bytes 786464 | tf_op jit(solution)/shard_map/ppermute | solution.py:16
  40.3 10.0 %collective-permute-done.5.refs_1_ = bf16[128,1536]{1,0:T(8,128)(2,1)S(1)} collective-permute-done((bf16[128,1536]{1,0:T(8,128)(2,1)S(1)}, bf16[128,1536]{1,0:T(8,128)(2,1)S(1)}, u32[]{:S(2)}, u32[]{:S(2)}) %collective-permute-start.5) | collective-permute-done | bytes 393248 | tf_op jit(solution)/shard_map/ppermute | solution.py:16
  50.5 4.1 %collective-permute-done.4.refs_1_ = bf16[128,1536]{1,0:T(8,128)(2,1)S(1)} collective-permute-done((bf16[128,1536]{1,0:T(8,128)(2,1)S(1)}, bf16[128,1536]{1,0:T(8,128)(2,1)S(1)}, u32[]{:S(2)}, u32[]{:S(2)}) %collective-permute-start.4) | collective-permute-done | bytes 393248 | tf_op jit(solution)/shard_map/ppermute | solution.py:16
  56.9 2.3 %collective-permute-start.11 = (bf16[128,1536]{1,0:T(8,128)(2,1)S(1)}, bf16[128,1536]{1,0:T(8,128)(2,1)S(1)}, u32[]{:S(2)}, u32[]{:S(2)}) collective-permute-start(bf16[128,1536]{1,0:T(8,128)(2,1)S(1)} %get-tuple-element.104), channel_id=1, source_target_pairs={{0,28},{4,24},{8,20},{12,16},{16,12},{20,8},{24,4},{28,0},{1,29},{... | collective-permute-start | bytes 1179656 | tf_op jit(solution)/shard_map/ppermute | solution.py:16
  59.2 2.5 %collective-permute-start.10 = (bf16[128,1536]{1,0:T(8,128)(2,1)S(1)}, bf16[128,1536]{1,0:T(8,128)(2,1)S(1)}, u32[]{:S(2)}, u32[]{:S(2)}) collective-permute-start(bf16[128,1536]{1,0:T(8,128)(2,1)S(1)} %get-tuple-element.102), channel_id=1, source_target_pairs={{0,24},{4,28},{8,16},{12,20},{16,8},{20,12},{24,0},{28,4},{1,25},{... | collective-permute-start | bytes 1179656 | tf_op jit(solution)/shard_map/ppermute | solution.py:16
  61.7 10.0 %collective-permute-done.11.refs_1_ = bf16[128,1536]{1,0:T(8,128)(2,1)S(1)} collective-permute-done((bf16[128,1536]{1,0:T(8,128)(2,1)S(1)}, bf16[128,1536]{1,0:T(8,128)(2,1)S(1)}, u32[]{:S(2)}, u32[]{:S(2)}) %collective-permute-start.11) | collective-permute-done | bytes 393248 | tf_op jit(solution)/shard_map/ppermute | solution.py:16
  71.7 8.4 %collective-permute-done.10.refs_0_ = bf16[128,1536]{1,0:T(8,128)(2,1)S(1)} collective-permute-done((bf16[128,1536]{1,0:T(8,128)(2,1)S(1)}, bf16[128,1536]{1,0:T(8,128)(2,1)S(1)}, u32[]{:S(2)}, u32[]{:S(2)}) %collective-permute-start.10) | collective-permute-done | bytes 393248 | tf_op jit(solution)/shard_map/ppermute | solution.py:16
  80.3 3.7 %collective-permute-done.9.refs_0_ = bf16[128,1536]{1,0:T(8,128)(2,1)S(1)} collective-permute-done((bf16[128,1536]{1,0:T(8,128)(2,1)S(1)}, bf16[128,1536]{1,0:T(8,128)(2,1)S(1)}, u32[]{:S(2)}, u32[]{:S(2)}) %collective-permute-start.9) | collective-permute-done | bytes 393248 | tf_op jit(solution)/shard_map/ppermute | solution.py:16
  84.0 5.4 %collective-permute-done.12.refs_3_ = bf16[2,128,1536]{2,1,0:T(8,128)(2,1)S(1)} collective-permute-done((bf16[2,128,1536]{2,1,0:T(8,128)(2,1)S(1)}, bf16[2,128,1536]{2,1,0:T(8,128)(2,1)S(1)}, u32[]{:S(2)}, u32[]{:S(2)}) %collective-permute-start.12) | collective-permute-done | bytes 786464 | tf_op jit(solution)/shard_map/ppermute | solution.py:16
  91.4 5.7 %collective-permute-start.19 = (bf16[128,1536]{1,0:T(8,128)(2,1)}, bf16[128,1536]{1,0:T(8,128)(2,1)S(1)}, u32[]{:S(2)}, u32[]{:S(2)}) collective-permute-start(bf16[128,1536]{1,0:T(8,128)(2,1)} %get-tuple-element.117), channel_id=1, source_target_pairs={{0,20},{4,16},{8,28},{12,24},{16,4},{20,0},{24,12},{28,8},{1,21},{... | collective-permute-start | bytes 1179656 | tf_op jit(solution)/shard_map/ppermute | solution.py:16
  99.0 10.2 %shard_map.59.refs_8_.refs_6_ = f32[2,256,1024]{2,1,0:T(8,128)} custom-call(s32[2]{0:T(128)S(1)} %pad_add_fusion.where_ref, bf16[256,1536]{1,0:T(8,128)(2,1)S(1)} %copy-done.13, bf16[256,1536]{1,0:T(8,128)(2,1)} %collective-permute-done.3.refs_1_, bf16[256,1536]{1,0:T(8,128)(2,1)} %collective-permute-done.1.refs_2_, bf16[256,1536]{1,0:T(8,128)(2,1)S(1)} %copy-done.15, ...), custom_call_target="tpu_custom_call" | custom-call | flops 4831838208 | bytes 14155776 | tf_op jit(solution)/shard_map/pallas_call | solution.py:212
  109.3 13.6 %collective-permute-done.19.refs_1_ = bf16[128,1536]{1,0:T(8,128)(2,1)S(1)} collective-permute-done((bf16[128,1536]{1,0:T(8,128)(2,1)}, bf16[128,1536]{1,0:T(8,128)(2,1)S(1)}, u32[]{:S(2)}, u32[]{:S(2)}) %collective-permute-start.19) | collective-permute-done | bytes 393248 | tf_op jit(solution)/shard_map/ppermute | solution.py:16
  122.9 7.2 %collective-permute-done.18.refs_0_ = bf16[128,1536]{1,0:T(8,128)(2,1)S(1)} collective-permute-done((bf16[128,1536]{1,0:T(8,128)(2,1)}, bf16[128,1536]{1,0:T(8,128)(2,1)S(1)}, u32[]{:S(2)}, u32[]{:S(2)}) %collective-permute-start.18) | collective-permute-done | bytes 393248 | tf_op jit(solution)/shard_map/ppermute | solution.py:16
  132.6 2.7 %collective-permute-start.21 = (bf16[96,1536]{1,0:T(8,128)(2,1)S(1)}, bf16[96,1536]{1,0:T(8,128)(2,1)S(1)}, u32[]{:S(2)}, u32[]{:S(2)}) collective-permute-start(bf16[96,1536]{1,0:T(8,128)(2,1)S(1)} %copy-done.19), channel_id=1, source_target_pairs={{0,28},{4,24},{8,20},{12,16},{16,12},{20,8},{24,4},{28,0},{1,29},{... | collective-permute-start | bytes 884744 | tf_op jit(solution)/shard_map/ppermute | solution.py:16
  135.3 1.9 collective-permute-start.20
  137.2 9.8 %shard_map.60 = (f32[2,64,512]{2,1,0:T(8,128)S(1)}, f32[2,64,512]{2,1,0:T(8,128)S(1)}, f32[2,64,512]{2,1,0:T(8,128)}, f32[2,64,512]{2,1,0:T(8,128)}) custom-call(s32[2]{0:T(128)S(1)} %pad_add_fusion.where_ref, bf16[128,1536]{1,0:T(8,128)(2,1)S(1)} %collective-permute-done.9.refs_0_, bf16[128,1536]{1,0:T(8,128)(2,1)S(1)} %collective-permute-done.14.refs_1_, ...), custom_call_target="tpu_custom_call" | custom-call | flops 4026531840 | bytes 19660800 | tf_op jit(solution)/shard_map/pallas_call | solution.py:212
  149.7 4.1 %collective-permute-done.16 = f32[2,64,512]{2,1,0:T(8,128)S(1)} collective-permute-done((f32[2,64,512]{2,1,0:T(8,128)S(1)}, f32[2,64,512]{2,1,0:T(8,128)S(1)}, u32[]{:S(2)}, u32[]{:S(2)}) %collective-permute-start.16) | collective-permute-done | bytes 262176 | tf_op jit(solution)/shard_map/ppermute | solution.py:16
  153.9 3.4 %collective-permute-done.23.refs_1_ = bf16[128,1536]{1,0:T(8,128)(2,1)S(1)} collective-permute-done((bf16[128,1536]{1,0:T(8,128)(2,1)S(1)}, bf16[128,1536]{1,0:T(8,128)(2,1)S(1)}, u32[]{:S(2)}, u32[]{:S(2)}) %collective-permute-start.23) | collective-permute-done | bytes 393248 | tf_op jit(solution)/shard_map/ppermute | solution.py:16
  159.8 2.3 %collective-permute-start.25 = (f32[2,64,512]{2,1,0:T(8,128)}, f32[2,64,512]{2,1,0:T(8,128)}, u32[]{:S(2)}, u32[]{:S(2)}) collective-permute-start(f32[2,64,512]{2,1,0:T(8,128)} %get-tuple-element.125), channel_id=1, source_target_pairs={{0,5},{1,4},{2,7},{3,6},{4,1},{5,0},{6,3},{7,2},{8,13},{9,12},{10,... | collective-permute-start | bytes 786440 | tf_op jit(solution)/shard_map/ppermute | solution.py:276
  162.3 2.9 %collective-permute-start.26 = (bf16[32,1536]{1,0:T(8,128)(2,1)S(1)}, bf16[32,1536]{1,0:T(8,128)(2,1)S(1)}, u32[]{:S(2)}, u32[]{:S(2)}) collective-permute-start(bf16[32,1536]{1,0:T(8,128)(2,1)S(1)} %get-tuple-element.126), channel_id=1, source_target_pairs={{0,24},{4,28},{8,16},{12,20},{16,8},{20,12},{24,0},{28,4},{1,25},{... | collective-permute-start | bytes 294920 | tf_op jit(solution)/shard_map/ppermute | solution.py:16
  166.2 6.4 %shard_map.63.refs_4_ = f32[2,128,1024]{2,1,0:T(8,128)S(1)} custom-call(s32[2]{0:T(128)S(1)} %pad_add_fusion.where_ref, bf16[128,1536]{1,0:T(8,128)(2,1)S(1)} %collective-permute-done.17.refs_0_, bf16[128,1536]{1,0:T(8,128)(2,1)S(1)} %copy-done.6, bf16[2,128,1536]{2,1,0:T(8,128)(2,1)S(1)} %shard_map.61.refs_2_, ...), custom_call_target="tpu_custom_call" | custom-call | flops 2415919104 | bytes 11796480 | tf_op jit(solution)/shard_map/pallas_call | solution.py:212
  174.5 2.4 %collective-permute-start.30 = (f32[64,512]{1,0:T(8,128)S(1)}, f32[64,512]{1,0:T(8,128)S(1)}, u32[]{:S(2)}, u32[]{:S(2)}) collective-permute-start(f32[64,512]{1,0:T(8,128)S(1)} %get-tuple-element.132), channel_id=1, source_target_pairs={{0,16},{4,20},{8,24},{12,28},{16,0},{20,4},{24,8},{28,12},{1,17},{... | collective-permute-start | bytes 393224 | tf_op jit(solution)/shard_map/ppermute | solution.py:16
  178.4 4.5 %shard_map.64 = (f32[2,48,512]{2,1,0:T(8,128)S(1)}, f32[2,48,512]{2,1,0:T(8,128)S(1)}, f32[2,48,512]{2,1,0:T(8,128)S(1)}, f32[2,48,512]{2,1,0:T(8,128)S(1)}) custom-call(s32[2]{0:T(128)S(1)} %pad_add_fusion.where_ref, bf16[2,96,1536]{2,1,0:T(8,128)(2,1)S(1)} %shard_map.62.refs_0_, bf16[2,96,1536]{2,1,0:T(8,128)(2,1)S(1)} %collective-permute-done.28.refs_1_, ...), custom_call_target="tpu_custom_call" | custom-call | flops 1207959552 | bytes 7471104 | tf_op jit(solution)/shard_map/pallas_call | solution.py:212
  187.8 4.2 %shard_map.66 = (f32[2,16,512]{2,1,0:T(8,128)S(1)}, f32[2,16,512]{2,1,0:T(8,128)S(1)}, f32[2,16,512]{2,1,0:T(8,128)S(1)}, f32[2,16,512]{2,1,0:T(8,128)S(1)}) custom-call(s32[2]{0:T(128)S(1)} %pad_add_fusion.where_ref, bf16[2,32,1536]{2,1,0:T(8,128)(2,1)S(1)} %shard_map.65.refs_0_, bf16[2,32,1536]{2,1,0:T(8,128)(2,1)S(1)} %collective-permute-done.32.refs_1_, ...), custom_call_target="tpu_custom_call" | custom-call | flops 402653184 | bytes 6684672 | tf_op jit(solution)/shard_map/pallas_call | solution.py:212
  202.4 5.2 %collective-permute-done.37 = f32[48,512]{1,0:T(8,128)S(1)} collective-permute-done((f32[48,512]{1,0:T(8,128)S(1)}, f32[48,512]{1,0:T(8,128)S(1)}, u32[]{:S(2)}, u32[]{:S(2)}) %collective-permute-start.37) | collective-permute-done | bytes 98336 | tf_op jit(solution)/shard_map/ppermute | solution.py:16
  207.7 2.8 %collective-permute-done.43 = f32[16,512]{1,0:T(8,128)S(1)} collective-permute-done((f32[16,512]{1,0:T(8,128)S(1)}, f32[16,512]{1,0:T(8,128)S(1)}, u32[]{:S(2)}, u32[]{:S(2)}) %collective-permute-start.43) | collective-permute-done | bytes 32800 | tf_op jit(solution)/shard_map/ppermute | solution.py:16
  (159 shorter events, 52.5 us)
Async XLA Ops:
  6.3 20.8 %collective-permute-start.2 = (bf16[128,1536]{1,0:T(8,128)(2,1)}, bf16[128,1536]{1,0:T(8,128)(2,1)S(1)}, u32[]{:S(2)}, u32[]{:S(2)}) collective-permute-start(bf16[128,1536]{1,0:T(8,128)(2,1)} %get-tuple-element.81), channel_id=1, source_target_pairs={{0,8},{4,12},{8,0},{12,4},{16,24},{20,28},{24,16},{28,20},{1,9},{5... | collective-permute-start | bytes 1179656 | tf_op jit(solution)/shard_map/ppermute | solution.py:16
  9.4 17.8 %collective-permute-start = (bf16[128,1536]{1,0:T(8,128)(2,1)S(1)}, bf16[128,1536]{1,0:T(8,128)(2,1)S(1)}, u32[]{:S(2)}, u32[]{:S(2)}) collective-permute-start(bf16[128,1536]{1,0:T(8,128)(2,1)S(1)} %get-tuple-element.79), channel_id=1, source_target_pairs={{0,16},{4,20},{8,24},{12,28},{16,0},{20,4},{24,8},{28,12},{1,17},{... | collective-permute-start | bytes 1179656 | tf_op jit(solution)/shard_map/ppermute | solution.py:16
  12.0 18.8 %collective-permute-start.3 = (bf16[256,1536]{1,0:T(8,128)(2,1)S(1)}, bf16[256,1536]{1,0:T(8,128)(2,1)}, u32[]{:S(2)}, u32[]{:S(2)}) collective-permute-start(bf16[256,1536]{1,0:T(8,128)(2,1)S(1)} %get-tuple-element.82.refs_0_), channel_id=1, source_target_pairs={{0,2},{1,3},{2,0},{3,1},{4,6},{5,7},{6,4},{7,5},{8,10},{9,11},{10,... | collective-permute-start | bytes 2359304 | tf_op jit(solution)/shard_map/ppermute | solution.py:16
  13.5 18.8 %collective-permute-start.1 = (bf16[256,1536]{1,0:T(8,128)(2,1)}, bf16[256,1536]{1,0:T(8,128)(2,1)}, u32[]{:S(2)}, u32[]{:S(2)}) collective-permute-start(bf16[256,1536]{1,0:T(8,128)(2,1)} %get-tuple-element.80), channel_id=1, source_target_pairs={{0,4},{4,0},{8,12},{12,8},{16,20},{20,16},{24,28},{28,24},{1,5},{5... | collective-permute-start | bytes 2359304 | tf_op jit(solution)/shard_map/ppermute | solution.py:16
  32.3 22.5 %collective-permute-start.8 = (bf16[5,512,1536]{2,1,0:T(8,128)(2,1)S(1)}, bf16[5,512,1536]{2,1,0:T(8,128)(2,1)S(1)}, u32[]{:S(2)}, u32[]{:S(2)}) collective-permute-start(bf16[5,512,1536]{2,1,0:T(8,128)(2,1)S(1)} %shard_map.48.refs_6_.refs_4_.refs_2_), channel_id=1, source_target_pairs={{0,1},{1,0},{2,3},{3,2},{4,5},{5,4},{6,7},{7,6},{8,9},{9,8},{10,11... | collective-permute-start | bytes 23592968 | tf_op jit(solution)/shard_map/ppermute | solution.py:16
  32.3 22.5 %collective-permute-start.7 = (bf16[3,512,1536]{2,1,0:T(8,128)(2,1)S(1)}, bf16[3,512,1536]{2,1,0:T(8,128)(2,1)S(1)}, u32[]{:S(2)}, u32[]{:S(2)}) collective-permute-start(bf16[3,512,1536]{2,1,0:T(8,128)(2,1)S(1)} %shard_map.47.refs_6_), channel_id=1, source_target_pairs={{0,1},{1,0},{2,3},{3,2},{4,5},{5,4},{6,7},{7,6},{8,9},{9,8},{10,11... | collective-permute-start | bytes 14155784 | tf_op jit(solution)/shard_map/ppermute | solution.py:16
  32.8 21.9 %collective-permute-start.6 = (bf16[256,1536]{1,0:T(8,128)(2,1)}, bf16[256,1536]{1,0:T(8,128)(2,1)S(1)}, u32[]{:S(2)}, u32[]{:S(2)}) collective-permute-start(bf16[256,1536]{1,0:T(8,128)(2,1)} %collective-permute-done.1.refs_2_), channel_id=1, source_target_pairs={{0,2},{1,3},{2,0},{3,1},{4,6},{5,7},{6,4},{7,5},{8,10},{9,11},{10,... | collective-permute-start | bytes 2359304 | tf_op jit(solution)/shard_map/ppermute | solution.py:16
  33.3 17.0 %collective-permute-start.5 = (bf16[128,1536]{1,0:T(8,128)(2,1)S(1)}, bf16[128,1536]{1,0:T(8,128)(2,1)S(1)}, u32[]{:S(2)}, u32[]{:S(2)}) collective-permute-start(bf16[128,1536]{1,0:T(8,128)(2,1)S(1)} %shard_map.50), channel_id=1, source_target_pairs={{0,8},{4,12},{8,0},{12,4},{16,24},{20,28},{24,16},{28,20},{1,9},{5... | collective-permute-start | bytes 1179656 | tf_op jit(solution)/shard_map/ppermute | solution.py:16
  33.8 20.8 %collective-permute-start.4 = (bf16[128,1536]{1,0:T(8,128)(2,1)S(1)}, bf16[128,1536]{1,0:T(8,128)(2,1)S(1)}, u32[]{:S(2)}, u32[]{:S(2)}) collective-permute-start(bf16[128,1536]{1,0:T(8,128)(2,1)S(1)} %shard_map.49), channel_id=1, source_target_pairs={{0,20},{4,16},{8,28},{12,24},{16,4},{20,0},{24,12},{28,8},{1,21},{... | collective-permute-start | bytes 1179656 | tf_op jit(solution)/shard_map/ppermute | solution.py:16
  54.8 29.2 %collective-permute-start.13 = (bf16[2,128,1536]{2,1,0:T(8,128)(2,1)S(1)}, bf16[2,128,1536]{2,1,0:T(8,128)(2,1)S(1)}, u32[]{:S(2)}, u32[]{:S(2)}) collective-permute-start(bf16[2,128,1536]{2,1,0:T(8,128)(2,1)S(1)} %shard_map.57.refs_4_), channel_id=1, source_target_pairs={{0,2},{1,3},{2,0},{3,1},{4,6},{5,7},{6,4},{7,5},{8,10},{9,11},{10,... | collective-permute-start | bytes 2359304 | tf_op jit(solution)/shard_map/ppermute | solution.py:16
  56.3 33.1 %collective-permute-start.12 = (bf16[2,128,1536]{2,1,0:T(8,128)(2,1)S(1)}, bf16[2,128,1536]{2,1,0:T(8,128)(2,1)S(1)}, u32[]{:S(2)}, u32[]{:S(2)}) collective-permute-start(bf16[2,128,1536]{2,1,0:T(8,128)(2,1)S(1)} %shard_map.56.refs_2_), channel_id=1, source_target_pairs={{0,2},{1,3},{2,0},{3,1},{4,6},{5,7},{6,4},{7,5},{8,10},{9,11},{10,... | collective-permute-start | bytes 2359304 | tf_op jit(solution)/shard_map/ppermute | solution.py:16
  56.9 14.8 %collective-permute-start.11 = (bf16[128,1536]{1,0:T(8,128)(2,1)S(1)}, bf16[128,1536]{1,0:T(8,128)(2,1)S(1)}, u32[]{:S(2)}, u32[]{:S(2)}) collective-permute-start(bf16[128,1536]{1,0:T(8,128)(2,1)S(1)} %get-tuple-element.104), channel_id=1, source_target_pairs={{0,28},{4,24},{8,20},{12,16},{16,12},{20,8},{24,4},{28,0},{1,29},{... | collective-permute-start | bytes 1179656 | tf_op jit(solution)/shard_map/ppermute | solution.py:16
  59.2 20.9 %collective-permute-start.10 = (bf16[128,1536]{1,0:T(8,128)(2,1)S(1)}, bf16[128,1536]{1,0:T(8,128)(2,1)S(1)}, u32[]{:S(2)}, u32[]{:S(2)}) collective-permute-start(bf16[128,1536]{1,0:T(8,128)(2,1)S(1)} %get-tuple-element.102), channel_id=1, source_target_pairs={{0,24},{4,28},{8,16},{12,20},{16,8},{20,12},{24,0},{28,4},{1,25},{... | collective-permute-start | bytes 1179656 | tf_op jit(solution)/shard_map/ppermute | solution.py:16
  61.6 22.3 %collective-permute-start.9 = (bf16[128,1536]{1,0:T(8,128)(2,1)S(1)}, bf16[128,1536]{1,0:T(8,128)(2,1)S(1)}, u32[]{:S(2)}, u32[]{:S(2)}) collective-permute-start(bf16[128,1536]{1,0:T(8,128)(2,1)S(1)} %shard_map.51), channel_id=1, source_target_pairs={{0,12},{4,8},{8,4},{12,0},{16,28},{20,24},{24,20},{28,16},{1,13},{... | collective-permute-start | bytes 1179656 | tf_op jit(solution)/shard_map/ppermute | solution.py:16
  89.4 41.1 %collective-permute-start.15 = (bf16[2,128,1536]{2,1,0:T(8,128)(2,1)S(1)}, bf16[2,128,1536]{2,1,0:T(8,128)(2,1)S(1)}, u32[]{:S(2)}, u32[]{:S(2)}) collective-permute-start(bf16[2,128,1536]{2,1,0:T(8,128)(2,1)S(1)} %shard_map.58.refs_4_), channel_id=1, source_target_pairs={{0,2},{1,3},{2,0},{3,1},{4,6},{5,7},{6,4},{7,5},{8,10},{9,11},{10,... | collective-permute-start | bytes 2359304 | tf_op jit(solution)/shard_map/ppermute | solution.py:16
  90.1 40.4 %collective-permute-start.14 = (bf16[128,1536]{1,0:T(8,128)(2,1)S(1)}, bf16[128,1536]{1,0:T(8,128)(2,1)S(1)}, u32[]{:S(2)}, u32[]{:S(2)}) collective-permute-start(bf16[128,1536]{1,0:T(8,128)(2,1)S(1)} %collective-permute-done.9.refs_0_), channel_id=1, source_target_pairs={{0,2},{1,3},{2,0},{3,1},{4,6},{5,7},{6,4},{7,5},{8,10},{9,11},{10,... | collective-permute-start | bytes 1179656 | tf_op jit(solution)/shard_map/ppermute | solution.py:16
  91.4 31.5 %collective-permute-start.19 = (bf16[128,1536]{1,0:T(8,128)(2,1)}, bf16[128,1536]{1,0:T(8,128)(2,1)S(1)}, u32[]{:S(2)}, u32[]{:S(2)}) collective-permute-start(bf16[128,1536]{1,0:T(8,128)(2,1)} %get-tuple-element.117), channel_id=1, source_target_pairs={{0,20},{4,16},{8,28},{12,24},{16,4},{20,0},{24,12},{28,8},{1,21},{... | collective-permute-start | bytes 1179656 | tf_op jit(solution)/shard_map/ppermute | solution.py:16
  97.1 33.0 %collective-permute-start.18 = (bf16[128,1536]{1,0:T(8,128)(2,1)}, bf16[128,1536]{1,0:T(8,128)(2,1)S(1)}, u32[]{:S(2)}, u32[]{:S(2)}) collective-permute-start(bf16[128,1536]{1,0:T(8,128)(2,1)} %get-tuple-element.115), channel_id=1, source_target_pairs={{0,16},{4,20},{8,24},{12,28},{16,0},{20,4},{24,8},{28,12},{1,17},{... | collective-permute-start | bytes 1179656 | tf_op jit(solution)/shard_map/ppermute | solution.py:16
  97.1 33.3 %collective-permute-start.17 = (bf16[128,1536]{1,0:T(8,128)(2,1)}, bf16[128,1536]{1,0:T(8,128)(2,1)S(1)}, u32[]{:S(2)}, u32[]{:S(2)}) collective-permute-start(bf16[128,1536]{1,0:T(8,128)(2,1)} %get-tuple-element.114), channel_id=1, source_target_pairs={{0,12},{4,8},{8,4},{12,0},{16,28},{20,24},{24,20},{28,16},{1,13},{... | collective-permute-start | bytes 1179656 | tf_op jit(solution)/shard_map/ppermute | solution.py:16
  130.5 27.5 %collective-permute-start.22 = (bf16[2,128,1536]{2,1,0:T(8,128)(2,1)S(1)}, bf16[2,128,1536]{2,1,0:T(8,128)(2,1)S(1)}, u32[]{:S(2)}, u32[]{:S(2)}) collective-permute-start(bf16[2,128,1536]{2,1,0:T(8,128)(2,1)S(1)} %shard_map.61.refs_2_), channel_id=1, source_target_pairs={{0,2},{1,3},{2,0},{3,1},{4,6},{5,7},{6,4},{7,5},{8,10},{9,11},{10,... | collective-permute-start | bytes 2359304 | tf_op jit(solution)/shard_map/ppermute | solution.py:16
  132.2 25.0 %collective-permute-start.23 = (bf16[128,1536]{1,0:T(8,128)(2,1)S(1)}, bf16[128,1536]{1,0:T(8,128)(2,1)S(1)}, u32[]{:S(2)}, u32[]{:S(2)}) collective-permute-start(bf16[128,1536]{1,0:T(8,128)(2,1)S(1)} %collective-permute-done.17.refs_0_), channel_id=1, source_target_pairs={{0,2},{1,3},{2,0},{3,1},{4,6},{5,7},{6,4},{7,5},{8,10},{9,11},{10,... | collective-permute-start | bytes 1179656 | tf_op jit(solution)/shard_map/ppermute | solution.py:16
  132.6 15.2 %collective-permute-start.21 = (bf16[96,1536]{1,0:T(8,128)(2,1)S(1)}, bf16[96,1536]{1,0:T(8,128)(2,1)S(1)}, u32[]{:S(2)}, u32[]{:S(2)}) collective-permute-start(bf16[96,1536]{1,0:T(8,128)(2,1)S(1)} %copy-done.19), channel_id=1, source_target_pairs={{0,28},{4,24},{8,20},{12,16},{16,12},{20,8},{24,4},{28,0},{1,29},{... | collective-permute-start | bytes 884744 | tf_op jit(solution)/shard_map/ppermute | solution.py:16
  135.3 14.3 %collective-permute-start.20 = (bf16[96,1536]{1,0:T(8,128)(2,1)S(1)}, bf16[96,1536]{1,0:T(8,128)(2,1)S(1)}, u32[]{:S(2)}, u32[]{:S(2)}) collective-permute-start(bf16[96,1536]{1,0:T(8,128)(2,1)S(1)} %copy-done.17), channel_id=1, source_target_pairs={{0,24},{4,28},{8,16},{12,20},{16,8},{20,12},{24,0},{28,4},{1,25},{... | collective-permute-start | bytes 884744 | tf_op jit(solution)/shard_map/ppermute | solution.py:16
  158.0 16.0 %collective-permute-start.28 = (bf16[2,96,1536]{2,1,0:T(8,128)(2,1)S(1)}, bf16[2,96,1536]{2,1,0:T(8,128)(2,1)S(1)}, u32[]{:S(2)}, u32[]{:S(2)}) collective-permute-start(bf16[2,96,1536]{2,1,0:T(8,128)(2,1)S(1)} %shard_map.62.refs_0_), channel_id=1, source_target_pairs={{0,2},{1,3},{2,0},{3,1},{4,6},{5,7},{6,4},{7,5},{8,10},{9,11},{10,... | collective-permute-start | bytes 1769480 | tf_op jit(solution)/shard_map/ppermute | solution.py:16
  159.8 13.0 %collective-permute-start.24 = (f32[2,64,512]{2,1,0:T(8,128)}, f32[2,64,512]{2,1,0:T(8,128)}, u32[]{:S(2)}, u32[]{:S(2)}) collective-permute-start(f32[2,64,512]{2,1,0:T(8,128)} %get-tuple-element.123), channel_id=1, source_target_pairs={{0,1},{1,0},{2,3},{3,2},{4,5},{5,4},{6,7},{7,6},{8,9},{9,8},{10,11... | collective-permute-start | bytes 786440 | tf_op jit(solution)/shard_map/ppermute | solution.py:16
  159.8 13.0 %collective-permute-start.25 = (f32[2,64,512]{2,1,0:T(8,128)}, f32[2,64,512]{2,1,0:T(8,128)}, u32[]{:S(2)}, u32[]{:S(2)}) collective-permute-start(f32[2,64,512]{2,1,0:T(8,128)} %get-tuple-element.125), channel_id=1, source_target_pairs={{0,5},{1,4},{2,7},{3,6},{4,1},{5,0},{6,3},{7,2},{8,13},{9,12},{10,... | collective-permute-start | bytes 786440 | tf_op jit(solution)/shard_map/ppermute | solution.py:276
  162.1 10.6 %collective-permute-start.27 = (bf16[32,1536]{1,0:T(8,128)(2,1)S(1)}, bf16[32,1536]{1,0:T(8,128)(2,1)S(1)}, u32[]{:S(2)}, u32[]{:S(2)}) collective-permute-start(bf16[32,1536]{1,0:T(8,128)(2,1)S(1)} %get-tuple-element.128), channel_id=1, source_target_pairs={{0,28},{4,24},{8,20},{12,16},{16,12},{20,8},{24,4},{28,0},{1,29},{... | collective-permute-start | bytes 294920 | tf_op jit(solution)/shard_map/ppermute | solution.py:16
  162.3 10.4 %collective-permute-start.26 = (bf16[32,1536]{1,0:T(8,128)(2,1)S(1)}, bf16[32,1536]{1,0:T(8,128)(2,1)S(1)}, u32[]{:S(2)}, u32[]{:S(2)}) collective-permute-start(bf16[32,1536]{1,0:T(8,128)(2,1)S(1)} %get-tuple-element.126), channel_id=1, source_target_pairs={{0,24},{4,28},{8,16},{12,20},{16,8},{20,12},{24,0},{28,4},{1,25},{... | collective-permute-start | bytes 294920 | tf_op jit(solution)/shard_map/ppermute | solution.py:16
  174.5 11.9 %collective-permute-start.30 = (f32[64,512]{1,0:T(8,128)S(1)}, f32[64,512]{1,0:T(8,128)S(1)}, u32[]{:S(2)}, u32[]{:S(2)}) collective-permute-start(f32[64,512]{1,0:T(8,128)S(1)} %get-tuple-element.132), channel_id=1, source_target_pairs={{0,16},{4,20},{8,24},{12,28},{16,0},{20,4},{24,8},{28,12},{1,17},{... | collective-permute-start | bytes 393224 | tf_op jit(solution)/shard_map/ppermute | solution.py:16
  182.9 11.3 %collective-permute-start.33 = (f32[2,48,512]{2,1,0:T(8,128)S(1)}, f32[2,48,512]{2,1,0:T(8,128)S(1)}, u32[]{:S(2)}, u32[]{:S(2)}) collective-permute-start(f32[2,48,512]{2,1,0:T(8,128)S(1)} %get-tuple-element.138), channel_id=1, source_target_pairs={{0,4},{4,0},{8,12},{12,8},{16,20},{20,16},{24,28},{28,24},{1,5},{5... | collective-permute-start | bytes 589832 | tf_op jit(solution)/shard_map/ppermute | solution.py:16
  196.2 11.5 %collective-permute-start.37 = (f32[48,512]{1,0:T(8,128)S(1)}, f32[48,512]{1,0:T(8,128)S(1)}, u32[]{:S(2)}, u32[]{:S(2)}) collective-permute-start(f32[48,512]{1,0:T(8,128)S(1)} %get-tuple-element.146), channel_id=1, source_target_pairs={{0,16},{4,20},{8,24},{12,28},{16,0},{20,4},{24,8},{28,12},{1,17},{... | collective-permute-start | bytes 294920 | tf_op jit(solution)/shard_map/ppermute | solution.py:16
  197.3 10.4 %collective-permute-start.38 = (f32[48,512]{1,0:T(8,128)S(1)}, f32[48,512]{1,0:T(8,128)S(1)}, u32[]{:S(2)}, u32[]{:S(2)}) collective-permute-start(f32[48,512]{1,0:T(8,128)S(1)} %get-tuple-element.147), channel_id=1, source_target_pairs={{0,24},{4,28},{8,16},{12,20},{16,8},{20,12},{24,0},{28,4},{1,25},{... | collective-permute-start | bytes 294920 | tf_op jit(solution)/shard_map/ppermute | solution.py:16
  (41 other events, 508.5 us)

commit v5 on v4

--- a/solution.py
+++ b/solution.py
@@ -316,15 +316,15 @@
         adjoint, (0, rows_out, [0, 1]), (0, rows_a, start_low), (0, rows_a, near_a)
     )
     low_a = over_space(packed_a, start_low)
+    got_na = over_space(packed_na, near_a)
     near_1 = over_space(packed_n, [1])[0]
-    got_na = over_space(packed_na, near_a)
     cross_0 = across(packed_n[0])
     own_1 = weigh(after(primal, packed_na[near_a[0]]), weights, table, 0, early, tiles)
     own_2 = weigh(after(primal, own_1), weights, table, early, tiles - early, tiles)
     packed_ar = pack_rows(after(adjoint, own_2), (0, rows_a, rest_low))
     packed_nr = pack_rows(after(adjoint, packed_ar[rest_low[0]]), (rows_a, rows_bc, near_a))
 
-    done = (*low_a, near_1, *got_na, cross_0[-1], packed_nr[near_a[0]])
+    done = (*got_na, *low_a, near_1, cross_0[-1], packed_nr[near_a[0]])
     low_a = low_a + over_space(packed_ar, rest_low, *done)
     got_na = got_na + over_space(packed_nr, near_a, *done)
     cross_1 = across(near_1, *done)

time: 212 us -> 212 us (level)
  no operation moved by 1% of the time
where the time goes in v5:
time: 212 us; the launch traced here: 211 us
  waiting for transfers between devices  88.4 us (42%)
  starting transfers between devices  58.2 us (27%)
  Pallas kernels  49.3 us (23%)
  local copies, waits for them, and re-layouts  12 us (6%)
  other arithmetic  2.8 us (1%)
    ppermute x42, waiting for transfers between devices, xor_send(): return lax.ppermute(x, axis, [(i, i ^ k) for i in range(n)])  88.4 us
    ppermute x42, starting transfers between devices, xor_send(): return lax.ppermute(x, axis, [(i, i ^ k) for i in range(n)])  55.1 us
    pallas_call x5, Pallas kernels, multiply(): pl.pallas_call(body, in_specs=[pl.BlockSpec(memory_space=pltpu.SMEM)] + [...  35.2 us
    unnamed x56, local copies, waits for them, and re-layouts  11.7 us
    pallas_call x8, Pallas kernels, pack(): pl.pallas_call(body, in_specs=[smem, smem, vmem], out_specs=[vmem] * len(...  8.67 us
    pallas_call x2, Pallas kernels, weigh(): pl.pallas_call(body, in_specs=[pl.BlockSpec(memory_space=pltpu.SMEM), vme...  4.49 us
  transfers between devices with their start and end apart: 45, of which 19 were waited for; matrix products, arithmetic and copies ran while one was open for 1% of the time, Pallas kernels for 22%

profile of v5, /device:TPU:0, one launch (start us, length us, event | category | flops | bytes accessed | tf_op | source)
XLA Modules:
  0.0 211.2 jit_solution(2355114635130336613)
XLA Ops:
  0.1 2.8 %copy-done = bf16[256,12288]{1,0:T(8,128)(2,1)S(1)} copy-done((bf16[256,12288]{1,0:T(8,128)(2,1)S(1)}, bf16[256,12288]{1,0:T(8,128)(2,1)}, u32[]{:S(2)}) %copy-start) | copy-done | bytes 6291480
  3.6 2.8 %shard_map.46 = (bf16[256,1536]{1,0:T(8,128)(2,1)S(1)}, bf16[256,1536]{1,0:T(8,128)(2,1)}, bf16[128,1536]{1,0:T(8,128)(2,1)S(1)}, bf16[128,1536]{1,0:T(8,128)(2,1)}, s32[96]{0:T(128)S(1)}) custom-call(s32[768]{0:T(1024)S(1)} %copy-done.10, s32[2]{0:T(128)S(1)} %pad_add_fusion.where_ref, bf16[2,128,12288]{2,1,0:T(8,128)(2,1)S(1)} %bitcast.46), custom_call_target="tpu_custom_call" | custom-call | bytes 4718592 | tf_op jit(solution)/shard_map/pallas_call | solution.py:63
  6.3 3.1 %collective-permute-start = (bf16[128,1536]{1,0:T(8,128)(2,1)}, bf16[128,1536]{1,0:T(8,128)(2,1)S(1)}, u32[]{:S(2)}, u32[]{:S(2)}) collective-permute-start(bf16[128,1536]{1,0:T(8,128)(2,1)} %get-tuple-element.79), channel_id=1, source_target_pairs={{0,8},{4,12},{8,0},{12,4},{16,24},{20,28},{24,16},{28,20},{1,9},{5... | collective-permute-start | bytes 1179656 | tf_op jit(solution)/shard_map/ppermute | solution.py:16
  9.4 2.6 %collective-permute-start.1 = (bf16[128,1536]{1,0:T(8,128)(2,1)S(1)}, bf16[128,1536]{1,0:T(8,128)(2,1)S(1)}, u32[]{:S(2)}, u32[]{:S(2)}) collective-permute-start(bf16[128,1536]{1,0:T(8,128)(2,1)S(1)} %get-tuple-element.80), channel_id=1, source_target_pairs={{0,16},{4,20},{8,24},{12,28},{16,0},{20,4},{24,8},{28,12},{1,17},{... | collective-permute-start | bytes 1179656 | tf_op jit(solution)/shard_map/ppermute | solution.py:16
  16.0 4.6 %copy-done.2 = bf16[512,12288]{1,0:T(8,128)(2,1)S(1)} copy-done((bf16[512,12288]{1,0:T(8,128)(2,1)S(1)}, bf16[512,12288]{1,0:T(8,128)(2,1)}, u32[]{:S(2)}) %copy-start.2) | copy-done | bytes 12582936
  22.4 2.7 %shard_map.48.refs_6_.refs_4_.refs_2_ = bf16[5,512,1536]{2,1,0:T(8,128)(2,1)S(1)} custom-call(s32[96]{0:T(128)S(1)} %reshape.70.table_ref, bf16[512,12288]{1,0:T(8,128)(2,1)S(1)} %copy-done.2, f32[1,12288]{1,0:T(1,128)S(1)} %bitcast.57), custom_call_target="tpu_custom_call" | custom-call | flops 3145728 | bytes 18874368 | tf_op jit(solution)/shard_map/pallas_call | solution.py:104
  27.2 3.7 %collective-permute-done.3.refs_1_ = bf16[256,1536]{1,0:T(8,128)(2,1)} collective-permute-done((bf16[256,1536]{1,0:T(8,128)(2,1)S(1)}, bf16[256,1536]{1,0:T(8,128)(2,1)}, u32[]{:S(2)}, u32[]{:S(2)}) %collective-permute-start.3) | collective-permute-done | bytes 786464 | tf_op jit(solution)/shard_map/ppermute | solution.py:16
  40.3 10.0 %collective-permute-done.5.refs_1_ = bf16[128,1536]{1,0:T(8,128)(2,1)S(1)} collective-permute-done((bf16[128,1536]{1,0:T(8,128)(2,1)S(1)}, bf16[128,1536]{1,0:T(8,128)(2,1)S(1)}, u32[]{:S(2)}, u32[]{:S(2)}) %collective-permute-start.5) | collective-permute-done | bytes 393248 | tf_op jit(solution)/shard_map/ppermute | solution.py:16
  50.5 4.1 %collective-permute-done.4.refs_1_ = bf16[128,1536]{1,0:T(8,128)(2,1)S(1)} collective-permute-done((bf16[128,1536]{1,0:T(8,128)(2,1)S(1)}, bf16[128,1536]{1,0:T(8,128)(2,1)S(1)}, u32[]{:S(2)}, u32[]{:S(2)}) %collective-permute-start.4) | collective-permute-done | bytes 393248 | tf_op jit(solution)/shard_map/ppermute | solution.py:16
  56.9 2.3 %collective-permute-start.11 = (bf16[128,1536]{1,0:T(8,128)(2,1)S(1)}, bf16[128,1536]{1,0:T(8,128)(2,1)S(1)}, u32[]{:S(2)}, u32[]{:S(2)}) collective-permute-start(bf16[128,1536]{1,0:T(8,128)(2,1)S(1)} %get-tuple-element.104), channel_id=1, source_target_pairs={{0,28},{4,24},{8,20},{12,16},{16,12},{20,8},{24,4},{28,0},{1,29},{... | collective-permute-start | bytes 1179656 | tf_op jit(solution)/shard_map/ppermute | solution.py:16
  59.2 2.5 %collective-permute-start.10 = (bf16[128,1536]{1,0:T(8,128)(2,1)S(1)}, bf16[128,1536]{1,0:T(8,128)(2,1)S(1)}, u32[]{:S(2)}, u32[]{:S(2)}) collective-permute-start(bf16[128,1536]{1,0:T(8,128)(2,1)S(1)} %get-tuple-element.102), channel_id=1, source_target_pairs={{0,24},{4,28},{8,16},{12,20},{16,8},{20,12},{24,0},{28,4},{1,25},{... | collective-permute-start | bytes 1179656 | tf_op jit(solution)/shard_map/ppermute | solution.py:16
  61.7 10.0 %collective-permute-done.11.refs_1_ = bf16[128,1536]{1,0:T(8,128)(2,1)S(1)} collective-permute-done((bf16[128,1536]{1,0:T(8,128)(2,1)S(1)}, bf16[128,1536]{1,0:T(8,128)(2,1)S(1)}, u32[]{:S(2)}, u32[]{:S(2)}) %collective-permute-start.11) | collective-permute-done | bytes 393248 | tf_op jit(solution)/shard_map/ppermute | solution.py:16
  71.7 8.5 %collective-permute-done.10.refs_0_ = bf16[128,1536]{1,0:T(8,128)(2,1)S(1)} collective-permute-done((bf16[128,1536]{1,0:T(8,128)(2,1)S(1)}, bf16[128,1536]{1,0:T(8,128)(2,1)S(1)}, u32[]{:S(2)}, u32[]{:S(2)}) %collective-permute-start.10) | collective-permute-done | bytes 393248 | tf_op jit(solution)/shard_map/ppermute | solution.py:16
  80.3 3.7 %collective-permute-done.9.refs_0_ = bf16[128,1536]{1,0:T(8,128)(2,1)S(1)} collective-permute-done((bf16[128,1536]{1,0:T(8,128)(2,1)S(1)}, bf16[128,1536]{1,0:T(8,128)(2,1)S(1)}, u32[]{:S(2)}, u32[]{:S(2)}) %collective-permute-start.9) | collective-permute-done | bytes 393248 | tf_op jit(solution)/shard_map/ppermute | solution.py:16
  84.0 5.4 %collective-permute-done.12.refs_3_ = bf16[2,128,1536]{2,1,0:T(8,128)(2,1)S(1)} collective-permute-done((bf16[2,128,1536]{2,1,0:T(8,128)(2,1)S(1)}, bf16[2,128,1536]{2,1,0:T(8,128)(2,1)S(1)}, u32[]{:S(2)}, u32[]{:S(2)}) %collective-permute-start.12) | collective-permute-done | bytes 786464 | tf_op jit(solution)/shard_map/ppermute | solution.py:16
  91.4 5.7 %collective-permute-start.19 = (bf16[128,1536]{1,0:T(8,128)(2,1)}, bf16[128,1536]{1,0:T(8,128)(2,1)S(1)}, u32[]{:S(2)}, u32[]{:S(2)}) collective-permute-start(bf16[128,1536]{1,0:T(8,128)(2,1)} %get-tuple-element.117), channel_id=1, source_target_pairs={{0,20},{4,16},{8,28},{12,24},{16,4},{20,0},{24,12},{28,8},{1,21},{... | collective-permute-start | bytes 1179656 | tf_op jit(solution)/shard_map/ppermute | solution.py:16
  99.0 10.2 %shard_map.59.refs_8_.refs_6_ = f32[2,256,1024]{2,1,0:T(8,128)} custom-call(s32[2]{0:T(128)S(1)} %pad_add_fusion.where_ref, bf16[256,1536]{1,0:T(8,128)(2,1)S(1)} %copy-done.13, bf16[256,1536]{1,0:T(8,128)(2,1)} %collective-permute-done.3.refs_1_, bf16[256,1536]{1,0:T(8,128)(2,1)} %collective-permute-done.2.refs_2_, bf16[256,1536]{1,0:T(8,128)(2,1)S(1)} %copy-done.15, ...), custom_call_target="tpu_custom_call" | custom-call | flops 4831838208 | bytes 14155776 | tf_op jit(solution)/shard_map/pallas_call | solution.py:212
  109.3 13.6 %collective-permute-done.19.refs_1_ = bf16[128,1536]{1,0:T(8,128)(2,1)S(1)} collective-permute-done((bf16[128,1536]{1,0:T(8,128)(2,1)}, bf16[128,1536]{1,0:T(8,128)(2,1)S(1)}, u32[]{:S(2)}, u32[]{:S(2)}) %collective-permute-start.19) | collective-permute-done | bytes 393248 | tf_op jit(solution)/shard_map/ppermute | solution.py:16
  122.9 7.2 %collective-permute-done.18.refs_0_ = bf16[128,1536]{1,0:T(8,128)(2,1)S(1)} collective-permute-done((bf16[128,1536]{1,0:T(8,128)(2,1)}, bf16[128,1536]{1,0:T(8,128)(2,1)S(1)}, u32[]{:S(2)}, u32[]{:S(2)}) %collective-permute-start.18) | collective-permute-done | bytes 393248 | tf_op jit(solution)/shard_map/ppermute | solution.py:16
  132.6 2.7 %collective-permute-start.21 = (bf16[96,1536]{1,0:T(8,128)(2,1)S(1)}, bf16[96,1536]{1,0:T(8,128)(2,1)S(1)}, u32[]{:S(2)}, u32[]{:S(2)}) collective-permute-start(bf16[96,1536]{1,0:T(8,128)(2,1)S(1)} %copy-done.19), channel_id=1, source_target_pairs={{0,28},{4,24},{8,20},{12,16},{16,12},{20,8},{24,4},{28,0},{1,29},{... | collective-permute-start | bytes 884744 | tf_op jit(solution)/shard_map/ppermute | solution.py:16
  135.3 1.9 collective-permute-start.20
  137.2 9.8 %shard_map.60 = (f32[2,64,512]{2,1,0:T(8,128)S(1)}, f32[2,64,512]{2,1,0:T(8,128)S(1)}, f32[2,64,512]{2,1,0:T(8,128)}, f32[2,64,512]{2,1,0:T(8,128)}) custom-call(s32[2]{0:T(128)S(1)} %pad_add_fusion.where_ref, bf16[128,1536]{1,0:T(8,128)(2,1)S(1)} %collective-permute-done.9.refs_0_, bf16[128,1536]{1,0:T(8,128)(2,1)S(1)} %collective-permute-done.14.refs_1_, ...), custom_call_target="tpu_custom_call" | custom-call | flops 4026531840 | bytes 19660800 | tf_op jit(solution)/shard_map/pallas_call | solution.py:212
  149.7 4.1 %collective-permute-done.16 = f32[2,64,512]{2,1,0:T(8,128)S(1)} collective-permute-done((f32[2,64,512]{2,1,0:T(8,128)S(1)}, f32[2,64,512]{2,1,0:T(8,128)S(1)}, u32[]{:S(2)}, u32[]{:S(2)}) %collective-permute-start.16) | collective-permute-done | bytes 262176 | tf_op jit(solution)/shard_map/ppermute | solution.py:16
  153.9 3.4 %collective-permute-done.23.refs_1_ = bf16[128,1536]{1,0:T(8,128)(2,1)S(1)} collective-permute-done((bf16[128,1536]{1,0:T(8,128)(2,1)S(1)}, bf16[128,1536]{1,0:T(8,128)(2,1)S(1)}, u32[]{:S(2)}, u32[]{:S(2)}) %collective-permute-start.23) | collective-permute-done | bytes 393248 | tf_op jit(solution)/shard_map/ppermute | solution.py:16
  159.8 2.3 %collective-permute-start.25 = (f32[2,64,512]{2,1,0:T(8,128)}, f32[2,64,512]{2,1,0:T(8,128)}, u32[]{:S(2)}, u32[]{:S(2)}) collective-permute-start(f32[2,64,512]{2,1,0:T(8,128)} %get-tuple-element.125), channel_id=1, source_target_pairs={{0,5},{1,4},{2,7},{3,6},{4,1},{5,0},{6,3},{7,2},{8,13},{9,12},{10,... | collective-permute-start | bytes 786440 | tf_op jit(solution)/shard_map/ppermute | solution.py:276
  162.3 2.9 %collective-permute-start.26 = (bf16[32,1536]{1,0:T(8,128)(2,1)S(1)}, bf16[32,1536]{1,0:T(8,128)(2,1)S(1)}, u32[]{:S(2)}, u32[]{:S(2)}) collective-permute-start(bf16[32,1536]{1,0:T(8,128)(2,1)S(1)} %get-tuple-element.126), channel_id=1, source_target_pairs={{0,24},{4,28},{8,16},{12,20},{16,8},{20,12},{24,0},{28,4},{1,25},{... | collective-permute-start | bytes 294920 | tf_op jit(solution)/shard_map/ppermute | solution.py:16
  166.2 6.4 %shard_map.63.refs_4_ = f32[2,128,1024]{2,1,0:T(8,128)S(1)} custom-call(s32[2]{0:T(128)S(1)} %pad_add_fusion.where_ref, bf16[128,1536]{1,0:T(8,128)(2,1)S(1)} %collective-permute-done.17.refs_0_, bf16[128,1536]{1,0:T(8,128)(2,1)S(1)} %copy-done.6, bf16[2,128,1536]{2,1,0:T(8,128)(2,1)S(1)} %shard_map.61.refs_2_, ...), custom_call_target="tpu_custom_call" | custom-call | flops 2415919104 | bytes 11796480 | tf_op jit(solution)/shard_map/pallas_call | solution.py:212
  174.5 2.4 %collective-permute-start.30 = (f32[64,512]{1,0:T(8,128)S(1)}, f32[64,512]{1,0:T(8,128)S(1)}, u32[]{:S(2)}, u32[]{:S(2)}) collective-permute-start(f32[64,512]{1,0:T(8,128)S(1)} %get-tuple-element.132), channel_id=1, source_target_pairs={{0,16},{4,20},{8,24},{12,28},{16,0},{20,4},{24,8},{28,12},{1,17},{... | collective-permute-start | bytes 393224 | tf_op jit(solution)/shard_map/ppermute | solution.py:16
  178.4 4.5 %shard_map.64 = (f32[2,48,512]{2,1,0:T(8,128)S(1)}, f32[2,48,512]{2,1,0:T(8,128)S(1)}, f32[2,48,512]{2,1,0:T(8,128)S(1)}, f32[2,48,512]{2,1,0:T(8,128)S(1)}) custom-call(s32[2]{0:T(128)S(1)} %pad_add_fusion.where_ref, bf16[2,96,1536]{2,1,0:T(8,128)(2,1)S(1)} %shard_map.62.refs_0_, bf16[2,96,1536]{2,1,0:T(8,128)(2,1)S(1)} %collective-permute-done.28.refs_1_, ...), custom_call_target="tpu_custom_call" | custom-call | flops 1207959552 | bytes 7471104 | tf_op jit(solution)/shard_map/pallas_call | solution.py:212
  187.8 4.2 %shard_map.66 = (f32[2,16,512]{2,1,0:T(8,128)S(1)}, f32[2,16,512]{2,1,0:T(8,128)S(1)}, f32[2,16,512]{2,1,0:T(8,128)S(1)}, f32[2,16,512]{2,1,0:T(8,128)S(1)}) custom-call(s32[2]{0:T(128)S(1)} %pad_add_fusion.where_ref, bf16[2,32,1536]{2,1,0:T(8,128)(2,1)S(1)} %shard_map.65.refs_0_, bf16[2,32,1536]{2,1,0:T(8,128)(2,1)S(1)} %collective-permute-done.32.refs_1_, ...), custom_call_target="tpu_custom_call" | custom-call | flops 402653184 | bytes 6684672 | tf_op jit(solution)/shard_map/pallas_call | solution.py:212
  202.4 5.2 %collective-permute-done.37 = f32[48,512]{1,0:T(8,128)S(1)} collective-permute-done((f32[48,512]{1,0:T(8,128)S(1)}, f32[48,512]{1,0:T(8,128)S(1)}, u32[]{:S(2)}, u32[]{:S(2)}) %collective-permute-start.37) | collective-permute-done | bytes 98336 | tf_op jit(solution)/shard_map/ppermute | solution.py:16
  207.7 2.8 %collective-permute-done.43 = f32[16,512]{1,0:T(8,128)S(1)} collective-permute-done((f32[16,512]{1,0:T(8,128)S(1)}, f32[16,512]{1,0:T(8,128)S(1)}, u32[]{:S(2)}, u32[]{:S(2)}) %collective-permute-start.43) | collective-permute-done | bytes 32800 | tf_op jit(solution)/shard_map/ppermute | solution.py:16
  (159 shorter events, 52.5 us)
Async XLA Ops:
  6.3 20.8 %collective-permute-start = (bf16[128,1536]{1,0:T(8,128)(2,1)}, bf16[128,1536]{1,0:T(8,128)(2,1)S(1)}, u32[]{:S(2)}, u32[]{:S(2)}) collective-permute-start(bf16[128,1536]{1,0:T(8,128)(2,1)} %get-tuple-element.79), channel_id=1, source_target_pairs={{0,8},{4,12},{8,0},{12,4},{16,24},{20,28},{24,16},{28,20},{1,9},{5... | collective-permute-start | bytes 1179656 | tf_op jit(solution)/shard_map/ppermute | solution.py:16
  9.4 17.8 %collective-permute-start.1 = (bf16[128,1536]{1,0:T(8,128)(2,1)S(1)}, bf16[128,1536]{1,0:T(8,128)(2,1)S(1)}, u32[]{:S(2)}, u32[]{:S(2)}) collective-permute-start(bf16[128,1536]{1,0:T(8,128)(2,1)S(1)} %get-tuple-element.80), channel_id=1, source_target_pairs={{0,16},{4,20},{8,24},{12,28},{16,0},{20,4},{24,8},{28,12},{1,17},{... | collective-permute-start | bytes 1179656 | tf_op jit(solution)/shard_map/ppermute | solution.py:16
  12.0 18.8 %collective-permute-start.3 = (bf16[256,1536]{1,0:T(8,128)(2,1)S(1)}, bf16[256,1536]{1,0:T(8,128)(2,1)}, u32[]{:S(2)}, u32[]{:S(2)}) collective-permute-start(bf16[256,1536]{1,0:T(8,128)(2,1)S(1)} %get-tuple-element.82.refs_0_), channel_id=1, source_target_pairs={{0,2},{1,3},{2,0},{3,1},{4,6},{5,7},{6,4},{7,5},{8,10},{9,11},{10,... | collective-permute-start | bytes 2359304 | tf_op jit(solution)/shard_map/ppermute | solution.py:16
  13.5 18.8 %collective-permute-start.2 = (bf16[256,1536]{1,0:T(8,128)(2,1)}, bf16[256,1536]{1,0:T(8,128)(2,1)}, u32[]{:S(2)}, u32[]{:S(2)}) collective-permute-start(bf16[256,1536]{1,0:T(8,128)(2,1)} %get-tuple-element.81), channel_id=1, source_target_pairs={{0,4},{4,0},{8,12},{12,8},{16,20},{20,16},{24,28},{28,24},{1,5},{5... | collective-permute-start | bytes 2359304 | tf_op jit(solution)/shard_map/ppermute | solution.py:16
  32.3 22.5 %collective-permute-start.8 = (bf16[5,512,1536]{2,1,0:T(8,128)(2,1)S(1)}, bf16[5,512,1536]{2,1,0:T(8,128)(2,1)S(1)}, u32[]{:S(2)}, u32[]{:S(2)}) collective-permute-start(bf16[5,512,1536]{2,1,0:T(8,128)(2,1)S(1)} %shard_map.48.refs_6_.refs_4_.refs_2_), channel_id=1, source_target_pairs={{0,1},{1,0},{2,3},{3,2},{4,5},{5,4},{6,7},{7,6},{8,9},{9,8},{10,11... | collective-permute-start | bytes 23592968 | tf_op jit(solution)/shard_map/ppermute | solution.py:16
  32.3 22.5 %collective-permute-start.7 = (bf16[3,512,1536]{2,1,0:T(8,128)(2,1)S(1)}, bf16[3,512,1536]{2,1,0:T(8,128)(2,1)S(1)}, u32[]{:S(2)}, u32[]{:S(2)}) collective-permute-start(bf16[3,512,1536]{2,1,0:T(8,128)(2,1)S(1)} %shard_map.47.refs_6_), channel_id=1, source_target_pairs={{0,1},{1,0},{2,3},{3,2},{4,5},{5,4},{6,7},{7,6},{8,9},{9,8},{10,11... | collective-permute-start | bytes 14155784 | tf_op jit(solution)/shard_map/ppermute | solution.py:16
  32.8 21.9 %collective-permute-start.6 = (bf16[256,1536]{1,0:T(8,128)(2,1)}, bf16[256,1536]{1,0:T(8,128)(2,1)S(1)}, u32[]{:S(2)}, u32[]{:S(2)}) collective-permute-start(bf16[256,1536]{1,0:T(8,128)(2,1)} %collective-permute-done.2.refs_2_), channel_id=1, source_target_pairs={{0,2},{1,3},{2,0},{3,1},{4,6},{5,7},{6,4},{7,5},{8,10},{9,11},{10,... | collective-permute-start | bytes 2359304 | tf_op jit(solution)/shard_map/ppermute | solution.py:16
  33.3 17.0 %collective-permute-start.5 = (bf16[128,1536]{1,0:T(8,128)(2,1)S(1)}, bf16[128,1536]{1,0:T(8,128)(2,1)S(1)}, u32[]{:S(2)}, u32[]{:S(2)}) collective-permute-start(bf16[128,1536]{1,0:T(8,128)(2,1)S(1)} %shard_map.50), channel_id=1, source_target_pairs={{0,8},{4,12},{8,0},{12,4},{16,24},{20,28},{24,16},{28,20},{1,9},{5... | collective-permute-start | bytes 1179656 | tf_op jit(solution)/shard_map/ppermute | solution.py:16
  33.8 20.8 %collective-permute-start.4 = (bf16[128,1536]{1,0:T(8,128)(2,1)S(1)}, bf16[128,1536]{1,0:T(8,128)(2,1)S(1)}, u32[]{:S(2)}, u32[]{:S(2)}) collective-permute-start(bf16[128,1536]{1,0:T(8,128)(2,1)S(1)} %shard_map.49), channel_id=1, source_target_pairs={{0,20},{4,16},{8,28},{12,24},{16,4},{20,0},{24,12},{28,8},{1,21},{... | collective-permute-start | bytes 1179656 | tf_op jit(solution)/shard_map/ppermute | solution.py:16
  54.8 29.2 %collective-permute-start.13 = (bf16[2,128,1536]{2,1,0:T(8,128)(2,1)S(1)}, bf16[2,128,1536]{2,1,0:T(8,128)(2,1)S(1)}, u32[]{:S(2)}, u32[]{:S(2)}) collective-permute-start(bf16[2,128,1536]{2,1,0:T(8,128)(2,1)S(1)} %shard_map.57.refs_4_), channel_id=1, source_target_pairs={{0,2},{1,3},{2,0},{3,1},{4,6},{5,7},{6,4},{7,5},{8,10},{9,11},{10,... | collective-permute-start | bytes 2359304 | tf_op jit(solution)/shard_map/ppermute | solution.py:16
  56.3 33.1 %collective-permute-start.12 = (bf16[2,128,1536]{2,1,0:T(8,128)(2,1)S(1)}, bf16[2,128,1536]{2,1,0:T(8,128)(2,1)S(1)}, u32[]{:S(2)}, u32[]{:S(2)}) collective-permute-start(bf16[2,128,1536]{2,1,0:T(8,128)(2,1)S(1)} %shard_map.56.refs_2_), channel_id=1, source_target_pairs={{0,2},{1,3},{2,0},{3,1},{4,6},{5,7},{6,4},{7,5},{8,10},{9,11},{10,... | collective-permute-start | bytes 2359304 | tf_op jit(solution)/shard_map/ppermute | solution.py:16
  56.9 14.8 %collective-permute-start.11 = (bf16[128,1536]{1,0:T(8,128)(2,1)S(1)}, bf16[128,1536]{1,0:T(8,128)(2,1)S(1)}, u32[]{:S(2)}, u32[]{:S(2)}) collective-permute-start(bf16[128,1536]{1,0:T(8,128)(2,1)S(1)} %get-tuple-element.104), channel_id=1, source_target_pairs={{0,28},{4,24},{8,20},{12,16},{16,12},{20,8},{24,4},{28,0},{1,29},{... | collective-permute-start | bytes 1179656 | tf_op jit(solution)/shard_map/ppermute | solution.py:16
  59.2 20.9 %collective-permute-start.10 = (bf16[128,1536]{1,0:T(8,128)(2,1)S(1)}, bf16[128,1536]{1,0:T(8,128)(2,1)S(1)}, u32[]{:S(2)}, u32[]{:S(2)}) collective-permute-start(bf16[128,1536]{1,0:T(8,128)(2,1)S(1)} %get-tuple-element.102), channel_id=1, source_target_pairs={{0,24},{4,28},{8,16},{12,20},{16,8},{20,12},{24,0},{28,4},{1,25},{... | collective-permute-start | bytes 1179656 | tf_op jit(solution)/shard_map/ppermute | solution.py:16
  61.7 22.3 %collective-permute-start.9 = (bf16[128,1536]{1,0:T(8,128)(2,1)S(1)}, bf16[128,1536]{1,0:T(8,128)(2,1)S(1)}, u32[]{:S(2)}, u32[]{:S(2)}) collective-permute-start(bf16[128,1536]{1,0:T(8,128)(2,1)S(1)} %shard_map.51), channel_id=1, source_target_pairs={{0,12},{4,8},{8,4},{12,0},{16,28},{20,24},{24,20},{28,16},{1,13},{... | collective-permute-start | bytes 1179656 | tf_op jit(solution)/shard_map/ppermute | solution.py:16
  89.4 41.1 %collective-permute-start.15 = (bf16[2,128,1536]{2,1,0:T(8,128)(2,1)S(1)}, bf16[2,128,1536]{2,1,0:T(8,128)(2,1)S(1)}, u32[]{:S(2)}, u32[]{:S(2)}) collective-permute-start(bf16[2,128,1536]{2,1,0:T(8,128)(2,1)S(1)} %shard_map.58.refs_4_), channel_id=1, source_target_pairs={{0,2},{1,3},{2,0},{3,1},{4,6},{5,7},{6,4},{7,5},{8,10},{9,11},{10,... | collective-permute-start | bytes 2359304 | tf_op jit(solution)/shard_map/ppermute | solution.py:16
  90.1 40.4 %collective-permute-start.14 = (bf16[128,1536]{1,0:T(8,128)(2,1)S(1)}, bf16[128,1536]{1,0:T(8,128)(2,1)S(1)}, u32[]{:S(2)}, u32[]{:S(2)}) collective-permute-start(bf16[128,1536]{1,0:T(8,128)(2,1)S(1)} %collective-permute-done.9.refs_0_), channel_id=1, source_target_pairs={{0,2},{1,3},{2,0},{3,1},{4,6},{5,7},{6,4},{7,5},{8,10},{9,11},{10,... | collective-permute-start | bytes 1179656 | tf_op jit(solution)/shard_map/ppermute | solution.py:16
  91.4 31.5 %collective-permute-start.19 = (bf16[128,1536]{1,0:T(8,128)(2,1)}, bf16[128,1536]{1,0:T(8,128)(2,1)S(1)}, u32[]{:S(2)}, u32[]{:S(2)}) collective-permute-start(bf16[128,1536]{1,0:T(8,128)(2,1)} %get-tuple-element.117), channel_id=1, source_target_pairs={{0,20},{4,16},{8,28},{12,24},{16,4},{20,0},{24,12},{28,8},{1,21},{... | collective-permute-start | bytes 1179656 | tf_op jit(solution)/shard_map/ppermute | solution.py:16
  97.1 33.0 %collective-permute-start.18 = (bf16[128,1536]{1,0:T(8,128)(2,1)}, bf16[128,1536]{1,0:T(8,128)(2,1)S(1)}, u32[]{:S(2)}, u32[]{:S(2)}) collective-permute-start(bf16[128,1536]{1,0:T(8,128)(2,1)} %get-tuple-element.115), channel_id=1, source_target_pairs={{0,16},{4,20},{8,24},{12,28},{16,0},{20,4},{24,8},{28,12},{1,17},{... | collective-permute-start | bytes 1179656 | tf_op jit(solution)/shard_map/ppermute | solution.py:16
  97.2 33.3 %collective-permute-start.17 = (bf16[128,1536]{1,0:T(8,128)(2,1)}, bf16[128,1536]{1,0:T(8,128)(2,1)S(1)}, u32[]{:S(2)}, u32[]{:S(2)}) collective-permute-start(bf16[128,1536]{1,0:T(8,128)(2,1)} %get-tuple-element.114), channel_id=1, source_target_pairs={{0,12},{4,8},{8,4},{12,0},{16,28},{20,24},{24,20},{28,16},{1,13},{... | collective-permute-start | bytes 1179656 | tf_op jit(solution)/shard_map/ppermute | solution.py:16
  130.5 27.6 %collective-permute-start.22 = (bf16[2,128,1536]{2,1,0:T(8,128)(2,1)S(1)}, bf16[2,128,1536]{2,1,0:T(8,128)(2,1)S(1)}, u32[]{:S(2)}, u32[]{:S(2)}) collective-permute-start(bf16[2,128,1536]{2,1,0:T(8,128)(2,1)S(1)} %shard_map.61.refs_2_), channel_id=1, source_target_pairs={{0,2},{1,3},{2,0},{3,1},{4,6},{5,7},{6,4},{7,5},{8,10},{9,11},{10,... | collective-permute-start | bytes 2359304 | tf_op jit(solution)/shard_map/ppermute | solution.py:16
  132.2 25.0 %collective-permute-start.23 = (bf16[128,1536]{1,0:T(8,128)(2,1)S(1)}, bf16[128,1536]{1,0:T(8,128)(2,1)S(1)}, u32[]{:S(2)}, u32[]{:S(2)}) collective-permute-start(bf16[128,1536]{1,0:T(8,128)(2,1)S(1)} %collective-permute-done.17.refs_0_), channel_id=1, source_target_pairs={{0,2},{1,3},{2,0},{3,1},{4,6},{5,7},{6,4},{7,5},{8,10},{9,11},{10,... | collective-permute-start | bytes 1179656 | tf_op jit(solution)/shard_map/ppermute | solution.py:16
  132.6 15.2 %collective-permute-start.21 = (bf16[96,1536]{1,0:T(8,128)(2,1)S(1)}, bf16[96,1536]{1,0:T(8,128)(2,1)S(1)}, u32[]{:S(2)}, u32[]{:S(2)}) collective-permute-start(bf16[96,1536]{1,0:T(8,128)(2,1)S(1)} %copy-done.19), channel_id=1, source_target_pairs={{0,28},{4,24},{8,20},{12,16},{16,12},{20,8},{24,4},{28,0},{1,29},{... | collective-permute-start | bytes 884744 | tf_op jit(solution)/shard_map/ppermute | solution.py:16
  135.3 14.4 %collective-permute-start.20 = (bf16[96,1536]{1,0:T(8,128)(2,1)S(1)}, bf16[96,1536]{1,0:T(8,128)(2,1)S(1)}, u32[]{:S(2)}, u32[]{:S(2)}) collective-permute-start(bf16[96,1536]{1,0:T(8,128)(2,1)S(1)} %copy-done.17), channel_id=1, source_target_pairs={{0,24},{4,28},{8,16},{12,20},{16,8},{20,12},{24,0},{28,4},{1,25},{... | collective-permute-start | bytes 884744 | tf_op jit(solution)/shard_map/ppermute | solution.py:16
  158.0 16.0 %collective-permute-start.28 = (bf16[2,96,1536]{2,1,0:T(8,128)(2,1)S(1)}, bf16[2,96,1536]{2,1,0:T(8,128)(2,1)S(1)}, u32[]{:S(2)}, u32[]{:S(2)}) collective-permute-start(bf16[2,96,1536]{2,1,0:T(8,128)(2,1)S(1)} %shard_map.62.refs_0_), channel_id=1, source_target_pairs={{0,2},{1,3},{2,0},{3,1},{4,6},{5,7},{6,4},{7,5},{8,10},{9,11},{10,... | collective-permute-start | bytes 1769480 | tf_op jit(solution)/shard_map/ppermute | solution.py:16
  159.8 13.0 %collective-permute-start.24 = (f32[2,64,512]{2,1,0:T(8,128)}, f32[2,64,512]{2,1,0:T(8,128)}, u32[]{:S(2)}, u32[]{:S(2)}) collective-permute-start(f32[2,64,512]{2,1,0:T(8,128)} %get-tuple-element.123), channel_id=1, source_target_pairs={{0,1},{1,0},{2,3},{3,2},{4,5},{5,4},{6,7},{7,6},{8,9},{9,8},{10,11... | collective-permute-start | bytes 786440 | tf_op jit(solution)/shard_map/ppermute | solution.py:16
  159.8 13.0 %collective-permute-start.25 = (f32[2,64,512]{2,1,0:T(8,128)}, f32[2,64,512]{2,1,0:T(8,128)}, u32[]{:S(2)}, u32[]{:S(2)}) collective-permute-start(f32[2,64,512]{2,1,0:T(8,128)} %get-tuple-element.125), channel_id=1, source_target_pairs={{0,5},{1,4},{2,7},{3,6},{4,1},{5,0},{6,3},{7,2},{8,13},{9,12},{10,... | collective-permute-start | bytes 786440 | tf_op jit(solution)/shard_map/ppermute | solution.py:276
  162.1 10.6 %collective-permute-start.27 = (bf16[32,1536]{1,0:T(8,128)(2,1)S(1)}, bf16[32,1536]{1,0:T(8,128)(2,1)S(1)}, u32[]{:S(2)}, u32[]{:S(2)}) collective-permute-start(bf16[32,1536]{1,0:T(8,128)(2,1)S(1)} %get-tuple-element.128), channel_id=1, source_target_pairs={{0,28},{4,24},{8,20},{12,16},{16,12},{20,8},{24,4},{28,0},{1,29},{... | collective-permute-start | bytes 294920 | tf_op jit(solution)/shard_map/ppermute | solution.py:16
  162.3 10.4 %collective-permute-start.26 = (bf16[32,1536]{1,0:T(8,128)(2,1)S(1)}, bf16[32,1536]{1,0:T(8,128)(2,1)S(1)}, u32[]{:S(2)}, u32[]{:S(2)}) collective-permute-start(bf16[32,1536]{1,0:T(8,128)(2,1)S(1)} %get-tuple-element.126), channel_id=1, source_target_pairs={{0,24},{4,28},{8,16},{12,20},{16,8},{20,12},{24,0},{28,4},{1,25},{... | collective-permute-start | bytes 294920 | tf_op jit(solution)/shard_map/ppermute | solution.py:16
  174.5 11.9 %collective-permute-start.30 = (f32[64,512]{1,0:T(8,128)S(1)}, f32[64,512]{1,0:T(8,128)S(1)}, u32[]{:S(2)}, u32[]{:S(2)}) collective-permute-start(f32[64,512]{1,0:T(8,128)S(1)} %get-tuple-element.132), channel_id=1, source_target_pairs={{0,16},{4,20},{8,24},{12,28},{16,0},{20,4},{24,8},{28,12},{1,17},{... | collective-permute-start | bytes 393224 | tf_op jit(solution)/shard_map/ppermute | solution.py:16
  182.9 11.3 %collective-permute-start.33 = (f32[2,48,512]{2,1,0:T(8,128)S(1)}, f32[2,48,512]{2,1,0:T(8,128)S(1)}, u32[]{:S(2)}, u32[]{:S(2)}) collective-permute-start(f32[2,48,512]{2,1,0:T(8,128)S(1)} %get-tuple-element.138), channel_id=1, source_target_pairs={{0,4},{4,0},{8,12},{12,8},{16,20},{20,16},{24,28},{28,24},{1,5},{5... | collective-permute-start | bytes 589832 | tf_op jit(solution)/shard_map/ppermute | solution.py:16
  196.1 11.5 %collective-permute-start.37 = (f32[48,512]{1,0:T(8,128)S(1)}, f32[48,512]{1,0:T(8,128)S(1)}, u32[]{:S(2)}, u32[]{:S(2)}) collective-permute-start(f32[48,512]{1,0:T(8,128)S(1)} %get-tuple-element.146), channel_id=1, source_target_pairs={{0,16},{4,20},{8,24},{12,28},{16,0},{20,4},{24,8},{28,12},{1,17},{... | collective-permute-start | bytes 294920 | tf_op jit(solution)/shard_map/ppermute | solution.py:16
  197.3 10.4 %collective-permute-start.38 = (f32[48,512]{1,0:T(8,128)S(1)}, f32[48,512]{1,0:T(8,128)S(1)}, u32[]{:S(2)}, u32[]{:S(2)}) collective-permute-start(f32[48,512]{1,0:T(8,128)S(1)} %get-tuple-element.147), channel_id=1, source_target_pairs={{0,24},{4,28},{8,16},{12,20},{16,8},{20,12},{24,0},{28,4},{1,25},{... | collective-permute-start | bytes 294920 | tf_op jit(solution)/shard_map/ppermute | solution.py:16
  (41 other events, 508.5 us)
